TPU v7x, 32 devices: a whole 2x2x4 slice. The times are simulated.
32 devices in a mesh: groups: 2 (over x), blk: 8 (over z, y), chan: 2 (over core).
Axes of the slice: x: 2, y: 2, z: 4, core: 2. Of those that a mesh axis runs over, the one named last changes fastest.
Arguments:
- records: bfloat16 [1024, 2048], P('chan', ('groups', 'blk')), parts along dimension 1, as said below
- templates: bfloat16 [100, 2048, 1024], P(None, ('groups', 'blk'), 'chan'), parts along dimension 1, as said below
- offsets: int32 [2048, 1024], P(('groups', 'blk'), 'chan'), parts along dimension 0, may hold values from 0 to 4
- masks: int32 [2048, 1024], P(('groups', 'blk'), 'chan'), parts along dimension 0, may hold values 0 or 1
Outputs:
- detection: float32 [2048, 1024], P(('groups', 'blk'), 'chan'), parts along dimension 0
There are 2 independent parts, one for each index of `groups`. A program takes and returns all parts, laid end to end along the dimension named above; each array names one. Nothing has to cross between parts.
Inputs may be any that keep to these rules, and one draw needn't show every extreme that they name: `records`: finite samples. `templates`: finite samples.
All inputs are finite; a program needn't handle non-finite values. No bound on the sum of `masks` on one device may be relied on, other than what follows from the above.
Results may differ from a plain program's by a relative error of at most 0.0041.
Values may be sent and summed in bfloat16 or wider, within the bound.
No kernel may reach another device: no remote copies, remote signals or barrier semaphores. Data moves between devices by JAX's collectives and lax.ppermute only.
A program may use at most 448 MiB of HBM per device.

v0:
```python
import jax
import jax.numpy as jnp
from jax import lax
from jax.sharding import PartitionSpec as P

L = 100
LE = 104


EPS = 1e-06


def window_inverse(zero_extended_signal):
    square = zero_extended_signal * zero_extended_signal
    zero = jnp.zeros((), square.dtype)
    dims = (1,) * (square.ndim - 1) + (LE,)
    strides = (1,) * square.ndim
    total = lax.reduce_window(square, zero, lax.add, dims, strides, "VALID")
    return lax.rsqrt(total / LE + EPS)


def unfold_lags(segment, width):
    length = segment.shape[-1]
    tiled = jnp.tile(segment, (1,) * (segment.ndim - 1) + (LE + 1,))
    cut = tiled[..., : LE * (length + 1)]
    return cut.reshape(segment.shape[:-1] + (LE, length + 1))[..., :width]


def embed_templates(templates, offsets, masks):
    tfloat = templates.astype(jnp.float32)
    tinv = lax.rsqrt(jnp.mean(tfloat * tfloat, axis=0) + EPS)
    scale = tinv * masks.astype(jnp.float32) / L
    scaled = tfloat * scale[None]
    embedded = jnp.zeros((LE,) + scaled.shape[1:], jnp.float32)
    for delay_amount in range(LE - L + 1):
        moved = jnp.pad(scaled, ((delay_amount, LE - L - delay_amount), (0, 0), (0, 0)))
        embedded = embedded + jnp.where((offsets == delay_amount)[None], moved, 0.0)
    embedded = embedded.astype(jnp.bfloat16)
    return jnp.transpose(embedded, (1, 2, 0)).reshape(scaled.shape[1], -1)


def window_matrix(segment, width):
    wide = segment.astype(jnp.float32)
    inverse = window_inverse(wide)
    shifted = unfold_lags(segment, width).astype(jnp.float32)
    windows = (shifted * inverse[..., None, :]).astype(jnp.bfloat16)
    return windows.reshape(segment.shape[:-2] + (segment.shape[-2] * LE, width))


def per_device(records, templates, offsets, masks):
    flat = embed_templates(templates, offsets, masks)
    rows = flat.shape[0]
    whole = lax.all_gather(records, "blk", axis=1, tiled=True)
    zero_extended_signal = jnp.concatenate(
        [whole, jnp.zeros((whole.shape[0], LE - 1), whole.dtype)], axis=1
    )
    block = 512
    count = whole.shape[1] // block

    def one_block(index):
        segment = lax.dynamic_slice_in_dim(zero_extended_signal, index * block, block + LE - 1, 1)
        return jnp.dot(flat, window_matrix(segment, block), preferred_element_type=jnp.float32)

    blocks = lax.map(one_block, jnp.arange(count, dtype=jnp.int32))
    partial_sum = jnp.transpose(blocks, (1, 0, 2)).reshape(rows, -1)
    return lax.psum_scatter(partial_sum, "chan", scatter_dimension=1, tiled=True)


def solution(mesh):
    return jax.shard_map(
        per_device,
        mesh=mesh,
        in_specs=(
            P("chan", ("groups", "blk")),
            P(None, ("groups", "blk"), "chan"),
            P(("groups", "blk"), "chan"),
            P(("groups", "blk"), "chan"),
        ),
        out_specs=P(("groups", "blk"), "chan"),
        check_vma=False,
    )
```

profile of v0, /device:TPU:0, one launch (start us, length us, event | category | flops | bytes accessed | tf_op | source)
XLA Modules:
  0.0 795.8 jit_solution(15934184214041245619)
XLA Ops:
  6.5 1.7 copy.32
  11.4 18.8 %copy.34 = bf16[100,128,512]{1,0,2:T(8,128)(2,1)} copy(bf16[100,128,512]{2,1,0:T(8,128)(2,1)} %param.7) | data formatting | bytes 26214400 | tf_op args[1]
  30.1 10.4 %fusion.1 = f32[128,512]{0,1:T(8,128)S(1)} fusion(bf16[100,128,512]{1,0,2:T(8,128)(2,1)} %copy.34), kind=kLoop, calls=%fused_computation.8 | loop fusion | flops 19595264 | bytes 13369344 | tf_op jit(solution)/shard_map/reduce_sum | solution.py:31
  40.6 15.6 %convert_multiply_fusion.1 = f32[100,128,512]{1,0,2:T(8,128)} fusion(bf16[100,128,512]{1,0,2:T(8,128)(2,1)} %copy.34, f32[128,512]{0,1:T(8,128)S(1)} %multiply_multiply_fusion), kind=kLoop, calls=%fused_computation.6 | loop fusion | flops 13107200 | bytes 39583744 | tf_op jit(solution)/shard_map/mul | solution.py:33
  56.1 64.5 %add_convert_fusion = bf16[104,128,512]{1,0,2:T(8,128)(2,1)} fusion(f32[100,128,512]{1,0,2:T(8,128)} %convert_multiply_fusion.1, pred[128,512]{0,1:T(8,128)(4,1)S(1)} %copy.39, pred[128,512]{0,1:T(8,128)(4,1)S(1)} %copy.38, pred[128,512]{0,1:T(8,128)(4,1)S(1)} %copy.37, pred[128,512]{0,1:T(8,128)(4,1)S(1)} %copy.36, pred[128,512]{0,1:T(8,128)(4,1)S(1)} %copy.33), kind=kLoop, calls=%fused_computation.9 | loop fusion | flops 68157440 | bytes 40173568 | tf_op jit(solution)/shard_map/convert_element_type | solution.py:38
  120.7 18.4 %copy.40 = bf16[128,53248]{1,0:T(8,128)(2,1)} copy(bf16[128,53248]{0,1:T(8,128)(2,1)} %bitcast.33) | data formatting | bytes 27262976 | tf_op jit(solution)/shard_map/while | solution.py:64
  139.1 2.3 concatenate.3
  141.9 633.7 %while.10 = (s32[]{:T(128)}, f32[2,128,512]{1,2,0:T(8,128)}, s32[2]{0:T(128)}, bf16[512,1127]{0,1:T(8,128)(2,1)}, bf16[128,53248]{1,0:T(8,128)(2,1)}, /*index=5*...) while((s32[]{:T(128)}, f32[2,128,512]{1,2,0:T(8,128)}, s32[2]{0:T(128)}, ...), condition=%wide.region_3.4_spmd, body=%wide.region_1.3_spmd.sunk | while | flops 7089265664 | bytes 628897984 | solution.py:64
  145.2 28.9 %reduce_window.8 = f32[512,512]{0,1:T(8,128)S(1)} reduce-window(f32[512,615]{0,1:T(8,128)S(1)} %get-tuple-element.99, f32[]{:T(128)} %constant.7.clone.1..sunk), window={size=1x104}, to_apply=%region_2.2 | reduce-window | flops 27000832 | bytes 2308100 | tf_op jit(solution)/shard_map/while/body/eval_jaxpr/reduce_window | solution.py:18
  174.3 21.0 %tile.11 = bf16[512,105,615]{0,2,1:T(8,128)(2,1)} broadcast(bf16[512,615]{0,1:T(8,128)(2,1)S(1)} %get-tuple-element.98), dimensions={0,2} | broadcast | bytes 66754560 | tf_op jit(solution)/shard_map/while/body/eval_jaxpr/tile | solution.py:24
  195.2 82.0 %tile.12 = bf16[512,64575]{0,1:T(8,128)(2,1)} reshape(bf16[512,105,615]{0,2,1:T(8,128)(2,1)} %tile.11) | data formatting | bytes 132249600 | tf_op jit(solution)/shard_map/while/body/eval_jaxpr/tile | solution.py:24
  277.2 43.4 %slice.12 = bf16[512,64064]{0,1:T(8,128)(2,1)} slice(bf16[512,64575]{0,1:T(8,128)(2,1)} %tile.12), slice={[0:512], [0:64064]} | slice | bytes 131203072 | tf_op jit(solution)/shard_map/while/body/eval_jaxpr/slice | solution.py:25
  320.6 36.2 %multiply_convert_fusion.2 = bf16[512,104,512]{0,2,1:T(8,128)(2,1)} fusion(bf16[512,104,616]{0,2,1:T(8,128)(2,1)} %bitcast.31, f32[512,512]{0,1:T(8,128)S(1)} %add_rsqrt_fusion.2), kind=kLoop, calls=%fused_computation.clone.1 | loop fusion | flops 81788928 | bytes 110100480 | tf_op jit(solution)/shard_map/while/body/eval_jaxpr/convert_element_type | solution.py:46
  356.8 74.8 %copy.44 = bf16[512,104,512]{2,1,0:T(8,128)(2,1)} copy(bf16[512,104,512]{0,2,1:T(8,128)(2,1)} %multiply_convert_fusion.2) | data formatting | bytes 109051904 | tf_op jit(solution)/shard_map/while/body/eval_jaxpr/convert_element_type | solution.py:46
  431.6 25.5 %fusion.9 = f32[2,128,512]{1,2,0:T(8,128)S(1)} fusion(f32[2,128,512]{1,2,0:T(8,128)S(1)} %copy-done, s32[]{:T(128)S(6)} %copy.48, bf16[53248,512]{1,0:T(8,128)(2,1)} %bitcast.32, bf16[128,53248]{1,0:T(8,128)(2,1)} %get-tuple-element.124), kind=kOutput, calls=%fused_computation.3.clone.1 | convolution fusion | flops 6979321856 | bytes 68419584 | tf_op jit(solution)/shard_map/while/body/eval_jaxpr/dot_general | solution.py:62
  461.5 28.9 %reduce_window.8 = f32[512,512]{0,1:T(8,128)S(1)} reduce-window(f32[512,615]{0,1:T(8,128)S(1)} %get-tuple-element.99, f32[]{:T(128)} %constant.7.clone.1..sunk), window={size=1x104}, to_apply=%region_2.2 | reduce-window | flops 27000832 | bytes 2308100 | tf_op jit(solution)/shard_map/while/body/eval_jaxpr/reduce_window | solution.py:18
  490.6 21.0 %tile.11 = bf16[512,105,615]{0,2,1:T(8,128)(2,1)} broadcast(bf16[512,615]{0,1:T(8,128)(2,1)S(1)} %get-tuple-element.98), dimensions={0,2} | broadcast | bytes 66754560 | tf_op jit(solution)/shard_map/while/body/eval_jaxpr/tile | solution.py:24
  511.6 82.0 %tile.12 = bf16[512,64575]{0,1:T(8,128)(2,1)} reshape(bf16[512,105,615]{0,2,1:T(8,128)(2,1)} %tile.11) | data formatting | bytes 132249600 | tf_op jit(solution)/shard_map/while/body/eval_jaxpr/tile | solution.py:24
  593.5 43.4 %slice.12 = bf16[512,64064]{0,1:T(8,128)(2,1)} slice(bf16[512,64575]{0,1:T(8,128)(2,1)} %tile.12), slice={[0:512], [0:64064]} | slice | bytes 131203072 | tf_op jit(solution)/shard_map/while/body/eval_jaxpr/slice | solution.py:25
  637.0 36.2 %multiply_convert_fusion.2 = bf16[512,104,512]{0,2,1:T(8,128)(2,1)} fusion(bf16[512,104,616]{0,2,1:T(8,128)(2,1)} %bitcast.31, f32[512,512]{0,1:T(8,128)S(1)} %add_rsqrt_fusion.2), kind=kLoop, calls=%fused_computation.clone.1 | loop fusion | flops 81788928 | bytes 110100480 | tf_op jit(solution)/shard_map/while/body/eval_jaxpr/convert_element_type | solution.py:46
  673.2 74.8 %copy.44 = bf16[512,104,512]{2,1,0:T(8,128)(2,1)} copy(bf16[512,104,512]{0,2,1:T(8,128)(2,1)} %multiply_convert_fusion.2) | data formatting | bytes 109051904 | tf_op jit(solution)/shard_map/while/body/eval_jaxpr/convert_element_type | solution.py:46
  748.0 25.6 %fusion.9 = f32[2,128,512]{1,2,0:T(8,128)S(1)} fusion(f32[2,128,512]{1,2,0:T(8,128)S(1)} %copy-done, s32[]{:T(128)S(6)} %copy.48, bf16[53248,512]{1,0:T(8,128)(2,1)} %bitcast.32, bf16[128,53248]{1,0:T(8,128)(2,1)} %get-tuple-element.124), kind=kOutput, calls=%fused_computation.3.clone.1 | convolution fusion | flops 6979321856 | bytes 68419584 | tf_op jit(solution)/shard_map/while/body/eval_jaxpr/dot_general | solution.py:62
  775.6 2.0 copy.42
  777.7 10.7 %reduce-scatter.2.cloned.1.call-done = f32[128,512]{1,0:T(8,128)} async-done(((f32[128,1024]{1,0:T(8,128)}), f32[128,512]{1,0:T(8,128)}) %reduce-scatter.2.cloned.1.call-update) | async-done | bytes 262160 | tf_op jit(solution)/shard_map/reduce_scatter | solution.py:66
  (29 shorter events, 10.9 us)
Async XLA Ops:
  6.5 132.5 %all-gather.2.cloned.1.call-start = ((), (), s32[]{:S(2)}) async-start(), calls=%async_computation.1 | async-start | bytes 1179648 | tf_op jit(solution)/shard_map/all_gather | solution.py:53
  8.2 780.2 %reduce-scatter.2.cloned.1.call-start = ((), (), s32[]{:S(2)}) async-start(), calls=%async_computation.2 | async-start | bytes 786432 | tf_op jit(solution)/shard_map/reduce_scatter | solution.py:66
  356.8 74.8 %copy-start = (f32[2,128,512]{1,2,0:T(8,128)S(1)}, f32[2,128,512]{1,2,0:T(8,128)}, u32[]{:S(2)}) copy-start(f32[2,128,512]{1,2,0:T(8,128)} %get-tuple-element.111) | copy-start | bytes 1572868 | tf_op jit(solution)/shard_map/while
  457.2 0.9 copy-start.1
  673.2 74.8 %copy-start = (f32[2,128,512]{1,2,0:T(8,128)S(1)}, f32[2,128,512]{1,2,0:T(8,128)}, u32[]{:S(2)}) copy-start(f32[2,128,512]{1,2,0:T(8,128)} %get-tuple-element.111) | copy-start | bytes 1572868 | tf_op jit(solution)/shard_map/while
  773.5 0.9 copy-start.1
Sparse Core Ops, SparseCore 0:
  9.5 42.9 all-gather.1
  777.8 10.5 reduce-scatter.1
where the time goes:
time: 811 us; the launch traced here: 796 us
  local copies, waits for them, and re-layouts  492 us (61%)
  other arithmetic  225 us (28%)
  matrix products  51.1 us (6%)
  between operations  14 us (2%)
  waiting for transfers between devices  10.8 us (1%)
    another operation x4, local copies, waits for them, and re-layouts, unfold_lags(): tiled = jnp.tile(segment, (1,) * (segment.ndim - 1) + (LE + 1,))  206 us
    convert_element_type x2, local copies, waits for them, and re-layouts, window_matrix(): windows = (shifted * inverse[..., None, :]).astype(jnp.bfloat16)  150 us
    slice x2, local copies, waits for them, and re-layouts, unfold_lags(): cut = tiled[..., :LE * (length + 1)]  86.8 us
    convert_element_type x2, other arithmetic, window_matrix(): windows = (shifted * inverse[..., None, :]).astype(jnp.bfloat16)  72.4 us
    convert_element_type x1, other arithmetic, embed_templates(): embedded = embedded.astype(jnp.bfloat16)  64.5 us
    another operation x2, other arithmetic, window_inverse(): total = lax.reduce_window(square, zero, lax.add, dims, strides, 'VALID')  57.8 us
    dot_general x2, matrix products, one_block(): jnp.dot(flat, window_matrix(segment, block), preferred_element_type=jnp.f...  51.1 us
    unnamed x3, local copies, waits for them, and re-layouts  21.5 us
  transfers between devices with their start and end apart: 2, of which 1 were waited for; matrix products, arithmetic and copies ran while one was open for 16% of the time, Pallas kernels for 0%

commit v1 on v0

v1 whole, which is shorter than its diff:
```python
import functools

import jax
import jax.numpy as jnp
from jax import lax
from jax.experimental import pallas as pl
from jax.experimental.pallas import tpu as pltpu
from jax.sharding import PartitionSpec as P

L = 100
LE = 104
SPAN = LE - L
EPS = 1e-06
LANES = 128
TAPS = 8
GROUP = 8
VMEM = 56 * 1024 * 1024


def embed_kernel(t_ref, off_ref, mask_ref, e_ref):
    rows, cols = off_ref.shape

    def square(l, acc):
        v = t_ref[l].astype(jnp.float32)
        return acc + v * v

    total = lax.fori_loop(0, L, square, jnp.zeros((rows, cols), jnp.float32), unroll=4)
    scale = lax.rsqrt(total / L + EPS) * mask_ref[...].astype(jnp.float32) / L
    off = off_ref[...].astype(jnp.float32).astype(jnp.bfloat16)
    zero = jnp.zeros((rows, cols), jnp.bfloat16)

    def place(j, read):
        value = read(j)
        for d in range(1, SPAN + 1):
            value = jnp.where(off == d, read(j - d), value)
        scaled = value.astype(jnp.float32) * scale
        e_ref[j] = scaled.T.astype(jnp.bfloat16)

    def edge(l):
        return t_ref[l] if 0 <= l < L else zero

    for j in range(SPAN):
        place(j, edge)
    for j in range(L, LE):
        place(j, edge)

    def body(j, carry):
        place(j, lambda l: t_ref[l])
        return carry

    lax.fori_loop(SPAN, L, body, 0, unroll=2)


def embed(templates, offsets, masks, start, width):
    k = offsets.shape[0]
    first = start // LANES
    steps = width // LANES
    return pl.pallas_call(
        embed_kernel,
        grid=(steps,),
        in_specs=[
            pl.BlockSpec((L, k, LANES), lambda i: (0, 0, first + i)),
            pl.BlockSpec((k, LANES), lambda i: (0, first + i)),
            pl.BlockSpec((k, LANES), lambda i: (0, first + i)),
        ],
        out_specs=pl.BlockSpec((LE, LANES, k), lambda i: (0, i, 0)),
        out_shape=jax.ShapeDtypeStruct((LE, width, k), jnp.bfloat16),
        compiler_params=pltpu.CompilerParams(vmem_limit_bytes=VMEM),
        cost_estimate=pl.CostEstimate(
            flops=20 * LE * width * k, bytes_accessed=2 * 2 * LE * width * k, transcendentals=0
        ),
    )(templates, offsets, masks)


def ring_position(b, n):
    z, y = b // 2, b % 2
    return z * (1 - y) + (n - 1 - z) * y


def ring_block(p, n):
    half = n // 2
    low = (p < half) * 1 if isinstance(p, int) else (p < half).astype(jnp.int32)
    return low * (2 * p) + (1 - low) * (2 * (n - 1 - p) + 1)


def ring_gather(x, n, forward_last):
    order = [ring_block(p, n) for p in range(n)]
    up = [(order[p], order[(p + 1) % n]) for p in range(n)]
    down = [(order[(p + 1) % n], order[p]) for p in range(n)]
    half = n // 2
    blocks = {0: x}
    a = b = x
    for step in range(1, half + 1):
        if step < half or forward_last:
            a = lax.ppermute(a, "blk", up)
            blocks[(-step) % n] = a
        if step < half or not forward_last:
            b = lax.ppermute(b, "blk", down)
            blocks[step] = b
    return [blocks[d] for d in range(n)]


def prepare(n, block_refs, flat_ref, x_ref, g_ref, n_ref):
    lags, width = block_refs[0].shape
    me = ring_position(lax.axis_index("blk"), n)
    for d in range(n):
        where = ring_block(lax.rem(me + d, n), n)
        for w in range(width // LANES):
            flat_ref[w, pl.ds(pl.multiple_of(where * lags, lags), lags), :] = block_refs[d][
                :, w * LANES : (w + 1) * LANES
            ].astype(jnp.float32)
    for w in range(width // LANES):
        flat_ref[w, n * lags :, :] = jnp.zeros((lags, LANES), jnp.float32)

    groups = (lags + LE) // GROUP

    def spread(g, carry):
        sums = [None] * (width // LANES)
        for r in range(GROUP):
            u = g * GROUP + r
            for w in range(width // LANES):
                value = flat_ref[w, pl.ds(u, n, stride=lags), :]
                x_ref[u, :, w * LANES : (w + 1) * LANES] = value
                square = value * value
                sums[w] = square if r == 0 else sums[w] + square
        for w in range(width // LANES):
            g_ref[g, :, w * LANES : (w + 1) * LANES] = sums[w]
        return carry

    lax.fori_loop(0, groups, spread, 0)

    def norms(g, carry):
        middle = g_ref[g + 1]
        for i in range(2, LE // GROUP):
            middle = middle + g_ref[g + i]
        tails = [None] * GROUP
        tail = None
        for r in range(GROUP - 1, -1, -1):
            value = x_ref[g * GROUP + r]
            square = value * value
            tail = square if tail is None else tail + square
            tails[r] = tail
        head = None
        for r in range(GROUP):
            total = middle + tails[r]
            if r > 0:
                value = x_ref[g * GROUP + LE + r - 1]
                square = value * value
                head = square if head is None else head + square
                total = total + head
            n_ref[g * GROUP + r] = lax.rsqrt(total / LE + EPS)
        return carry

    lax.fori_loop(0, lags // GROUP, norms, 0)


def correlate_kernel(n, steps, carried, *refs):
    blocks = refs[:n]
    e_ref = refs[n]
    rest = refs[n + 1 :]
    if carried:
        before_ref, mine_ref, other_ref, acc_ref, flat_ref, x_ref, g_ref, n_ref = rest
    else:
        acc_ref, flat_ref, x_ref, g_ref, n_ref = rest
    lags, width = blocks[0].shape
    k = e_ref.shape[-1]
    step = pl.program_id(0)

    @pl.when(step == 0)
    def _():
        prepare(n, blocks, flat_ref, x_ref, g_ref, n_ref)
        if carried:
            acc_ref[...] = before_ref[...]
        else:
            acc_ref[...] = jnp.zeros_like(acc_ref)

    chunk = 256 // n
    weights = e_ref[...].reshape(TAPS * width, k)

    def tile(m, carry):
        u = m * chunk
        norm = n_ref[pl.ds(u, chunk)]
        parts = []
        for tap in range(TAPS):
            value = x_ref[pl.ds(u + step * TAPS + tap, chunk)] * norm
            parts.append(value.reshape(chunk * n, width).astype(jnp.bfloat16))
        windows = jnp.concatenate(parts, axis=1)
        rows = pl.ds(pl.multiple_of(m * chunk * n, chunk * n), chunk * n)
        acc_ref[rows, :] += jnp.dot(windows, weights, preferred_element_type=jnp.float32)
        return carry

    lax.fori_loop(0, lags // chunk, tile, 0)

    if carried:

        @pl.when(step == steps - 1)
        def _():
            core = lax.axis_index("chan")
            half = n // 2
            for out_ref, first in ((mine_ref, core * half), (other_ref, (1 - core) * half)):
                for v in range(half):
                    value = acc_ref[pl.ds(first + v, lags, stride=n), :]
                    out_ref[:, v * lags : (v + 1) * lags] = value.T


def correlate(blocks, embedded, before):
    n = len(blocks)
    lags, width = blocks[0].shape
    k = embedded.shape[-1]
    steps = LE // TAPS
    whole = pl.BlockSpec(memory_space=pltpu.VMEM)
    carried = before is not None
    in_specs = [whole] * n + [pl.BlockSpec((TAPS, width, k), lambda i: (i, 0, 0))]
    scratch = [
        pltpu.VMEM((width // LANES, (n + 1) * lags, LANES), jnp.float32),
        pltpu.VMEM((lags + LE, n, width), jnp.float32),
        pltpu.VMEM(((lags + LE) // GROUP, n, width), jnp.float32),
        pltpu.VMEM((lags, n, width), jnp.float32),
    ]
    args = list(blocks) + [embedded]
    if carried:
        in_specs.append(whole)
        args.append(before)
        out_specs = [whole, whole]
        out_shape = [jax.ShapeDtypeStruct((k, n * lags // 2), jnp.float32)] * 2
        scratch = [pltpu.VMEM((n * lags, k), jnp.float32)] + scratch
    else:
        out_specs = whole
        out_shape = jax.ShapeDtypeStruct((n * lags, k), jnp.float32)
    return pl.pallas_call(
        functools.partial(correlate_kernel, n, steps, carried),
        grid=(steps,),
        in_specs=in_specs,
        out_specs=out_specs,
        out_shape=out_shape,
        scratch_shapes=scratch,
        compiler_params=pltpu.CompilerParams(vmem_limit_bytes=VMEM),
        cost_estimate=pl.CostEstimate(
            flops=2 * n * lags * LE * width * k,
            bytes_accessed=2 * LE * width * k,
            transcendentals=0,
        ),
    )(*args)


def per_device(n, records, templates, offsets, masks):
    channels = records.shape[0]
    half = channels // 2
    turned = records.T
    first = ring_gather(turned[:, :half], n, True)
    second = ring_gather(turned[:, half:], n, False)
    first_weights = embed(templates, offsets, masks, 0, half)
    second_weights = embed(templates, offsets, masks, half, half)
    partial_sum = correlate(first, first_weights, None)
    mine, other = correlate(second, second_weights, partial_sum)
    return mine + lax.ppermute(other, "chan", [(0, 1), (1, 0)])


def solution(mesh):
    return jax.shard_map(
        functools.partial(per_device, mesh.shape["blk"]),
        mesh=mesh,
        in_specs=(
            P("chan", ("groups", "blk")),
            P(None, ("groups", "blk"), "chan"),
            P(("groups", "blk"), "chan"),
            P(("groups", "blk"), "chan"),
        ),
        out_specs=P(("groups", "blk"), "chan"),
        check_vma=False,
    )
```

time: 811 us -> 117 us (0.14); the launches traced: 796 us -> 117 us
  local copies, waits for them, and re-layouts: 492 us -> 3.54 us
  other arithmetic: 225 us -> 1.7 us
  Pallas kernels: 0 us -> 91.1 us
  matrix products: 51.1 us -> 0 us
  starting transfers between devices: 0.04 us -> 17.5 us
  between operations: 14 us -> 0.15 us
    another operation x4 -> x0, local copies, waits for them, and re-layouts: 206 us -> none  [unfold_lags(): tiled = jnp.tile(segment, (1,) * (segment.ndim - 1) + (LE + 1,))]
    convert_element_type x2 -> x0, local copies, waits for them, and re-layouts: 150 us -> none  [window_matrix(): windows = (shifted * inverse[..., None, :]).astype(jnp.bfloat16)]
    convert_element_type x3 -> x0, other arithmetic: 137 us -> none  [the longest x2 72.4 us: window_matrix(): windows = (shifted * inverse[..., None, :]).astype(jnp.bfloat16)]
    pallas_call x0 -> x4, Pallas kernels: none -> 91.1 us  [the longest x2 57.9 us: correlate(): pl.pallas_call(functools.partial(correlate_kernel, n, steps, carried), gr...]
    slice x2 -> x1, local copies, waits for them, and re-layouts: 86.8 us -> 0.01 us  [per_device(): first = ring_gather(turned[:, :half], n, True)]
    another operation x2 -> x0, other arithmetic: 57.8 us -> none  [window_inverse(): total = lax.reduce_window(square, zero, lax.add, dims, strides, 'VALID')]
    dot_general x2 -> x0, matrix products: 51.1 us -> none  [one_block(): jnp.dot(flat, window_matrix(segment, block), preferred_element_type=jnp.f...]
    while x9 -> x0, local copies, waits for them, and re-layouts: 20.1 us -> none  [the longest x1 18.4 us: per_device(): blocks = lax.map(one_block, jnp.arange(count, dtype=jnp.int32))]
  transfers between devices with their start and end apart: 2 -> 15, of which waited for: 1 -> 4; matrix products, arithmetic and copies ran while one was open for 16% -> 0% of each run, Pallas kernels for 0% -> 53%
where the time goes in v1:
time: 117 us
  Pallas kernels  91.1 us (78%)
  starting transfers between devices  17.5 us (15%)
  local copies, waits for them, and re-layouts  3.54 us (3%)
  waiting for transfers between devices  3.13 us (3%)
  other arithmetic  1.7 us (1%)
    pallas_call x2, Pallas kernels, correlate(): pl.pallas_call(functools.partial(correlate_kernel, n, steps, carried), gr...  57.9 us
    pallas_call x2, Pallas kernels, embed(): pl.pallas_call(embed_kernel, grid=(steps,), in_specs=[pl.BlockSpec((L, k,...  33.2 us
    ppermute x7, starting transfers between devices, ring_gather(): a = lax.ppermute(a, 'blk', up)  13.6 us
    ppermute x7, starting transfers between devices, ring_gather(): b = lax.ppermute(b, 'blk', down)  3.85 us
    unnamed x33, local copies, waits for them, and re-layouts  3.53 us
  transfers between devices with their start and end apart: 15, of which 4 were waited for; matrix products, arithmetic and copies ran while one was open for 0% of the time, Pallas kernels for 53%

profile of v1, /device:TPU:0, one launch (start us, length us, event | category | flops | bytes accessed | tf_op | source)
XLA Modules:
  0.0 117.2 jit_solution(14433663049793091931)
XLA Ops:
  0.0 1.0 copy.5
  1.1 3.1 %collective-permute-start.10 = (bf16[128,256]{1,0:T(8,128)(2,1)S(1)}, bf16[128,256]{1,0:T(8,128)(2,1)S(1)}, u32[]{:S(2)}, u32[]{:S(2)}) collective-permute-start(bf16[128,256]{1,0:T(8,128)(2,1)S(1)} %get-tuple-element.9.refs_0_), channel_id=1, source_target_pairs={{0,4},{4,8},{8,12},{12,14},{14,10},{10,6},{6,2},{2,0},{1,5},{5,9},... | collective-permute-start | bytes 196616 | tf_op jit(solution)/shard_map/ppermute | solution.py:95
  4.1 2.0 %collective-permute-start.7 = (bf16[128,256]{1,0:T(8,128)(2,1)S(1)}, bf16[128,256]{1,0:T(8,128)(2,1)S(1)}, u32[]{:S(2)}, u32[]{:S(2)}) collective-permute-start(bf16[128,256]{1,0:T(8,128)(2,1)S(1)} %get-tuple-element.9.refs_0_), channel_id=1, source_target_pairs={{4,0},{8,4},{12,8},{14,12},{10,14},{6,10},{2,6},{0,2},{5,1},{9,5},... | collective-permute-start | bytes 196616 | tf_op jit(solution)/shard_map/ppermute | solution.py:98
  6.3 2.1 %collective-permute-start.11 = (bf16[128,256]{1,0:T(8,128)(2,1)S(1)}, bf16[128,256]{1,0:T(8,128)(2,1)S(1)}, u32[]{:S(2)}, u32[]{:S(2)}) collective-permute-start(bf16[128,256]{1,0:T(8,128)(2,1)S(1)} %collective-permute-done.10.refs_7_), channel_id=1, source_target_pairs={{0,4},{4,8},{8,12},{12,14},{14,10},{10,6},{6,2},{2,0},{1,5},{5,9},... | collective-permute-start | bytes 196616 | tf_op jit(solution)/shard_map/ppermute | solution.py:95
  8.4 1.6 %collective-permute-start.4 = (bf16[128,256]{1,0:T(8,128)(2,1)S(1)}, bf16[128,256]{1,0:T(8,128)(2,1)S(1)}, u32[]{:S(2)}, u32[]{:S(2)}) collective-permute-start(bf16[128,256]{1,0:T(8,128)(2,1)S(1)} %get-tuple-element.10.refs_0_), channel_id=1, source_target_pairs={{0,4},{4,8},{8,12},{12,14},{14,10},{10,6},{6,2},{2,0},{1,5},{5,9},... | collective-permute-start | bytes 196616 | tf_op jit(solution)/shard_map/ppermute | solution.py:95
  10.0 0.4 collective-permute-start.1
  10.4 0.5 collective-permute-start.8
  11.0 1.7 %collective-permute-start.12 = (bf16[128,256]{1,0:T(8,128)(2,1)S(1)}, bf16[128,256]{1,0:T(8,128)(2,1)S(1)}, u32[]{:S(2)}, u32[]{:S(2)}) collective-permute-start(bf16[128,256]{1,0:T(8,128)(2,1)S(1)} %collective-permute-done.11.refs_6_), channel_id=1, source_target_pairs={{0,4},{4,8},{8,12},{12,14},{14,10},{10,6},{6,2},{2,0},{1,5},{5,9},... | collective-permute-start | bytes 196616 | tf_op jit(solution)/shard_map/ppermute | solution.py:95
  12.9 1.7 %collective-permute-start.5 = (bf16[128,256]{1,0:T(8,128)(2,1)S(1)}, bf16[128,256]{1,0:T(8,128)(2,1)S(1)}, u32[]{:S(2)}, u32[]{:S(2)}) collective-permute-start(bf16[128,256]{1,0:T(8,128)(2,1)S(1)} %collective-permute-done.4.refs_7_), channel_id=1, source_target_pairs={{0,4},{4,8},{8,12},{12,14},{14,10},{10,6},{6,2},{2,0},{1,5},{5,9},... | collective-permute-start | bytes 196616 | tf_op jit(solution)/shard_map/ppermute | solution.py:95
  14.6 0.3 collective-permute-start.2
  15.0 0.9 collective-permute-done.8.refs_2_
  16.0 1.9 %collective-permute-start.13 = (bf16[128,256]{1,0:T(8,128)(2,1)S(1)}, bf16[128,256]{1,0:T(8,128)(2,1)S(1)}, u32[]{:S(2)}, u32[]{:S(2)}) collective-permute-start(bf16[128,256]{1,0:T(8,128)(2,1)S(1)} %collective-permute-done.12.refs_5_), channel_id=1, source_target_pairs={{0,4},{4,8},{8,12},{12,14},{14,10},{10,6},{6,2},{2,0},{1,5},{5,9},... | collective-permute-start | bytes 196616 | tf_op jit(solution)/shard_map/ppermute | solution.py:95
  17.9 16.6 %shard_map.47.refs_8_ = bf16[104,256,128]{2,1,0:T(8,128)(2,1)} custom-call(bf16[100,128,512]{2,1,0:T(8,128)(2,1)} %t_ref.3, s32[128,512]{1,0:T(8,128)} %off_ref.3, s32[128,512]{1,0:T(8,128)} %mask_ref.3), custom_call_target="tpu_custom_call" | custom-call | flops 68157440 | bytes 13631488 | tf_op jit(solution)/shard_map/pallas_call | solution.py:58
  34.6 16.6 %shard_map.46.refs_8_ = bf16[104,256,128]{2,1,0:T(8,128)(2,1)} custom-call(bf16[100,128,512]{2,1,0:T(8,128)(2,1)} %t_ref.3, s32[128,512]{1,0:T(8,128)} %off_ref.3, s32[128,512]{1,0:T(8,128)} %mask_ref.3), custom_call_target="tpu_custom_call" | custom-call | flops 68157440 | bytes 13631488 | tf_op jit(solution)/shard_map/pallas_call | solution.py:58
  51.2 1.6 %collective-permute-start.6 = (bf16[128,256]{1,0:T(8,128)(2,1)S(1)}, bf16[128,256]{1,0:T(8,128)(2,1)S(1)}, u32[]{:S(2)}, u32[]{:S(2)}) collective-permute-start(bf16[128,256]{1,0:T(8,128)(2,1)S(1)} %collective-permute-done.5.refs_6_), channel_id=1, source_target_pairs={{0,4},{4,8},{8,12},{12,14},{14,10},{10,6},{6,2},{2,0},{1,5},{5,9},... | collective-permute-start | bytes 196616 | tf_op jit(solution)/shard_map/ppermute | solution.py:95
  52.8 0.5 collective-permute-start.3
  53.3 0.6 copy-done.13
  53.9 0.6 copy-done.15
  54.5 28.7 %shard_map.48.refs_9_ = f32[1024,128]{1,0:T(8,128)} custom-call(bf16[128,256]{1,0:T(8,128)(2,1)} %copy-done.1, bf16[128,256]{1,0:T(8,128)(2,1)} %copy-done.6, bf16[128,256]{1,0:T(8,128)(2,1)} %copy-done.9, bf16[128,256]{1,0:T(8,128)(2,1)} %copy-done.13, bf16[128,256]{1,0:T(8,128)(2,1)} %copy-done.15, bf16[128,256]{1,0:T(8,128)(2,1)} %copy-done.11, ...), custom_call_target="tpu_custom_call" | custom-call | flops 6979321856 | bytes 6815744 | tf_op jit(solution)/shard_map/pallas_call | solution.py:230
  83.3 0.6 copy-done.12
  83.9 0.6 copy-done.14
  84.5 29.2 %shard_map.49 = (f32[128,512]{1,0:T(8,128)}, f32[128,512]{1,0:T(8,128)}) custom-call(bf16[128,256]{1,0:T(8,128)(2,1)} %copy-done, bf16[128,256]{1,0:T(8,128)(2,1)} %copy-done.2, bf16[128,256]{1,0:T(8,128)(2,1)} %copy-done.5, bf16[128,256]{1,0:T(8,128)(2,1)} %copy-done.10, bf16[128,256]{1,0:T(8,128)(2,1)} %copy-done.14, bf16[128,256]{1,0:T(8,128)(2,1)} %copy-done.12, ...), custom_call_target="tpu_custom_call" | custom-call | flops 6979321856 | bytes 6815744 | tf_op jit(solution)/shard_map/pallas_call | solution.py:230
  113.7 1.7 %collective-permute-done.14 = f32[128,512]{1,0:T(8,128)S(1)} collective-permute-done((f32[128,512]{1,0:T(8,128)}, f32[128,512]{1,0:T(8,128)S(1)}, u32[]{:S(2)}, u32[]{:S(2)}) %collective-permute-start.14) | collective-permute-done | bytes 262176 | tf_op jit(solution)/shard_map/ppermute | solution.py:256
  115.5 1.7 %add.3 = f32[128,512]{1,0:T(8,128)} add(f32[128,512]{1,0:T(8,128)} %get-tuple-element.7, f32[128,512]{1,0:T(8,128)S(1)} %collective-permute-done.14) | non-fusion elementwise | flops 65536 | bytes 786432 | tf_op jit(solution)/shard_map/add | solution.py:256
  (45 shorter events, 0.7 us)
Async XLA Ops:
  1.0 33.5 %copy-start = (bf16[128,256]{1,0:T(8,128)(2,1)}, bf16[128,256]{1,0:T(8,128)(2,1)S(1)}, u32[]{:S(2)}) copy-start(bf16[128,256]{1,0:T(8,128)(2,1)S(1)} %get-tuple-element.10.refs_0_) | copy-start | bytes 196612
  1.0 33.4 %copy-start.1 = (bf16[128,256]{1,0:T(8,128)(2,1)}, bf16[128,256]{1,0:T(8,128)(2,1)S(1)}, u32[]{:S(2)}) copy-start(bf16[128,256]{1,0:T(8,128)(2,1)S(1)} %get-tuple-element.9.refs_0_) | copy-start | bytes 196612
  1.1 5.3 %collective-permute-start.10 = (bf16[128,256]{1,0:T(8,128)(2,1)S(1)}, bf16[128,256]{1,0:T(8,128)(2,1)S(1)}, u32[]{:S(2)}, u32[]{:S(2)}) collective-permute-start(bf16[128,256]{1,0:T(8,128)(2,1)S(1)} %get-tuple-element.9.refs_0_), channel_id=1, source_target_pairs={{0,4},{4,8},{8,12},{12,14},{14,10},{10,6},{6,2},{2,0},{1,5},{5,9},... | collective-permute-start | bytes 196616 | tf_op jit(solution)/shard_map/ppermute | solution.py:95
  4.1 5.8 %collective-permute-start = (bf16[128,256]{1,0:T(8,128)(2,1)S(1)}, bf16[128,256]{1,0:T(8,128)(2,1)S(1)}, u32[]{:S(2)}, u32[]{:S(2)}) collective-permute-start(bf16[128,256]{1,0:T(8,128)(2,1)S(1)} %get-tuple-element.10.refs_0_), channel_id=1, source_target_pairs={{4,0},{8,4},{12,8},{14,12},{10,14},{6,10},{2,6},{0,2},{5,1},{9,5},... | collective-permute-start | bytes 196616 | tf_op jit(solution)/shard_map/ppermute | solution.py:98
  4.1 6.3 %collective-permute-start.7 = (bf16[128,256]{1,0:T(8,128)(2,1)S(1)}, bf16[128,256]{1,0:T(8,128)(2,1)S(1)}, u32[]{:S(2)}, u32[]{:S(2)}) collective-permute-start(bf16[128,256]{1,0:T(8,128)(2,1)S(1)} %get-tuple-element.9.refs_0_), channel_id=1, source_target_pairs={{4,0},{8,4},{12,8},{14,12},{10,14},{6,10},{2,6},{0,2},{5,1},{9,5},... | collective-permute-start | bytes 196616 | tf_op jit(solution)/shard_map/ppermute | solution.py:98
  6.3 28.2 %copy-start.3 = (bf16[128,256]{1,0:T(8,128)(2,1)}, bf16[128,256]{1,0:T(8,128)(2,1)S(1)}, u32[]{:S(2)}) copy-start(bf16[128,256]{1,0:T(8,128)(2,1)S(1)} %collective-permute-done.10.refs_7_) | copy-start | bytes 196612
  6.3 4.6 %collective-permute-start.11 = (bf16[128,256]{1,0:T(8,128)(2,1)S(1)}, bf16[128,256]{1,0:T(8,128)(2,1)S(1)}, u32[]{:S(2)}, u32[]{:S(2)}) collective-permute-start(bf16[128,256]{1,0:T(8,128)(2,1)S(1)} %collective-permute-done.10.refs_7_), channel_id=1, source_target_pairs={{0,4},{4,8},{8,12},{12,14},{14,10},{10,6},{6,2},{2,0},{1,5},{5,9},... | collective-permute-start | bytes 196616 | tf_op jit(solution)/shard_map/ppermute | solution.py:95
  8.4 4.5 %collective-permute-start.4 = (bf16[128,256]{1,0:T(8,128)(2,1)S(1)}, bf16[128,256]{1,0:T(8,128)(2,1)S(1)}, u32[]{:S(2)}, u32[]{:S(2)}) collective-permute-start(bf16[128,256]{1,0:T(8,128)(2,1)S(1)} %get-tuple-element.10.refs_0_), channel_id=1, source_target_pairs={{0,4},{4,8},{8,12},{12,14},{14,10},{10,6},{6,2},{2,0},{1,5},{5,9},... | collective-permute-start | bytes 196616 | tf_op jit(solution)/shard_map/ppermute | solution.py:95
  10.0 24.5 %copy-start.2 = (bf16[128,256]{1,0:T(8,128)(2,1)}, bf16[128,256]{1,0:T(8,128)(2,1)S(1)}, u32[]{:S(2)}) copy-start(bf16[128,256]{1,0:T(8,128)(2,1)S(1)} %collective-permute-done.refs_1_) | copy-start | bytes 196612
  10.0 4.6 %collective-permute-start.1 = (bf16[128,256]{1,0:T(8,128)(2,1)S(1)}, bf16[128,256]{1,0:T(8,128)(2,1)S(1)}, u32[]{:S(2)}, u32[]{:S(2)}) collective-permute-start(bf16[128,256]{1,0:T(8,128)(2,1)S(1)} %collective-permute-done.refs_1_), channel_id=1, source_target_pairs={{4,0},{8,4},{12,8},{14,12},{10,14},{6,10},{2,6},{0,2},{5,1},{9,5},... | collective-permute-start | bytes 196616 | tf_op jit(solution)/shard_map/ppermute | solution.py:98
  10.4 24.1 %copy-start.6 = (bf16[128,256]{1,0:T(8,128)(2,1)}, bf16[128,256]{1,0:T(8,128)(2,1)S(1)}, u32[]{:S(2)}) copy-start(bf16[128,256]{1,0:T(8,128)(2,1)S(1)} %collective-permute-done.7.refs_1_) | copy-start | bytes 196612
  10.4 5.4 %collective-permute-start.8 = (bf16[128,256]{1,0:T(8,128)(2,1)S(1)}, bf16[128,256]{1,0:T(8,128)(2,1)S(1)}, u32[]{:S(2)}, u32[]{:S(2)}) collective-permute-start(bf16[128,256]{1,0:T(8,128)(2,1)S(1)} %collective-permute-done.7.refs_1_), channel_id=1, source_target_pairs={{4,0},{8,4},{12,8},{14,12},{10,14},{6,10},{2,6},{0,2},{5,1},{9,5},... | collective-permute-start | bytes 196616 | tf_op jit(solution)/shard_map/ppermute | solution.py:98
  11.0 23.6 %copy-start.7 = (bf16[128,256]{1,0:T(8,128)(2,1)}, bf16[128,256]{1,0:T(8,128)(2,1)S(1)}, u32[]{:S(2)}) copy-start(bf16[128,256]{1,0:T(8,128)(2,1)S(1)} %collective-permute-done.11.refs_6_) | copy-start | bytes 196612
  11.0 5.0 %collective-permute-start.12 = (bf16[128,256]{1,0:T(8,128)(2,1)S(1)}, bf16[128,256]{1,0:T(8,128)(2,1)S(1)}, u32[]{:S(2)}, u32[]{:S(2)}) collective-permute-start(bf16[128,256]{1,0:T(8,128)(2,1)S(1)} %collective-permute-done.11.refs_6_), channel_id=1, source_target_pairs={{0,4},{4,8},{8,12},{12,14},{14,10},{10,6},{6,2},{2,0},{1,5},{5,9},... | collective-permute-start | bytes 196616 | tf_op jit(solution)/shard_map/ppermute | solution.py:95
  12.9 21.6 %copy-start.4 = (bf16[128,256]{1,0:T(8,128)(2,1)}, bf16[128,256]{1,0:T(8,128)(2,1)S(1)}, u32[]{:S(2)}) copy-start(bf16[128,256]{1,0:T(8,128)(2,1)S(1)} %collective-permute-done.4.refs_7_) | copy-start | bytes 196612
  12.9 38.3 %collective-permute-start.5 = (bf16[128,256]{1,0:T(8,128)(2,1)S(1)}, bf16[128,256]{1,0:T(8,128)(2,1)S(1)}, u32[]{:S(2)}, u32[]{:S(2)}) collective-permute-start(bf16[128,256]{1,0:T(8,128)(2,1)S(1)} %collective-permute-done.4.refs_7_), channel_id=1, source_target_pairs={{0,4},{4,8},{8,12},{12,14},{14,10},{10,6},{6,2},{2,0},{1,5},{5,9},... | collective-permute-start | bytes 196616 | tf_op jit(solution)/shard_map/ppermute | solution.py:95
  14.6 38.2 %collective-permute-start.2 = (bf16[128,256]{1,0:T(8,128)(2,1)S(1)}, bf16[128,256]{1,0:T(8,128)(2,1)S(1)}, u32[]{:S(2)}, u32[]{:S(2)}) collective-permute-start(bf16[128,256]{1,0:T(8,128)(2,1)S(1)} %collective-permute-done.1.refs_2_), channel_id=1, source_target_pairs={{4,0},{8,4},{12,8},{14,12},{10,14},{6,10},{2,6},{0,2},{5,1},{9,5},... | collective-permute-start | bytes 196616 | tf_op jit(solution)/shard_map/ppermute | solution.py:98
  15.8 37.4 %collective-permute-start.9 = (bf16[128,256]{1,0:T(8,128)(2,1)S(1)}, bf16[128,256]{1,0:T(8,128)(2,1)S(1)}, u32[]{:S(2)}, u32[]{:S(2)}) collective-permute-start(bf16[128,256]{1,0:T(8,128)(2,1)S(1)} %collective-permute-done.8.refs_2_), channel_id=1, source_target_pairs={{4,0},{8,4},{12,8},{14,12},{10,14},{6,10},{2,6},{0,2},{5,1},{9,5},... | collective-permute-start | bytes 196616 | tf_op jit(solution)/shard_map/ppermute | solution.py:98
  16.0 37.3 %collective-permute-start.13 = (bf16[128,256]{1,0:T(8,128)(2,1)S(1)}, bf16[128,256]{1,0:T(8,128)(2,1)S(1)}, u32[]{:S(2)}, u32[]{:S(2)}) collective-permute-start(bf16[128,256]{1,0:T(8,128)(2,1)S(1)} %collective-permute-done.12.refs_5_), channel_id=1, source_target_pairs={{0,4},{4,8},{8,12},{12,14},{14,10},{10,6},{6,2},{2,0},{1,5},{5,9},... | collective-permute-start | bytes 196616 | tf_op jit(solution)/shard_map/ppermute | solution.py:95
  51.2 32.0 %copy-start.8 = (bf16[128,256]{1,0:T(8,128)(2,1)}, bf16[128,256]{1,0:T(8,128)(2,1)S(1)}, u32[]{:S(2)}) copy-start(bf16[128,256]{1,0:T(8,128)(2,1)S(1)} %collective-permute-done.5.refs_6_) | copy-start | bytes 196612
  51.2 32.0 %collective-permute-start.6 = (bf16[128,256]{1,0:T(8,128)(2,1)S(1)}, bf16[128,256]{1,0:T(8,128)(2,1)S(1)}, u32[]{:S(2)}, u32[]{:S(2)}) collective-permute-start(bf16[128,256]{1,0:T(8,128)(2,1)S(1)} %collective-permute-done.5.refs_6_), channel_id=1, source_target_pairs={{0,4},{4,8},{8,12},{12,14},{14,10},{10,6},{6,2},{2,0},{1,5},{5,9},... | collective-permute-start | bytes 196616 | tf_op jit(solution)/shard_map/ppermute | solution.py:95
  52.8 30.4 %copy-start.10 = (bf16[128,256]{1,0:T(8,128)(2,1)}, bf16[128,256]{1,0:T(8,128)(2,1)S(1)}, u32[]{:S(2)}) copy-start(bf16[128,256]{1,0:T(8,128)(2,1)S(1)} %collective-permute-done.2.refs_3_) | copy-start | bytes 196612
  52.8 30.4 %collective-permute-start.3 = (bf16[128,256]{1,0:T(8,128)(2,1)S(1)}, bf16[128,256]{1,0:T(8,128)(2,1)S(1)}, u32[]{:S(2)}, u32[]{:S(2)}) collective-permute-start(bf16[128,256]{1,0:T(8,128)(2,1)S(1)} %collective-permute-done.2.refs_3_), channel_id=1, source_target_pairs={{4,0},{8,4},{12,8},{14,12},{10,14},{6,10},{2,6},{0,2},{5,1},{9,5},... | collective-permute-start | bytes 196616 | tf_op jit(solution)/shard_map/ppermute | solution.py:98
  113.7 1.7 %collective-permute-start.14 = (f32[128,512]{1,0:T(8,128)}, f32[128,512]{1,0:T(8,128)S(1)}, u32[]{:S(2)}, u32[]{:S(2)}) collective-permute-start(f32[128,512]{1,0:T(8,128)} %get-tuple-element.8), channel_id=1, source_target_pairs={{0,1},{1,0},{2,3},{3,2},{4,5},{5,4},{6,7},{7,6},{8,9},{9,8},{10,11... | collective-permute-start | bytes 786440 | tf_op jit(solution)/shard_map/ppermute | solution.py:256
  (7 other events, 59.7 us)

commit v2 on v1

v2 whole, which is shorter than its diff:
```python
import functools

import jax
import jax.numpy as jnp
from jax import lax
from jax.experimental import pallas as pl
from jax.experimental.pallas import tpu as pltpu
from jax.sharding import PartitionSpec as P

L = 100
LE = 104
SPAN = LE - L
EPS = 1e-06
LANES = 128
PIECES = 4
ROWS = 16
TAPS = 4
TILE = 512
GROUP = 8
VMEM = 56 * 1024 * 1024


def embed_kernel(t_ref, off_ref, mask_ref, e_ref):
    rows, cols = off_ref.shape

    def square(l, acc):
        v = t_ref[l].astype(jnp.float32)
        return acc + v * v

    total = lax.fori_loop(0, L, square, jnp.zeros((rows, cols), jnp.float32), unroll=4)
    scale = lax.rsqrt(total / L + EPS) * mask_ref[...].astype(jnp.float32) / L
    off = off_ref[...].astype(jnp.float32).astype(jnp.bfloat16)
    zero = jnp.zeros((rows, cols), jnp.bfloat16)

    def place(j, read):
        value = read(j)
        for d in range(1, SPAN + 1):
            value = jnp.where(off == d, read(j - d), value)
        e_ref[j] = (value.astype(jnp.float32) * scale).astype(jnp.bfloat16)

    def edge(l):
        return t_ref[l] if 0 <= l < L else zero

    for j in range(SPAN):
        place(j, edge)
    for j in range(L, LE):
        place(j, edge)

    def body(j, carry):
        place(j, lambda l: t_ref[l])
        return carry

    lax.fori_loop(SPAN, L, body, 0, unroll=4)


def embed(templates, offsets, masks, piece):
    k, channels = offsets.shape
    rows = k // PIECES
    steps = rows // ROWS
    first = piece * steps
    return pl.pallas_call(
        embed_kernel,
        grid=(steps,),
        in_specs=[
            pl.BlockSpec((L, ROWS, channels), lambda i: (0, first + i, 0)),
            pl.BlockSpec((ROWS, channels), lambda i: (first + i, 0)),
            pl.BlockSpec((ROWS, channels), lambda i: (first + i, 0)),
        ],
        out_specs=pl.BlockSpec((LE, ROWS, channels), lambda i: (0, i, 0)),
        out_shape=jax.ShapeDtypeStruct((LE, rows, channels), jnp.bfloat16),
        compiler_params=pltpu.CompilerParams(vmem_limit_bytes=VMEM),
        cost_estimate=pl.CostEstimate(
            flops=20 * LE * rows * channels,
            bytes_accessed=2 * 2 * LE * rows * channels,
            transcendentals=0,
        ),
    )(templates, offsets, masks)


def ring_position(b, n):
    z, y = b // 2, b % 2
    return z * (1 - y) + (n - 1 - z) * y


def ring_block(p, n):
    half = n // 2
    low = (p < half) * 1 if isinstance(p, int) else (p < half).astype(jnp.int32)
    return low * (2 * p) + (1 - low) * (2 * (n - 1 - p) + 1)


def ring_gather(x, n):
    order = [ring_block(p, n) for p in range(n)]
    up = [(order[p], order[(p + 1) % n]) for p in range(n)]
    down = [(order[(p + 1) % n], order[p]) for p in range(n)]
    blocks = {0: x}
    a = b = x
    for step in range(1, n // 2 + 1):
        a = lax.ppermute(a, "blk", up)
        blocks[n - step] = a
        if step < n // 2:
            b = lax.ppermute(b, "blk", down)
            blocks[step] = b
    return [blocks[d] for d in range(n)]


def prepare(n, block_refs, flat_ref, x_ref, g_ref, n_ref):
    lags, width = block_refs[0].shape
    me = ring_position(lax.axis_index("blk"), n)
    for d in range(n):
        where = ring_block(lax.rem(me + d, n), n)
        for w in range(width // LANES):
            flat_ref[w, pl.ds(pl.multiple_of(where * lags, lags), lags), :] = block_refs[d][
                :, w * LANES : (w + 1) * LANES
            ].astype(jnp.float32)
    for w in range(width // LANES):
        flat_ref[w, n * lags :, :] = jnp.zeros((lags, LANES), jnp.float32)

    groups = (lags + LE) // GROUP

    def spread(g, carry):
        sums = [None] * (width // LANES)
        for r in range(GROUP):
            u = g * GROUP + r
            for w in range(width // LANES):
                value = flat_ref[w, pl.ds(u, n, stride=lags), :]
                x_ref[u, :, w * LANES : (w + 1) * LANES] = value
                square = value * value
                sums[w] = square if r == 0 else sums[w] + square
        for w in range(width // LANES):
            g_ref[g, :, w * LANES : (w + 1) * LANES] = sums[w]
        return carry

    lax.fori_loop(0, groups, spread, 0)
    x_ref[lags + LE :] = jnp.zeros((2 * TAPS, n, width), jnp.float32)

    def norms(g, carry):
        middle = g_ref[g + 1]
        for i in range(2, LE // GROUP):
            middle = middle + g_ref[g + i]
        tails = [None] * GROUP
        tail = None
        for r in range(GROUP - 1, -1, -1):
            value = x_ref[g * GROUP + r]
            square = value * value
            tail = square if tail is None else tail + square
            tails[r] = tail
        head = None
        for r in range(GROUP):
            total = middle + tails[r]
            if r > 0:
                value = x_ref[g * GROUP + LE + r - 1]
                square = value * value
                head = square if head is None else head + square
                total = total + head
            n_ref[g * GROUP + r] = lax.rsqrt(total / LE + EPS)
        return carry

    lax.fori_loop(0, lags // GROUP, norms, 0)


def build(x_ref, n_ref, w_ref, n, tap0, m):
    width = x_ref.shape[-1]
    for u8 in range(TILE // (n * 8)):
        u = m * (TILE // n) + u8 * 8
        rows = pl.ds(pl.multiple_of(u * n, 8 * n), 8 * n)
        for w in range(width // LANES):
            lanes = slice(w * LANES, (w + 1) * LANES)
            norm = n_ref[pl.ds(u, 8), :, lanes]
            xs = x_ref[pl.ds(u + tap0, TAPS + 7), :, lanes]
            for tap in range(TAPS):
                value = (xs[tap : tap + 8] * norm).reshape(8 * n, LANES).astype(jnp.bfloat16)
                w_ref[rows, tap * width + w * LANES : tap * width + (w + 1) * LANES] = value


def correlate_kernel(n, steps, *refs):
    blocks = refs[:n]
    e_refs = refs[n : n + PIECES]
    mine_ref, other_ref, acc_ref, flat_ref, x_ref, g_ref, n_ref, even_ref, odd_ref = refs[n + PIECES :]
    lags, width = blocks[0].shape
    tiles = n * lags // TILE
    step = pl.program_id(0)

    @pl.when(step == 0)
    def _():
        prepare(n, blocks, flat_ref, x_ref, g_ref, n_ref)
        acc_ref[...] = jnp.zeros_like(acc_ref)

        def first(m, carry):
            build(x_ref, n_ref, even_ref, n, 0, m)
            return carry

        lax.fori_loop(0, tiles, first, 0)

    def advance(now_ref, later_ref, part, tap0):
        weights = jnp.concatenate(
            [
                jnp.concatenate([e_ref[part * TAPS + tap] for e_ref in e_refs], axis=0)
                for tap in range(TAPS)
            ],
            axis=1,
        )

        def tile(m, carry):
            rows = pl.ds(pl.multiple_of(m * TILE, TILE), TILE)
            acc_ref[rows, :] += lax.dot_general(
                now_ref[rows, :],
                weights,
                (((1,), (1,)), ((), ())),
                preferred_element_type=jnp.float32,
            )
            build(x_ref, n_ref, later_ref, n, tap0, m)
            return carry

        lax.fori_loop(0, tiles, tile, 0)

    advance(even_ref, odd_ref, 0, step * 2 * TAPS + TAPS)
    advance(odd_ref, even_ref, 1, step * 2 * TAPS + 2 * TAPS)

    @pl.when(step == steps - 1)
    def _():
        core = lax.axis_index("chan")
        half = n // 2
        for out_ref, first in ((mine_ref, core * half), (other_ref, (1 - core) * half)):
            for v in range(half):
                value = acc_ref[pl.ds(first + v, lags, stride=n), :]
                out_ref[:, v * lags : (v + 1) * lags] = value.T


def correlate(blocks, pieces):
    n = len(blocks)
    lags, width = blocks[0].shape
    k = PIECES * pieces[0].shape[1]
    steps = LE // (2 * TAPS)
    whole = pl.BlockSpec(memory_space=pltpu.VMEM)
    e_spec = pl.BlockSpec((2 * TAPS, k // PIECES, width), lambda i: (i, 0, 0))
    return pl.pallas_call(
        functools.partial(correlate_kernel, n, steps),
        grid=(steps,),
        in_specs=[whole] * n + [e_spec] * PIECES,
        out_specs=[whole, whole],
        out_shape=[jax.ShapeDtypeStruct((k, n * lags // 2), jnp.float32)] * 2,
        scratch_shapes=[
            pltpu.VMEM((n * lags, k), jnp.float32),
            pltpu.VMEM((width // LANES, (n + 1) * lags, LANES), jnp.float32),
            pltpu.VMEM((lags + LE + 2 * TAPS, n, width), jnp.float32),
            pltpu.VMEM(((lags + LE) // GROUP, n, width), jnp.float32),
            pltpu.VMEM((lags, n, width), jnp.float32),
            pltpu.VMEM((n * lags, TAPS * width), jnp.bfloat16),
            pltpu.VMEM((n * lags, TAPS * width), jnp.bfloat16),
        ],
        compiler_params=pltpu.CompilerParams(vmem_limit_bytes=VMEM),
        cost_estimate=pl.CostEstimate(
            flops=2 * n * lags * LE * width * k,
            bytes_accessed=2 * LE * width * k,
            transcendentals=0,
        ),
    )(*blocks, *pieces)


def per_device(n, records, templates, offsets, masks):
    blocks = ring_gather(records.T, n)
    pieces = [embed(templates, offsets, masks, piece) for piece in range(PIECES)]
    mine, other = correlate(blocks, pieces)
    return mine + lax.ppermute(other, "chan", [(0, 1), (1, 0)])


def solution(mesh):
    return jax.shard_map(
        functools.partial(per_device, mesh.shape["blk"]),
        mesh=mesh,
        in_specs=(
            P("chan", ("groups", "blk")),
            P(None, ("groups", "blk"), "chan"),
            P(("groups", "blk"), "chan"),
            P(("groups", "blk"), "chan"),
        ),
        out_specs=P(("groups", "blk"), "chan"),
        check_vma=False,
    )
```

time: 117 us -> 109 us (0.932)
  waiting for transfers between devices: 3.13 us -> 11.5 us
  starting transfers between devices: 17.5 us -> 9.23 us
  Pallas kernels: 91.1 us -> 83.9 us
  local copies, waits for them, and re-layouts: 3.54 us -> 2.31 us
    ppermute x7 -> x4, waiting for transfers between devices: 0.49 us -> 9.73 us  [ring_gather(): a = lax.ppermute(a, 'blk', up)]
    pallas_call x4 -> x5, Pallas kernels: 91.1 us -> 83.9 us  [the longest x1 64 us: correlate(): pl.pallas_call(functools.partial(correlate_kernel, n, steps), grid=(steps...]
    ppermute x7 -> x4, starting transfers between devices: 13.6 us -> 8.76 us  [ring_gather(): a = lax.ppermute(a, 'blk', up)]
    ppermute x7 -> x3, starting transfers between devices: 3.85 us -> 0.47 us  [ring_gather(): b = lax.ppermute(b, 'blk', down)]
    unnamed x33 -> x17, local copies, waits for them, and re-layouts: 3.53 us -> 2.31 us
  transfers between devices with their start and end apart: 15 -> 8, of which waited for: 4 -> 4; matrix products, arithmetic and copies ran while one was open for 0% -> 0% of each run, Pallas kernels for 53% -> 18%
where the time goes in v2:
time: 109 us
  Pallas kernels  83.9 us (77%)
  waiting for transfers between devices  11.5 us (11%)
  starting transfers between devices  9.23 us (8%)
  local copies, waits for them, and re-layouts  2.31 us (2%)
  other arithmetic  1.7 us (2%)
    pallas_call x1, Pallas kernels, correlate(): pl.pallas_call(functools.partial(correlate_kernel, n, steps), grid=(steps...  64 us
    pallas_call x4, Pallas kernels, embed(): pl.pallas_call(embed_kernel, grid=(steps,), in_specs=[pl.BlockSpec((L, RO...  19.9 us
    ppermute x4, waiting for transfers between devices, ring_gather(): a = lax.ppermute(a, 'blk', up)  9.73 us
    ppermute x4, starting transfers between devices, ring_gather(): a = lax.ppermute(a, 'blk', up)  8.76 us
    unnamed x17, local copies, waits for them, and re-layouts  2.31 us
  transfers between devices with their start and end apart: 8, of which 4 were waited for; matrix products, arithmetic and copies ran while one was open for 0% of the time, Pallas kernels for 18%

profile of v2, /device:TPU:0, one launch (start us, length us, event | category | flops | bytes accessed | tf_op | source)
XLA Modules:
  0.0 108.7 jit_solution(10660604543551092319)
XLA Ops:
  0.0 1.0 copy.5
  1.0 3.1 %collective-permute-start.3 = (bf16[128,512]{1,0:T(8,128)(2,1)S(1)}, bf16[128,512]{1,0:T(8,128)(2,1)S(1)}, u32[]{:S(2)}, u32[]{:S(2)}) collective-permute-start(bf16[128,512]{1,0:T(8,128)(2,1)S(1)} %bitcast.1), channel_id=1, source_target_pairs={{0,4},{4,8},{8,12},{12,14},{14,10},{10,6},{6,2},{2,0},{1,5},{5,9},... | collective-permute-start | bytes 393224 | tf_op jit(solution)/shard_map/ppermute | solution.py:98
  4.1 0.0 collective-permute-start
  4.1 3.4 %collective-permute-done.3.refs_7_ = bf16[128,512]{1,0:T(8,128)(2,1)S(1)} collective-permute-done((bf16[128,512]{1,0:T(8,128)(2,1)S(1)}, bf16[128,512]{1,0:T(8,128)(2,1)S(1)}, u32[]{:S(2)}, u32[]{:S(2)}) %collective-permute-start.3) | collective-permute-done | bytes 131104 | tf_op jit(solution)/shard_map/ppermute | solution.py:98
  7.5 1.8 %collective-permute-start.4 = (bf16[128,512]{1,0:T(8,128)(2,1)S(1)}, bf16[128,512]{1,0:T(8,128)(2,1)S(1)}, u32[]{:S(2)}, u32[]{:S(2)}) collective-permute-start(bf16[128,512]{1,0:T(8,128)(2,1)S(1)} %collective-permute-done.3.refs_7_), channel_id=1, source_target_pairs={{0,4},{4,8},{8,12},{12,14},{14,10},{10,6},{6,2},{2,0},{1,5},{5,9},... | collective-permute-start | bytes 393224 | tf_op jit(solution)/shard_map/ppermute | solution.py:98
  9.3 0.0 collective-permute-done.refs_1_
  9.3 0.2 collective-permute-start.1
  9.6 2.9 %collective-permute-done.4.refs_6_ = bf16[128,512]{1,0:T(8,128)(2,1)S(1)} collective-permute-done((bf16[128,512]{1,0:T(8,128)(2,1)S(1)}, bf16[128,512]{1,0:T(8,128)(2,1)S(1)}, u32[]{:S(2)}, u32[]{:S(2)}) %collective-permute-start.4) | collective-permute-done | bytes 131104 | tf_op jit(solution)/shard_map/ppermute | solution.py:98
  12.5 1.8 %collective-permute-start.5 = (bf16[128,512]{1,0:T(8,128)(2,1)S(1)}, bf16[128,512]{1,0:T(8,128)(2,1)S(1)}, u32[]{:S(2)}, u32[]{:S(2)}) collective-permute-start(bf16[128,512]{1,0:T(8,128)(2,1)S(1)} %collective-permute-done.4.refs_6_), channel_id=1, source_target_pairs={{0,4},{4,8},{8,12},{12,14},{14,10},{10,6},{6,2},{2,0},{1,5},{5,9},... | collective-permute-start | bytes 393224 | tf_op jit(solution)/shard_map/ppermute | solution.py:98
  14.3 0.0 collective-permute-done.1.refs_2_
  14.3 0.2 collective-permute-start.2
  14.5 3.4 %collective-permute-done.5.refs_5_ = bf16[128,512]{1,0:T(8,128)(2,1)S(1)} collective-permute-done((bf16[128,512]{1,0:T(8,128)(2,1)S(1)}, bf16[128,512]{1,0:T(8,128)(2,1)S(1)}, u32[]{:S(2)}, u32[]{:S(2)}) %collective-permute-start.5) | collective-permute-done | bytes 131104 | tf_op jit(solution)/shard_map/ppermute | solution.py:98
  17.9 2.1 %collective-permute-start.6 = (bf16[128,512]{1,0:T(8,128)(2,1)S(1)}, bf16[128,512]{1,0:T(8,128)(2,1)S(1)}, u32[]{:S(2)}, u32[]{:S(2)}) collective-permute-start(bf16[128,512]{1,0:T(8,128)(2,1)S(1)} %collective-permute-done.5.refs_5_), channel_id=1, source_target_pairs={{0,4},{4,8},{8,12},{12,14},{14,10},{10,6},{6,2},{2,0},{1,5},{5,9},... | collective-permute-start | bytes 393224 | tf_op jit(solution)/shard_map/ppermute | solution.py:98
  20.0 5.0 %shard_map.47.refs_9_ = bf16[104,32,512]{2,1,0:T(8,128)(2,1)} custom-call(bf16[100,128,512]{2,1,0:T(8,128)(2,1)} %t_ref.7, s32[128,512]{1,0:T(8,128)} %off_ref.7, s32[128,512]{1,0:T(8,128)} %mask_ref.7), custom_call_target="tpu_custom_call" | custom-call | flops 34078720 | bytes 6815744 | tf_op jit(solution)/shard_map/pallas_call | solution.py:61
  25.0 5.0 %shard_map.46.refs_8_ = bf16[104,32,512]{2,1,0:T(8,128)(2,1)} custom-call(bf16[100,128,512]{2,1,0:T(8,128)(2,1)} %t_ref.7, s32[128,512]{1,0:T(8,128)} %off_ref.7, s32[128,512]{1,0:T(8,128)} %mask_ref.7), custom_call_target="tpu_custom_call" | custom-call | flops 34078720 | bytes 6815744 | tf_op jit(solution)/shard_map/pallas_call | solution.py:61
  30.0 5.0 %shard_map.49.refs_11_ = bf16[104,32,512]{2,1,0:T(8,128)(2,1)} custom-call(bf16[100,128,512]{2,1,0:T(8,128)(2,1)} %t_ref.7, s32[128,512]{1,0:T(8,128)} %off_ref.7, s32[128,512]{1,0:T(8,128)} %mask_ref.7), custom_call_target="tpu_custom_call" | custom-call | flops 34078720 | bytes 6815744 | tf_op jit(solution)/shard_map/pallas_call | solution.py:61
  35.0 5.0 %shard_map.48.refs_10_ = bf16[104,32,512]{2,1,0:T(8,128)(2,1)} custom-call(bf16[100,128,512]{2,1,0:T(8,128)(2,1)} %t_ref.7, s32[128,512]{1,0:T(8,128)} %off_ref.7, s32[128,512]{1,0:T(8,128)} %mask_ref.7), custom_call_target="tpu_custom_call" | custom-call | flops 34078720 | bytes 6815744 | tf_op jit(solution)/shard_map/pallas_call | solution.py:61
  40.0 0.0 collective-permute-done.6.refs_4_
  40.0 0.6 copy-done.6
  40.6 0.6 copy-done.7
  41.3 64.0 %shard_map.50 = (f32[128,512]{1,0:T(8,128)}, f32[128,512]{1,0:T(8,128)}) custom-call(bf16[128,512]{1,0:T(8,128)(2,1)} %bitcast.3, bf16[128,512]{1,0:T(8,128)(2,1)} %copy-done.2, bf16[128,512]{1,0:T(8,128)(2,1)} %copy-done.4, bf16[128,512]{1,0:T(8,128)(2,1)} %copy-done.6, bf16[128,512]{1,0:T(8,128)(2,1)} %copy-done.7, bf16[128,512]{1,0:T(8,128)(2,1)} %copy-done.5, ...), custom_call_target="tpu_custom_call" | custom-call | flops 13958643712 | bytes 13631488 | tf_op jit(solution)/shard_map/pallas_call | solution.py:236
  105.3 0.0 collective-permute-start.7
  105.3 1.7 %collective-permute-done.7 = f32[128,512]{1,0:T(8,128)S(1)} collective-permute-done((f32[128,512]{1,0:T(8,128)}, f32[128,512]{1,0:T(8,128)S(1)}, u32[]{:S(2)}, u32[]{:S(2)}) %collective-permute-start.7) | collective-permute-done | bytes 262176 | tf_op jit(solution)/shard_map/ppermute | solution.py:264
  107.0 1.7 %add.3 = f32[128,512]{1,0:T(8,128)} add(f32[128,512]{1,0:T(8,128)} %get-tuple-element.7, f32[128,512]{1,0:T(8,128)S(1)} %collective-permute-done.7) | non-fusion elementwise | flops 65536 | bytes 786432 | tf_op jit(solution)/shard_map/add | solution.py:264
  (15 shorter events, 0.0 us)
Async XLA Ops:
  1.0 24.0 %copy-start = (bf16[512,128]{0,1:T(8,128)(2,1)}, bf16[512,128]{0,1:T(8,128)(2,1)S(1)}, u32[]{:S(2)}) copy-start(bf16[512,128]{0,1:T(8,128)(2,1)S(1)} %copy.5) | copy-start | bytes 393220
  1.0 6.5 %collective-permute-start.3 = (bf16[128,512]{1,0:T(8,128)(2,1)S(1)}, bf16[128,512]{1,0:T(8,128)(2,1)S(1)}, u32[]{:S(2)}, u32[]{:S(2)}) collective-permute-start(bf16[128,512]{1,0:T(8,128)(2,1)S(1)} %bitcast.1), channel_id=1, source_target_pairs={{0,4},{4,8},{8,12},{12,14},{14,10},{10,6},{6,2},{2,0},{1,5},{5,9},... | collective-permute-start | bytes 393224 | tf_op jit(solution)/shard_map/ppermute | solution.py:98
  4.1 5.2 %collective-permute-start = (bf16[128,512]{1,0:T(8,128)(2,1)S(1)}, bf16[128,512]{1,0:T(8,128)(2,1)S(1)}, u32[]{:S(2)}, u32[]{:S(2)}) collective-permute-start(bf16[128,512]{1,0:T(8,128)(2,1)S(1)} %bitcast.2), channel_id=1, source_target_pairs={{4,0},{8,4},{12,8},{14,12},{10,14},{6,10},{2,6},{0,2},{5,1},{9,5},... | collective-permute-start | bytes 393224 | tf_op jit(solution)/shard_map/ppermute | solution.py:101
  7.5 17.5 %copy-start.1 = (bf16[128,512]{1,0:T(8,128)(2,1)}, bf16[128,512]{1,0:T(8,128)(2,1)S(1)}, u32[]{:S(2)}) copy-start(bf16[128,512]{1,0:T(8,128)(2,1)S(1)} %collective-permute-done.3.refs_7_) | copy-start | bytes 393220
  7.5 5.0 %collective-permute-start.4 = (bf16[128,512]{1,0:T(8,128)(2,1)S(1)}, bf16[128,512]{1,0:T(8,128)(2,1)S(1)}, u32[]{:S(2)}, u32[]{:S(2)}) collective-permute-start(bf16[128,512]{1,0:T(8,128)(2,1)S(1)} %collective-permute-done.3.refs_7_), channel_id=1, source_target_pairs={{0,4},{4,8},{8,12},{12,14},{14,10},{10,6},{6,2},{2,0},{1,5},{5,9},... | collective-permute-start | bytes 393224 | tf_op jit(solution)/shard_map/ppermute | solution.py:98
  9.3 15.7 %copy-start.2 = (bf16[128,512]{1,0:T(8,128)(2,1)}, bf16[128,512]{1,0:T(8,128)(2,1)S(1)}, u32[]{:S(2)}) copy-start(bf16[128,512]{1,0:T(8,128)(2,1)S(1)} %collective-permute-done.refs_1_) | copy-start | bytes 393220
  9.3 5.0 %collective-permute-start.1 = (bf16[128,512]{1,0:T(8,128)(2,1)S(1)}, bf16[128,512]{1,0:T(8,128)(2,1)S(1)}, u32[]{:S(2)}, u32[]{:S(2)}) collective-permute-start(bf16[128,512]{1,0:T(8,128)(2,1)S(1)} %collective-permute-done.refs_1_), channel_id=1, source_target_pairs={{4,0},{8,4},{12,8},{14,12},{10,14},{6,10},{2,6},{0,2},{5,1},{9,5},... | collective-permute-start | bytes 393224 | tf_op jit(solution)/shard_map/ppermute | solution.py:101
  12.5 12.5 %copy-start.3 = (bf16[128,512]{1,0:T(8,128)(2,1)}, bf16[128,512]{1,0:T(8,128)(2,1)S(1)}, u32[]{:S(2)}) copy-start(bf16[128,512]{1,0:T(8,128)(2,1)S(1)} %collective-permute-done.4.refs_6_) | copy-start | bytes 393220
  12.5 5.4 %collective-permute-start.5 = (bf16[128,512]{1,0:T(8,128)(2,1)S(1)}, bf16[128,512]{1,0:T(8,128)(2,1)S(1)}, u32[]{:S(2)}, u32[]{:S(2)}) collective-permute-start(bf16[128,512]{1,0:T(8,128)(2,1)S(1)} %collective-permute-done.4.refs_6_), channel_id=1, source_target_pairs={{0,4},{4,8},{8,12},{12,14},{14,10},{10,6},{6,2},{2,0},{1,5},{5,9},... | collective-permute-start | bytes 393224 | tf_op jit(solution)/shard_map/ppermute | solution.py:98
  14.3 10.7 %copy-start.4 = (bf16[128,512]{1,0:T(8,128)(2,1)}, bf16[128,512]{1,0:T(8,128)(2,1)S(1)}, u32[]{:S(2)}) copy-start(bf16[128,512]{1,0:T(8,128)(2,1)S(1)} %collective-permute-done.1.refs_2_) | copy-start | bytes 393220
  14.3 25.7 %collective-permute-start.2 = (bf16[128,512]{1,0:T(8,128)(2,1)S(1)}, bf16[128,512]{1,0:T(8,128)(2,1)S(1)}, u32[]{:S(2)}, u32[]{:S(2)}) collective-permute-start(bf16[128,512]{1,0:T(8,128)(2,1)S(1)} %collective-permute-done.1.refs_2_), channel_id=1, source_target_pairs={{4,0},{8,4},{12,8},{14,12},{10,14},{6,10},{2,6},{0,2},{5,1},{9,5},... | collective-permute-start | bytes 393224 | tf_op jit(solution)/shard_map/ppermute | solution.py:101
  17.9 7.1 %copy-start.5 = (bf16[128,512]{1,0:T(8,128)(2,1)}, bf16[128,512]{1,0:T(8,128)(2,1)S(1)}, u32[]{:S(2)}) copy-start(bf16[128,512]{1,0:T(8,128)(2,1)S(1)} %collective-permute-done.5.refs_5_) | copy-start | bytes 393220
  17.9 22.1 %collective-permute-start.6 = (bf16[128,512]{1,0:T(8,128)(2,1)S(1)}, bf16[128,512]{1,0:T(8,128)(2,1)S(1)}, u32[]{:S(2)}, u32[]{:S(2)}) collective-permute-start(bf16[128,512]{1,0:T(8,128)(2,1)S(1)} %collective-permute-done.5.refs_5_), channel_id=1, source_target_pairs={{0,4},{4,8},{8,12},{12,14},{14,10},{10,6},{6,2},{2,0},{1,5},{5,9},... | collective-permute-start | bytes 393224 | tf_op jit(solution)/shard_map/ppermute | solution.py:98
  40.0 0.6 copy-start.6
  40.6 0.6 copy-start.7
  105.3 1.7 %collective-permute-start.7 = (f32[128,512]{1,0:T(8,128)}, f32[128,512]{1,0:T(8,128)S(1)}, u32[]{:S(2)}, u32[]{:S(2)}) collective-permute-start(f32[128,512]{1,0:T(8,128)} %get-tuple-element.8), channel_id=1, source_target_pairs={{0,1},{1,0},{2,3},{3,2},{4,5},{5,4},{6,7},{7,6},{8,9},{9,8},{10,11... | collective-permute-start | bytes 786440 | tf_op jit(solution)/shard_map/ppermute | solution.py:264

commit v3 on v2

v3 whole, which is shorter than its diff:
```python
import functools

import jax
import jax.numpy as jnp
from jax import lax
from jax.experimental import pallas as pl
from jax.experimental.pallas import tpu as pltpu
from jax.sharding import PartitionSpec as P

L = 100
LE = 104
SPAN = LE - L
EPS = 1e-06
LANES = 128
PIECES = 4
ROWS = 16
TAPS = 4
TILE = 512
GROUP = 8
VMEM = 56 * 1024 * 1024


def embed_kernel(t_ref, off_ref, mask_ref, e_ref):
    rows, cols = off_ref.shape
    for w in range(cols // LANES):
        lanes = slice(w * LANES, (w + 1) * LANES)
        total = jnp.zeros((rows, LANES), jnp.float32)
        for l in range(L):
            v = t_ref[l, :, lanes].astype(jnp.float32)
            total = total + v * v
        scale = lax.rsqrt(total / L + EPS) * mask_ref[:, lanes].astype(jnp.float32) / L
        off = off_ref[:, lanes]
        odd = ((off & 1) == 1).astype(jnp.bfloat16) > 0
        high = (off >= 2).astype(jnp.bfloat16) > 0
        full = (off == SPAN).astype(jnp.bfloat16) > 0
        zero = jnp.zeros((rows, LANES), jnp.bfloat16)
        plain = [zero] * SPAN
        moved = [zero] * 2
        for j in range(LE):
            sample = t_ref[j, :, lanes] if j < L else zero
            now = jnp.where(odd, plain[-1], sample)
            value = jnp.where(full, plain[0], jnp.where(high, moved[0], now))
            e_ref[j, :, lanes] = (value.astype(jnp.float32) * scale).astype(jnp.bfloat16)
            plain = plain[1:] + [sample]
            moved = moved[1:] + [now]


def embed(templates, offsets, masks, piece):
    k, channels = offsets.shape
    rows = k // PIECES
    steps = rows // ROWS
    first = piece * steps
    width = 2 * LANES
    return pl.pallas_call(
        embed_kernel,
        grid=(steps, channels // width),
        in_specs=[
            pl.BlockSpec((L, ROWS, width), lambda i, j: (0, first + i, j)),
            pl.BlockSpec((ROWS, width), lambda i, j: (first + i, j)),
            pl.BlockSpec((ROWS, width), lambda i, j: (first + i, j)),
        ],
        out_specs=pl.BlockSpec((LE, ROWS, width), lambda i, j: (0, i, j)),
        out_shape=jax.ShapeDtypeStruct((LE, rows, channels), jnp.bfloat16),
        compiler_params=pltpu.CompilerParams(vmem_limit_bytes=VMEM),
        cost_estimate=pl.CostEstimate(
            flops=20 * LE * rows * channels,
            bytes_accessed=2 * 2 * LE * rows * channels,
            transcendentals=0,
        ),
    )(templates, offsets, masks)


def ring_position(b, n):
    z, y = b // 2, b % 2
    return z * (1 - y) + (n - 1 - z) * y


def ring_block(p, n):
    half = n // 2
    low = (p < half) * 1 if isinstance(p, int) else (p < half).astype(jnp.int32)
    return low * (2 * p) + (1 - low) * (2 * (n - 1 - p) + 1)


def ring_gather(x, n, beside):
    order = [ring_block(p, n) for p in range(n)]
    up = [(order[p], order[(p + 1) % n]) for p in range(n)]
    down = [(order[(p + 1) % n], order[p]) for p in range(n)]
    blocks = {0: x}
    done = []
    a = b = x
    for step in range(1, n // 2 + 1):
        a = lax.ppermute(a, "blk", up)
        if step < n // 2:
            b = lax.ppermute(b, "blk", down)
        if step <= PIECES:
            done.append(beside(step - 1))
            a, b, done[-1] = lax.optimization_barrier((a, b, done[-1]))
        blocks[n - step] = a
        if step < n // 2:
            blocks[step] = b
    return [blocks[d] for d in range(n)], done


def prepare(n, block_refs, x_ref, g_ref, n_ref):
    lags, width = block_refs[0].shape
    me = ring_position(lax.axis_index("blk"), n)
    for d in range(n):
        v = ring_block(lax.rem(me + d, n), n)
        for w in range(width // LANES):
            for u in range(0, lags, 16):
                value = block_refs[d][u : u + 16, w * LANES : (w + 1) * LANES].astype(jnp.float32)
                for i in range(2):
                    x_ref[w, pl.ds((u + 8 * i) * n + v, 8, stride=n), :] = value[8 * i : 8 * i + 8]

        @pl.when(v > 0)
        def _():
            for w in range(width // LANES):
                for u in range(0, LE, 8):
                    value = x_ref[w, pl.ds(u * n + v, 8, stride=n), :]
                    x_ref[w, pl.ds((lags + u) * n + v - 1, 8, stride=n), :] = value

        @pl.when(v == 0)
        def _():
            for w in range(width // LANES):
                for u in range(0, LE, 8):
                    x_ref[w, pl.ds((lags + u) * n + n - 1, 8, stride=n), :] = jnp.zeros(
                        (8, LANES), jnp.float32
                    )

    x_ref[:, (lags + LE) * n :, :] = jnp.zeros((width // LANES, 2 * TAPS * n, LANES), jnp.float32)
    size = GROUP * n

    def energy(g, carry):
        for w in range(width // LANES):
            value = x_ref[w, pl.ds(pl.multiple_of(g * size, size), size), :].reshape(GROUP, n, LANES)
            g_ref[w, g] = jnp.sum(value * value, axis=0)
        return carry

    lax.fori_loop(0, (lags + LE) // GROUP, energy, 0)

    def norms(g, carry):
        for w in range(width // LANES):
            middle = g_ref[w, g + 1]
            for i in range(2, LE // GROUP):
                middle = middle + g_ref[w, g + i]
            left = x_ref[w, pl.ds(pl.multiple_of(g * size, size), size), :].reshape(GROUP, n, LANES)
            right = x_ref[w, pl.ds(pl.multiple_of(g * size + LE * n, size), size), :]
            right = right.reshape(GROUP, n, LANES)
            left = left * left
            right = right * right
            tails = [None] * GROUP
            tail = middle
            for r in range(GROUP - 1, -1, -1):
                tail = tail + left[r]
                tails[r] = tail
            head = None
            for r in range(GROUP):
                total = tails[r]
                if r > 0:
                    head = right[0] if r == 1 else head + right[r - 1]
                    total = total + head
                row = pl.ds(pl.multiple_of((g * GROUP + r) * n, n), n)
                n_ref[w, row, :] = lax.rsqrt(total / LE + EPS)
        return carry

    lax.fori_loop(0, lags // GROUP, norms, 0)


def build(x_ref, n_ref, w_ref, n, tap0, m):
    tiles = x_ref.shape[0]
    size = 8 * n
    for i in range(TILE // size):
        row = m * TILE + i * size
        rows = pl.ds(pl.multiple_of(row, size), size)
        for w in range(tiles):
            norm = n_ref[w, rows, :]
            xs = x_ref[w, pl.ds(pl.multiple_of(row + tap0 * n, n), (TAPS + 7) * n), :]
            for tap in range(TAPS):
                value = (xs[tap * n : tap * n + size] * norm).astype(jnp.bfloat16)
                w_ref[rows, (tap * tiles + w) * LANES : (tap * tiles + w + 1) * LANES] = value


def correlate_kernel(n, steps, *refs):
    blocks = refs[:n]
    e_refs = refs[n : n + PIECES]
    mine_ref, other_ref, acc0_ref, acc1_ref, x_ref, g_ref, n_ref, even_ref, odd_ref = refs[n + PIECES :]
    lags, width = blocks[0].shape
    tiles = n * lags // TILE
    step = pl.program_id(0)

    @pl.when(step == 0)
    def _():
        prepare(n, blocks, x_ref, g_ref, n_ref)
        acc0_ref[...] = jnp.zeros_like(acc0_ref)
        acc1_ref[...] = jnp.zeros_like(acc1_ref)

        def first(m, carry):
            build(x_ref, n_ref, even_ref, n, 0, m)
            return carry

        lax.fori_loop(0, tiles, first, 0)

    def advance(now_ref, later_ref, part, tap0):
        weights = jnp.concatenate(
            [
                jnp.concatenate([e_ref[part * TAPS + tap] for e_ref in e_refs], axis=0)
                for tap in range(TAPS)
            ],
            axis=1,
        )

        def tile(m, carry):
            rows = pl.ds(pl.multiple_of(m * TILE, TILE), TILE)
            half = TAPS * width // 2
            for acc_ref, part in ((acc0_ref, slice(0, half)), (acc1_ref, slice(half, 2 * half))):
                acc_ref[rows, :] += lax.dot_general(
                    now_ref[rows, part],
                    weights[:, part],
                    (((1,), (1,)), ((), ())),
                    preferred_element_type=jnp.float32,
                )
            build(x_ref, n_ref, later_ref, n, tap0, m)
            return carry

        lax.fori_loop(0, tiles, tile, 0)

    advance(even_ref, odd_ref, 0, step * 2 * TAPS + TAPS)
    advance(odd_ref, even_ref, 1, step * 2 * TAPS + 2 * TAPS)

    @pl.when(step == steps - 1)
    def _():
        core = lax.axis_index("chan")
        half = n // 2
        for out_ref, first in ((mine_ref, core * half), (other_ref, (1 - core) * half)):
            for v in range(half):
                rows = pl.ds(first + v, lags, stride=n)
                value = acc0_ref[rows, :] + acc1_ref[rows, :]
                out_ref[:, v * lags : (v + 1) * lags] = value.T


def correlate(blocks, pieces):
    n = len(blocks)
    lags, width = blocks[0].shape
    k = PIECES * pieces[0].shape[1]
    steps = LE // (2 * TAPS)
    whole = pl.BlockSpec(memory_space=pltpu.VMEM)
    e_spec = pl.BlockSpec((2 * TAPS, k // PIECES, width), lambda i: (i, 0, 0))
    return pl.pallas_call(
        functools.partial(correlate_kernel, n, steps),
        grid=(steps,),
        in_specs=[whole] * n + [e_spec] * PIECES,
        out_specs=[whole, whole],
        out_shape=[jax.ShapeDtypeStruct((k, n * lags // 2), jnp.float32)] * 2,
        scratch_shapes=[
            pltpu.VMEM((n * lags, k), jnp.float32),
            pltpu.VMEM((n * lags, k), jnp.float32),
            pltpu.VMEM((width // LANES, (lags + LE + 2 * TAPS) * n, LANES), jnp.float32),
            pltpu.VMEM((width // LANES, (lags + LE) // GROUP, n, LANES), jnp.float32),
            pltpu.VMEM((width // LANES, lags * n, LANES), jnp.float32),
            pltpu.VMEM((n * lags, TAPS * width), jnp.bfloat16),
            pltpu.VMEM((n * lags, TAPS * width), jnp.bfloat16),
        ],
        compiler_params=pltpu.CompilerParams(vmem_limit_bytes=VMEM),
        cost_estimate=pl.CostEstimate(
            flops=2 * n * lags * LE * width * k,
            bytes_accessed=2 * LE * width * k,
            transcendentals=0,
        ),
    )(*blocks, *pieces)


def per_device(n, records, templates, offsets, masks):
    blocks, pieces = ring_gather(
        records.T, n, lambda piece: embed(templates, offsets, masks, piece)
    )
    mine, other = correlate(blocks, pieces)
    return mine + lax.ppermute(other, "chan", [(0, 1), (1, 0)])


def solution(mesh):
    return jax.shard_map(
        functools.partial(per_device, mesh.shape["blk"]),
        mesh=mesh,
        in_specs=(
            P("chan", ("groups", "blk")),
            P(None, ("groups", "blk"), "chan"),
            P(("groups", "blk"), "chan"),
            P(("groups", "blk"), "chan"),
        ),
        out_specs=P(("groups", "blk"), "chan"),
        check_vma=False,
    )
```

time: 109 us -> 99 us (0.908)
  waiting for transfers between devices: 11.5 us -> 1.76 us
    ppermute x4, waiting for transfers between devices: 9.73 us -> 0.01 us  [ring_gather(): a = lax.ppermute(a, 'blk', up)]
    ppermute x3, starting transfers between devices: 0.47 us -> 6.93 us  [ring_gather(): b = lax.ppermute(b, 'blk', down)]
    ppermute x4, starting transfers between devices: 8.76 us -> 2.38 us  [ring_gather(): a = lax.ppermute(a, 'blk', up)]
    pallas_call x4, Pallas kernels: 19.9 us -> 21.3 us  [embed(): pl.pallas_call(embed_kernel, grid=(steps, channels // width), in_specs=[p...]
    pallas_call x1, Pallas kernels: 64 us -> 62.6 us  [correlate(): pl.pallas_call(functools.partial(correlate_kernel, n, steps), grid=(steps...]
  transfers between devices with their start and end apart: 8 -> 8, of which waited for: 4 -> 1; matrix products, arithmetic and copies ran while one was open for 0% -> 0% of each run, Pallas kernels for 18% -> 22%
where the time goes in v3:
time: 99 us; the launch traced here: 98.5 us
  Pallas kernels  84 us (85%)
  starting transfers between devices  9.31 us (9%)
  waiting for transfers between devices  1.76 us (2%)
  other arithmetic  1.7 us (2%)
  local copies, waits for them, and re-layouts  1.68 us (2%)
    pallas_call x1, Pallas kernels, correlate(): pl.pallas_call(functools.partial(correlate_kernel, n, steps), grid=(steps...  62.6 us
    pallas_call x4, Pallas kernels, embed(): pl.pallas_call(embed_kernel, grid=(steps, channels // width), in_specs=[p...  21.3 us
    ppermute x3, starting transfers between devices, ring_gather(): b = lax.ppermute(b, 'blk', down)  6.93 us
    ppermute x4, starting transfers between devices, ring_gather(): a = lax.ppermute(a, 'blk', up)  2.38 us
  transfers between devices with their start and end apart: 8, of which 1 were waited for; matrix products, arithmetic and copies ran while one was open for 0% of the time, Pallas kernels for 22%

profile of v3, /device:TPU:0, one launch (start us, length us, event | category | flops | bytes accessed | tf_op | source)
XLA Modules:
  0.0 98.5 jit_solution(11107212338702061356)
XLA Ops:
  0.0 1.0 %copy.5 = bf16[512,128]{0,1:T(8,128)(2,1)S(1)} copy(bf16[512,128]{1,0:T(8,128)(2,1)} %param.4) | data formatting | bytes 262144 | tf_op args[0]
  1.0 3.0 %collective-permute-start.1 = (bf16[128,512]{1,0:T(8,128)(2,1)S(1)}, bf16[128,512]{1,0:T(8,128)(2,1)S(1)}, u32[]{:S(2)}, u32[]{:S(2)}) collective-permute-start(bf16[128,512]{1,0:T(8,128)(2,1)S(1)} %bitcast.1), channel_id=1, source_target_pairs={{4,0},{8,4},{12,8},{14,12},{10,14},{6,10},{2,6},{0,2},{5,1},{9,5},... | collective-permute-start | bytes 393224 | tf_op jit(solution)/shard_map/ppermute | solution.py:94
  4.0 0.1 collective-permute-start
  4.2 5.3 %shard_map.46.refs_8_ = bf16[104,32,512]{2,1,0:T(8,128)(2,1)} custom-call(bf16[100,128,512]{2,1,0:T(8,128)(2,1)} %t_ref.7, s32[128,512]{1,0:T(8,128)} %off_ref.7, s32[128,512]{1,0:T(8,128)} %mask_ref.7), custom_call_target="tpu_custom_call" | custom-call | flops 34078720 | bytes 6815744 | tf_op jit(solution)/shard_map/pallas_call | solution.py:54
  9.5 0.0 collective-permute-done.1.refs_1_
  9.5 0.0 collective-permute-done.refs_7_
  9.5 2.0 %collective-permute-start.3 = (bf16[128,512]{1,0:T(8,128)(2,1)S(1)}, bf16[128,512]{1,0:T(8,128)(2,1)S(1)}, u32[]{:S(2)}, u32[]{:S(2)}) collective-permute-start(bf16[128,512]{1,0:T(8,128)(2,1)S(1)} %collective-permute-done.1.refs_1_), channel_id=1, source_target_pairs={{4,0},{8,4},{12,8},{14,12},{10,14},{6,10},{2,6},{0,2},{5,1},{9,5},... | collective-permute-start | bytes 393224 | tf_op jit(solution)/shard_map/ppermute | solution.py:94
  11.5 0.1 collective-permute-start.2
  11.6 5.4 %shard_map.47.refs_9_ = bf16[104,32,512]{2,1,0:T(8,128)(2,1)} custom-call(bf16[100,128,512]{2,1,0:T(8,128)(2,1)} %t_ref.7, s32[128,512]{1,0:T(8,128)} %off_ref.7, s32[128,512]{1,0:T(8,128)} %mask_ref.7), custom_call_target="tpu_custom_call" | custom-call | flops 34078720 | bytes 6815744 | tf_op jit(solution)/shard_map/pallas_call | solution.py:54
  16.9 0.0 collective-permute-done.3.refs_2_
  17.0 0.0 collective-permute-done.2.refs_6_
  17.0 2.0 %collective-permute-start.5 = (bf16[128,512]{1,0:T(8,128)(2,1)S(1)}, bf16[128,512]{1,0:T(8,128)(2,1)S(1)}, u32[]{:S(2)}, u32[]{:S(2)}) collective-permute-start(bf16[128,512]{1,0:T(8,128)(2,1)S(1)} %collective-permute-done.3.refs_2_), channel_id=1, source_target_pairs={{4,0},{8,4},{12,8},{14,12},{10,14},{6,10},{2,6},{0,2},{5,1},{9,5},... | collective-permute-start | bytes 393224 | tf_op jit(solution)/shard_map/ppermute | solution.py:94
  18.9 0.1 collective-permute-start.4
  19.1 5.4 %shard_map.48.refs_10_ = bf16[104,32,512]{2,1,0:T(8,128)(2,1)} custom-call(bf16[100,128,512]{2,1,0:T(8,128)(2,1)} %t_ref.7, s32[128,512]{1,0:T(8,128)} %off_ref.7, s32[128,512]{1,0:T(8,128)} %mask_ref.7), custom_call_target="tpu_custom_call" | custom-call | flops 34078720 | bytes 6815744 | tf_op jit(solution)/shard_map/pallas_call | solution.py:54
  24.4 0.0 collective-permute-done.5.refs_3_
  24.5 0.0 collective-permute-done.4.refs_5_
  24.5 2.0 %collective-permute-start.6 = (bf16[128,512]{1,0:T(8,128)(2,1)S(1)}, bf16[128,512]{1,0:T(8,128)(2,1)S(1)}, u32[]{:S(2)}, u32[]{:S(2)}) collective-permute-start(bf16[128,512]{1,0:T(8,128)(2,1)S(1)} %collective-permute-done.4.refs_5_), channel_id=1, source_target_pairs={{0,4},{4,8},{8,12},{12,14},{14,10},{10,6},{6,2},{2,0},{1,5},{5,9},... | collective-permute-start | bytes 393224 | tf_op jit(solution)/shard_map/ppermute | solution.py:92
  26.5 5.3 %shard_map.49.refs_11_ = bf16[104,32,512]{2,1,0:T(8,128)(2,1)} custom-call(bf16[100,128,512]{2,1,0:T(8,128)(2,1)} %t_ref.7, s32[128,512]{1,0:T(8,128)} %off_ref.7, s32[128,512]{1,0:T(8,128)} %mask_ref.7), custom_call_target="tpu_custom_call" | custom-call | flops 34078720 | bytes 6815744 | tf_op jit(solution)/shard_map/pallas_call | solution.py:54
  31.8 0.0 collective-permute-done.6.refs_4_
  31.8 0.6 copy-done.7
  32.5 62.6 %shard_map.50 = (f32[128,512]{1,0:T(8,128)}, f32[128,512]{1,0:T(8,128)}) custom-call(bf16[128,512]{1,0:T(8,128)(2,1)} %bitcast.3, bf16[128,512]{1,0:T(8,128)(2,1)} %copy-done.1, bf16[128,512]{1,0:T(8,128)(2,1)} %copy-done.3, bf16[128,512]{1,0:T(8,128)(2,1)} %copy-done.5, bf16[128,512]{1,0:T(8,128)(2,1)} %copy-done.7, bf16[128,512]{1,0:T(8,128)(2,1)} %copy-done.6, ...), custom_call_target="tpu_custom_call" | custom-call | flops 13958643712 | bytes 13631488 | tf_op jit(solution)/shard_map/pallas_call | solution.py:248
  95.1 0.0 collective-permute-start.7
  95.1 1.7 %collective-permute-done.7 = f32[128,512]{1,0:T(8,128)S(1)} collective-permute-done((f32[128,512]{1,0:T(8,128)}, f32[128,512]{1,0:T(8,128)S(1)}, u32[]{:S(2)}, u32[]{:S(2)}) %collective-permute-start.7) | collective-permute-done | bytes 262176 | tf_op jit(solution)/shard_map/ppermute | solution.py:277
  96.8 1.7 %add.3 = f32[128,512]{1,0:T(8,128)} add(f32[128,512]{1,0:T(8,128)} %get-tuple-element.29, f32[128,512]{1,0:T(8,128)S(1)} %collective-permute-done.7) | non-fusion elementwise | flops 65536 | bytes 786432 | tf_op jit(solution)/shard_map/add | solution.py:277
  (15 shorter events, 0.0 us)
Async XLA Ops:
  1.0 8.5 %copy-start = (bf16[512,128]{0,1:T(8,128)(2,1)}, bf16[512,128]{0,1:T(8,128)(2,1)S(1)}, u32[]{:S(2)}) copy-start(bf16[512,128]{0,1:T(8,128)(2,1)S(1)} %copy.5) | copy-start | bytes 393220
  1.0 8.4 %collective-permute-start.1 = (bf16[128,512]{1,0:T(8,128)(2,1)S(1)}, bf16[128,512]{1,0:T(8,128)(2,1)S(1)}, u32[]{:S(2)}, u32[]{:S(2)}) collective-permute-start(bf16[128,512]{1,0:T(8,128)(2,1)S(1)} %bitcast.1), channel_id=1, source_target_pairs={{4,0},{8,4},{12,8},{14,12},{10,14},{6,10},{2,6},{0,2},{5,1},{9,5},... | collective-permute-start | bytes 393224 | tf_op jit(solution)/shard_map/ppermute | solution.py:94
  4.0 5.4 %collective-permute-start = (bf16[128,512]{1,0:T(8,128)(2,1)S(1)}, bf16[128,512]{1,0:T(8,128)(2,1)S(1)}, u32[]{:S(2)}, u32[]{:S(2)}) collective-permute-start(bf16[128,512]{1,0:T(8,128)(2,1)S(1)} %bitcast.2), channel_id=1, source_target_pairs={{0,4},{4,8},{8,12},{12,14},{14,10},{10,6},{6,2},{2,0},{1,5},{5,9},... | collective-permute-start | bytes 393224 | tf_op jit(solution)/shard_map/ppermute | solution.py:92
  9.5 7.5 %copy-start.1 = (bf16[128,512]{1,0:T(8,128)(2,1)}, bf16[128,512]{1,0:T(8,128)(2,1)S(1)}, u32[]{:S(2)}) copy-start(bf16[128,512]{1,0:T(8,128)(2,1)S(1)} %collective-permute-done.1.refs_1_) | copy-start | bytes 393220
  9.5 7.5 %copy-start.2 = (bf16[128,512]{1,0:T(8,128)(2,1)}, bf16[128,512]{1,0:T(8,128)(2,1)S(1)}, u32[]{:S(2)}) copy-start(bf16[128,512]{1,0:T(8,128)(2,1)S(1)} %collective-permute-done.refs_7_) | copy-start | bytes 393220
  9.5 7.5 %collective-permute-start.3 = (bf16[128,512]{1,0:T(8,128)(2,1)S(1)}, bf16[128,512]{1,0:T(8,128)(2,1)S(1)}, u32[]{:S(2)}, u32[]{:S(2)}) collective-permute-start(bf16[128,512]{1,0:T(8,128)(2,1)S(1)} %collective-permute-done.1.refs_1_), channel_id=1, source_target_pairs={{4,0},{8,4},{12,8},{14,12},{10,14},{6,10},{2,6},{0,2},{5,1},{9,5},... | collective-permute-start | bytes 393224 | tf_op jit(solution)/shard_map/ppermute | solution.py:94
  11.5 5.5 %collective-permute-start.2 = (bf16[128,512]{1,0:T(8,128)(2,1)S(1)}, bf16[128,512]{1,0:T(8,128)(2,1)S(1)}, u32[]{:S(2)}, u32[]{:S(2)}) collective-permute-start(bf16[128,512]{1,0:T(8,128)(2,1)S(1)} %collective-permute-done.refs_7_), channel_id=1, source_target_pairs={{0,4},{4,8},{8,12},{12,14},{14,10},{10,6},{6,2},{2,0},{1,5},{5,9},... | collective-permute-start | bytes 393224 | tf_op jit(solution)/shard_map/ppermute | solution.py:92
  17.0 7.5 %copy-start.3 = (bf16[128,512]{1,0:T(8,128)(2,1)}, bf16[128,512]{1,0:T(8,128)(2,1)S(1)}, u32[]{:S(2)}) copy-start(bf16[128,512]{1,0:T(8,128)(2,1)S(1)} %collective-permute-done.3.refs_2_) | copy-start | bytes 393220
  17.0 7.5 %copy-start.4 = (bf16[128,512]{1,0:T(8,128)(2,1)}, bf16[128,512]{1,0:T(8,128)(2,1)S(1)}, u32[]{:S(2)}) copy-start(bf16[128,512]{1,0:T(8,128)(2,1)S(1)} %collective-permute-done.2.refs_6_) | copy-start | bytes 393220
  17.0 7.5 %collective-permute-start.5 = (bf16[128,512]{1,0:T(8,128)(2,1)S(1)}, bf16[128,512]{1,0:T(8,128)(2,1)S(1)}, u32[]{:S(2)}, u32[]{:S(2)}) collective-permute-start(bf16[128,512]{1,0:T(8,128)(2,1)S(1)} %collective-permute-done.3.refs_2_), channel_id=1, source_target_pairs={{4,0},{8,4},{12,8},{14,12},{10,14},{6,10},{2,6},{0,2},{5,1},{9,5},... | collective-permute-start | bytes 393224 | tf_op jit(solution)/shard_map/ppermute | solution.py:94
  18.9 5.5 %collective-permute-start.4 = (bf16[128,512]{1,0:T(8,128)(2,1)S(1)}, bf16[128,512]{1,0:T(8,128)(2,1)S(1)}, u32[]{:S(2)}, u32[]{:S(2)}) collective-permute-start(bf16[128,512]{1,0:T(8,128)(2,1)S(1)} %collective-permute-done.2.refs_6_), channel_id=1, source_target_pairs={{0,4},{4,8},{8,12},{12,14},{14,10},{10,6},{6,2},{2,0},{1,5},{5,9},... | collective-permute-start | bytes 393224 | tf_op jit(solution)/shard_map/ppermute | solution.py:92
  24.4 7.4 %copy-start.5 = (bf16[128,512]{1,0:T(8,128)(2,1)}, bf16[128,512]{1,0:T(8,128)(2,1)S(1)}, u32[]{:S(2)}) copy-start(bf16[128,512]{1,0:T(8,128)(2,1)S(1)} %collective-permute-done.5.refs_3_) | copy-start | bytes 393220
  24.5 7.3 %copy-start.6 = (bf16[128,512]{1,0:T(8,128)(2,1)}, bf16[128,512]{1,0:T(8,128)(2,1)S(1)}, u32[]{:S(2)}) copy-start(bf16[128,512]{1,0:T(8,128)(2,1)S(1)} %collective-permute-done.4.refs_5_) | copy-start | bytes 393220
  24.5 7.3 %collective-permute-start.6 = (bf16[128,512]{1,0:T(8,128)(2,1)S(1)}, bf16[128,512]{1,0:T(8,128)(2,1)S(1)}, u32[]{:S(2)}, u32[]{:S(2)}) collective-permute-start(bf16[128,512]{1,0:T(8,128)(2,1)S(1)} %collective-permute-done.4.refs_5_), channel_id=1, source_target_pairs={{0,4},{4,8},{8,12},{12,14},{14,10},{10,6},{6,2},{2,0},{1,5},{5,9},... | collective-permute-start | bytes 393224 | tf_op jit(solution)/shard_map/ppermute | solution.py:92
  31.8 0.6 copy-start.7
  95.1 1.7 %collective-permute-start.7 = (f32[128,512]{1,0:T(8,128)}, f32[128,512]{1,0:T(8,128)S(1)}, u32[]{:S(2)}, u32[]{:S(2)}) collective-permute-start(f32[128,512]{1,0:T(8,128)} %get-tuple-element.30), channel_id=1, source_target_pairs={{0,1},{1,0},{2,3},{3,2},{4,5},{5,4},{6,7},{7,6},{8,9},{9,8},{10,11... | collective-permute-start | bytes 786440 | tf_op jit(solution)/shard_map/ppermute | solution.py:277

commit v4 on v3

--- a/solution.py
+++ b/solution.py
@@ -183,7 +183,7 @@
 def correlate_kernel(n, steps, *refs):
     blocks = refs[:n]
     e_refs = refs[n : n + PIECES]
-    mine_ref, other_ref, acc0_ref, acc1_ref, x_ref, g_ref, n_ref, even_ref, odd_ref = refs[n + PIECES :]
+    mine_ref, other_ref, acc_ref, turned_ref, x_ref, g_ref, n_ref, even_ref, odd_ref = refs[n + PIECES :]
     lags, width = blocks[0].shape
     tiles = n * lags // TILE
     step = pl.program_id(0)
@@ -191,8 +191,7 @@
     @pl.when(step == 0)
     def _():
         prepare(n, blocks, x_ref, g_ref, n_ref)
-        acc0_ref[...] = jnp.zeros_like(acc0_ref)
-        acc1_ref[...] = jnp.zeros_like(acc1_ref)
+        acc_ref[...] = jnp.zeros_like(acc_ref)
 
         def first(m, carry):
             build(x_ref, n_ref, even_ref, n, 0, m)
@@ -211,14 +210,12 @@
 
         def tile(m, carry):
             rows = pl.ds(pl.multiple_of(m * TILE, TILE), TILE)
-            half = TAPS * width // 2
-            for acc_ref, part in ((acc0_ref, slice(0, half)), (acc1_ref, slice(half, 2 * half))):
-                acc_ref[rows, :] += lax.dot_general(
-                    now_ref[rows, part],
-                    weights[:, part],
-                    (((1,), (1,)), ((), ())),
-                    preferred_element_type=jnp.float32,
-                )
+            acc_ref[:, rows] += lax.dot_general(
+                weights,
+                now_ref[rows, :],
+                (((1,), (1,)), ((), ())),
+                preferred_element_type=jnp.float32,
+            )
             build(x_ref, n_ref, later_ref, n, tap0, m)
             return carry
 
@@ -229,12 +226,13 @@
 
     @pl.when(step == steps - 1)
     def _():
+        for u in range(0, n * lags, LANES):
+            turned_ref[u : u + LANES, :] = acc_ref[:, u : u + LANES].T
         core = lax.axis_index("chan")
         half = n // 2
         for out_ref, first in ((mine_ref, core * half), (other_ref, (1 - core) * half)):
             for v in range(half):
-                rows = pl.ds(first + v, lags, stride=n)
-                value = acc0_ref[rows, :] + acc1_ref[rows, :]
+                value = turned_ref[pl.ds(first + v, lags, stride=n), :]
                 out_ref[:, v * lags : (v + 1) * lags] = value.T
 
 
@@ -252,7 +250,7 @@
         out_specs=[whole, whole],
         out_shape=[jax.ShapeDtypeStruct((k, n * lags // 2), jnp.float32)] * 2,
         scratch_shapes=[
-            pltpu.VMEM((n * lags, k), jnp.float32),
+            pltpu.VMEM((k, n * lags), jnp.float32),
             pltpu.VMEM((n * lags, k), jnp.float32),
             pltpu.VMEM((width // LANES, (lags + LE + 2 * TAPS) * n, LANES), jnp.float32),
             pltpu.VMEM((width // LANES, (lags + LE) // GROUP, n, LANES), jnp.float32),

time: 99 us -> 106 us (1.071)
  Pallas kernels: 84 us -> 90.9 us
    pallas_call x1, Pallas kernels: 62.6 us -> 69.5 us  [correlate(): pl.pallas_call(functools.partial(correlate_kernel, n, steps), grid=(steps...]
  transfers between devices with their start and end apart: 8 -> 8, of which waited for: 1 -> 1; matrix products, arithmetic and copies ran while one was open for 0% -> 0% of each run, Pallas kernels for 22% -> 20%
where the time goes in v4:
time: 106 us; the launch traced here: 105 us
  Pallas kernels  90.9 us (86%)
  starting transfers between devices  9.31 us (9%)
  waiting for transfers between devices  1.76 us (2%)
  other arithmetic  1.7 us (2%)
  local copies, waits for them, and re-layouts  1.68 us (2%)
    pallas_call x1, Pallas kernels, correlate(): pl.pallas_call(functools.partial(correlate_kernel, n, steps), grid=(steps...  69.5 us
    pallas_call x4, Pallas kernels, embed(): pl.pallas_call(embed_kernel, grid=(steps, channels // width), in_specs=[p...  21.3 us
    ppermute x3, starting transfers between devices, ring_gather(): b = lax.ppermute(b, 'blk', down)  6.93 us
    ppermute x4, starting transfers between devices, ring_gather(): a = lax.ppermute(a, 'blk', up)  2.38 us
  transfers between devices with their start and end apart: 8, of which 1 were waited for; matrix products, arithmetic and copies ran while one was open for 0% of the time, Pallas kernels for 20%

profile of v4, /device:TPU:0, one launch (start us, length us, event | category | flops | bytes accessed | tf_op | source)
XLA Modules:
  0.0 105.4 jit_solution(12708436499996972067)
XLA Ops:
  0.0 1.0 copy.5
  1.0 3.0 %collective-permute-start.1 = (bf16[128,512]{1,0:T(8,128)(2,1)S(1)}, bf16[128,512]{1,0:T(8,128)(2,1)S(1)}, u32[]{:S(2)}, u32[]{:S(2)}) collective-permute-start(bf16[128,512]{1,0:T(8,128)(2,1)S(1)} %bitcast.1), channel_id=1, source_target_pairs={{4,0},{8,4},{12,8},{14,12},{10,14},{6,10},{2,6},{0,2},{5,1},{9,5},... | collective-permute-start | bytes 393224 | tf_op jit(solution)/shard_map/ppermute | solution.py:94
  4.0 0.1 collective-permute-start
  4.2 5.3 %shard_map.46.refs_8_ = bf16[104,32,512]{2,1,0:T(8,128)(2,1)} custom-call(bf16[100,128,512]{2,1,0:T(8,128)(2,1)} %t_ref.7, s32[128,512]{1,0:T(8,128)} %off_ref.7, s32[128,512]{1,0:T(8,128)} %mask_ref.7), custom_call_target="tpu_custom_call" | custom-call | flops 34078720 | bytes 6815744 | tf_op jit(solution)/shard_map/pallas_call | solution.py:54
  9.5 0.0 collective-permute-done.1.refs_1_
  9.5 0.0 collective-permute-done.refs_7_
  9.5 2.0 %collective-permute-start.3 = (bf16[128,512]{1,0:T(8,128)(2,1)S(1)}, bf16[128,512]{1,0:T(8,128)(2,1)S(1)}, u32[]{:S(2)}, u32[]{:S(2)}) collective-permute-start(bf16[128,512]{1,0:T(8,128)(2,1)S(1)} %collective-permute-done.1.refs_1_), channel_id=1, source_target_pairs={{4,0},{8,4},{12,8},{14,12},{10,14},{6,10},{2,6},{0,2},{5,1},{9,5},... | collective-permute-start | bytes 393224 | tf_op jit(solution)/shard_map/ppermute | solution.py:94
  11.5 0.1 collective-permute-start.2
  11.6 5.4 %shard_map.47.refs_9_ = bf16[104,32,512]{2,1,0:T(8,128)(2,1)} custom-call(bf16[100,128,512]{2,1,0:T(8,128)(2,1)} %t_ref.7, s32[128,512]{1,0:T(8,128)} %off_ref.7, s32[128,512]{1,0:T(8,128)} %mask_ref.7), custom_call_target="tpu_custom_call" | custom-call | flops 34078720 | bytes 6815744 | tf_op jit(solution)/shard_map/pallas_call | solution.py:54
  16.9 0.0 collective-permute-done.3.refs_2_
  17.0 0.0 collective-permute-done.2.refs_6_
  17.0 2.0 %collective-permute-start.5 = (bf16[128,512]{1,0:T(8,128)(2,1)S(1)}, bf16[128,512]{1,0:T(8,128)(2,1)S(1)}, u32[]{:S(2)}, u32[]{:S(2)}) collective-permute-start(bf16[128,512]{1,0:T(8,128)(2,1)S(1)} %collective-permute-done.3.refs_2_), channel_id=1, source_target_pairs={{4,0},{8,4},{12,8},{14,12},{10,14},{6,10},{2,6},{0,2},{5,1},{9,5},... | collective-permute-start | bytes 393224 | tf_op jit(solution)/shard_map/ppermute | solution.py:94
  18.9 0.1 collective-permute-start.4
  19.1 5.4 %shard_map.48.refs_10_ = bf16[104,32,512]{2,1,0:T(8,128)(2,1)} custom-call(bf16[100,128,512]{2,1,0:T(8,128)(2,1)} %t_ref.7, s32[128,512]{1,0:T(8,128)} %off_ref.7, s32[128,512]{1,0:T(8,128)} %mask_ref.7), custom_call_target="tpu_custom_call" | custom-call | flops 34078720 | bytes 6815744 | tf_op jit(solution)/shard_map/pallas_call | solution.py:54
  24.4 0.0 collective-permute-done.5.refs_3_
  24.5 0.0 collective-permute-done.4.refs_5_
  24.5 2.0 %collective-permute-start.6 = (bf16[128,512]{1,0:T(8,128)(2,1)S(1)}, bf16[128,512]{1,0:T(8,128)(2,1)S(1)}, u32[]{:S(2)}, u32[]{:S(2)}) collective-permute-start(bf16[128,512]{1,0:T(8,128)(2,1)S(1)} %collective-permute-done.4.refs_5_), channel_id=1, source_target_pairs={{0,4},{4,8},{8,12},{12,14},{14,10},{10,6},{6,2},{2,0},{1,5},{5,9},... | collective-permute-start | bytes 393224 | tf_op jit(solution)/shard_map/ppermute | solution.py:92
  26.5 5.3 %shard_map.49.refs_11_ = bf16[104,32,512]{2,1,0:T(8,128)(2,1)} custom-call(bf16[100,128,512]{2,1,0:T(8,128)(2,1)} %t_ref.7, s32[128,512]{1,0:T(8,128)} %off_ref.7, s32[128,512]{1,0:T(8,128)} %mask_ref.7), custom_call_target="tpu_custom_call" | custom-call | flops 34078720 | bytes 6815744 | tf_op jit(solution)/shard_map/pallas_call | solution.py:54
  31.8 0.0 collective-permute-done.6.refs_4_
  31.8 0.6 copy-done.7
  32.5 69.5 %shard_map.50 = (f32[128,512]{1,0:T(8,128)}, f32[128,512]{1,0:T(8,128)}) custom-call(bf16[128,512]{1,0:T(8,128)(2,1)} %bitcast.3, bf16[128,512]{1,0:T(8,128)(2,1)} %copy-done.1, bf16[128,512]{1,0:T(8,128)(2,1)} %copy-done.3, bf16[128,512]{1,0:T(8,128)(2,1)} %copy-done.5, bf16[128,512]{1,0:T(8,128)(2,1)} %copy-done.7, bf16[128,512]{1,0:T(8,128)(2,1)} %copy-done.6, ...), custom_call_target="tpu_custom_call" | custom-call | flops 13958643712 | bytes 13631488 | tf_op jit(solution)/shard_map/pallas_call | solution.py:246
  102.0 0.0 collective-permute-start.7
  102.0 1.7 %collective-permute-done.7 = f32[128,512]{1,0:T(8,128)S(1)} collective-permute-done((f32[128,512]{1,0:T(8,128)}, f32[128,512]{1,0:T(8,128)S(1)}, u32[]{:S(2)}, u32[]{:S(2)}) %collective-permute-start.7) | collective-permute-done | bytes 262176 | tf_op jit(solution)/shard_map/ppermute | solution.py:275
  103.7 1.7 %add.3 = f32[128,512]{1,0:T(8,128)} add(f32[128,512]{1,0:T(8,128)} %get-tuple-element.29, f32[128,512]{1,0:T(8,128)S(1)} %collective-permute-done.7) | non-fusion elementwise | flops 65536 | bytes 786432 | tf_op jit(solution)/shard_map/add | solution.py:275
  (15 shorter events, 0.0 us)
Async XLA Ops:
  1.0 8.5 %copy-start = (bf16[512,128]{0,1:T(8,128)(2,1)}, bf16[512,128]{0,1:T(8,128)(2,1)S(1)}, u32[]{:S(2)}) copy-start(bf16[512,128]{0,1:T(8,128)(2,1)S(1)} %copy.5) | copy-start | bytes 393220
  1.0 8.4 %collective-permute-start.1 = (bf16[128,512]{1,0:T(8,128)(2,1)S(1)}, bf16[128,512]{1,0:T(8,128)(2,1)S(1)}, u32[]{:S(2)}, u32[]{:S(2)}) collective-permute-start(bf16[128,512]{1,0:T(8,128)(2,1)S(1)} %bitcast.1), channel_id=1, source_target_pairs={{4,0},{8,4},{12,8},{14,12},{10,14},{6,10},{2,6},{0,2},{5,1},{9,5},... | collective-permute-start | bytes 393224 | tf_op jit(solution)/shard_map/ppermute | solution.py:94
  4.0 5.4 %collective-permute-start = (bf16[128,512]{1,0:T(8,128)(2,1)S(1)}, bf16[128,512]{1,0:T(8,128)(2,1)S(1)}, u32[]{:S(2)}, u32[]{:S(2)}) collective-permute-start(bf16[128,512]{1,0:T(8,128)(2,1)S(1)} %bitcast.2), channel_id=1, source_target_pairs={{0,4},{4,8},{8,12},{12,14},{14,10},{10,6},{6,2},{2,0},{1,5},{5,9},... | collective-permute-start | bytes 393224 | tf_op jit(solution)/shard_map/ppermute | solution.py:92
  9.5 7.5 %copy-start.1 = (bf16[128,512]{1,0:T(8,128)(2,1)}, bf16[128,512]{1,0:T(8,128)(2,1)S(1)}, u32[]{:S(2)}) copy-start(bf16[128,512]{1,0:T(8,128)(2,1)S(1)} %collective-permute-done.1.refs_1_) | copy-start | bytes 393220
  9.5 7.5 %copy-start.2 = (bf16[128,512]{1,0:T(8,128)(2,1)}, bf16[128,512]{1,0:T(8,128)(2,1)S(1)}, u32[]{:S(2)}) copy-start(bf16[128,512]{1,0:T(8,128)(2,1)S(1)} %collective-permute-done.refs_7_) | copy-start | bytes 393220
  9.5 7.5 %collective-permute-start.3 = (bf16[128,512]{1,0:T(8,128)(2,1)S(1)}, bf16[128,512]{1,0:T(8,128)(2,1)S(1)}, u32[]{:S(2)}, u32[]{:S(2)}) collective-permute-start(bf16[128,512]{1,0:T(8,128)(2,1)S(1)} %collective-permute-done.1.refs_1_), channel_id=1, source_target_pairs={{4,0},{8,4},{12,8},{14,12},{10,14},{6,10},{2,6},{0,2},{5,1},{9,5},... | collective-permute-start | bytes 393224 | tf_op jit(solution)/shard_map/ppermute | solution.py:94
  11.5 5.5 %collective-permute-start.2 = (bf16[128,512]{1,0:T(8,128)(2,1)S(1)}, bf16[128,512]{1,0:T(8,128)(2,1)S(1)}, u32[]{:S(2)}, u32[]{:S(2)}) collective-permute-start(bf16[128,512]{1,0:T(8,128)(2,1)S(1)} %collective-permute-done.refs_7_), channel_id=1, source_target_pairs={{0,4},{4,8},{8,12},{12,14},{14,10},{10,6},{6,2},{2,0},{1,5},{5,9},... | collective-permute-start | bytes 393224 | tf_op jit(solution)/shard_map/ppermute | solution.py:92
  17.0 7.5 %copy-start.3 = (bf16[128,512]{1,0:T(8,128)(2,1)}, bf16[128,512]{1,0:T(8,128)(2,1)S(1)}, u32[]{:S(2)}) copy-start(bf16[128,512]{1,0:T(8,128)(2,1)S(1)} %collective-permute-done.3.refs_2_) | copy-start | bytes 393220
  17.0 7.5 %copy-start.4 = (bf16[128,512]{1,0:T(8,128)(2,1)}, bf16[128,512]{1,0:T(8,128)(2,1)S(1)}, u32[]{:S(2)}) copy-start(bf16[128,512]{1,0:T(8,128)(2,1)S(1)} %collective-permute-done.2.refs_6_) | copy-start | bytes 393220
  17.0 7.5 %collective-permute-start.5 = (bf16[128,512]{1,0:T(8,128)(2,1)S(1)}, bf16[128,512]{1,0:T(8,128)(2,1)S(1)}, u32[]{:S(2)}, u32[]{:S(2)}) collective-permute-start(bf16[128,512]{1,0:T(8,128)(2,1)S(1)} %collective-permute-done.3.refs_2_), channel_id=1, source_target_pairs={{4,0},{8,4},{12,8},{14,12},{10,14},{6,10},{2,6},{0,2},{5,1},{9,5},... | collective-permute-start | bytes 393224 | tf_op jit(solution)/shard_map/ppermute | solution.py:94
  18.9 5.5 %collective-permute-start.4 = (bf16[128,512]{1,0:T(8,128)(2,1)S(1)}, bf16[128,512]{1,0:T(8,128)(2,1)S(1)}, u32[]{:S(2)}, u32[]{:S(2)}) collective-permute-start(bf16[128,512]{1,0:T(8,128)(2,1)S(1)} %collective-permute-done.2.refs_6_), channel_id=1, source_target_pairs={{0,4},{4,8},{8,12},{12,14},{14,10},{10,6},{6,2},{2,0},{1,5},{5,9},... | collective-permute-start | bytes 393224 | tf_op jit(solution)/shard_map/ppermute | solution.py:92
  24.4 7.4 %copy-start.5 = (bf16[128,512]{1,0:T(8,128)(2,1)}, bf16[128,512]{1,0:T(8,128)(2,1)S(1)}, u32[]{:S(2)}) copy-start(bf16[128,512]{1,0:T(8,128)(2,1)S(1)} %collective-permute-done.5.refs_3_) | copy-start | bytes 393220
  24.5 7.3 %copy-start.6 = (bf16[128,512]{1,0:T(8,128)(2,1)}, bf16[128,512]{1,0:T(8,128)(2,1)S(1)}, u32[]{:S(2)}) copy-start(bf16[128,512]{1,0:T(8,128)(2,1)S(1)} %collective-permute-done.4.refs_5_) | copy-start | bytes 393220
  24.5 7.3 %collective-permute-start.6 = (bf16[128,512]{1,0:T(8,128)(2,1)S(1)}, bf16[128,512]{1,0:T(8,128)(2,1)S(1)}, u32[]{:S(2)}, u32[]{:S(2)}) collective-permute-start(bf16[128,512]{1,0:T(8,128)(2,1)S(1)} %collective-permute-done.4.refs_5_), channel_id=1, source_target_pairs={{0,4},{4,8},{8,12},{12,14},{14,10},{10,6},{6,2},{2,0},{1,5},{5,9},... | collective-permute-start | bytes 393224 | tf_op jit(solution)/shard_map/ppermute | solution.py:92
  31.8 0.6 copy-start.7
  102.0 1.7 %collective-permute-start.7 = (f32[128,512]{1,0:T(8,128)}, f32[128,512]{1,0:T(8,128)S(1)}, u32[]{:S(2)}, u32[]{:S(2)}) collective-permute-start(f32[128,512]{1,0:T(8,128)} %get-tuple-element.30), channel_id=1, source_target_pairs={{0,1},{1,0},{2,3},{3,2},{4,5},{5,4},{6,7},{7,6},{8,9},{9,8},{10,11... | collective-permute-start | bytes 786440 | tf_op jit(solution)/shard_map/ppermute | solution.py:275

commit v5 on v4

v5 whole, which is shorter than its diff:
```python
import functools

import jax
import jax.numpy as jnp
from jax import lax
from jax.experimental import pallas as pl
from jax.experimental.pallas import tpu as pltpu
from jax.sharding import PartitionSpec as P

L = 100
LE = 104
SPAN = LE - L
EPS = 1e-06
LANES = 128
PIECES = 4
ROWS = 16
TAPS = 4
TILE = 512
GROUP = 8
VMEM = 56 * 1024 * 1024


def embed_kernel(t_ref, off_ref, mask_ref, e_ref):
    rows, cols = off_ref.shape
    for w in range(cols // LANES):
        lanes = slice(w * LANES, (w + 1) * LANES)
        total = jnp.zeros((rows, LANES), jnp.float32)
        for l in range(L):
            v = t_ref[l, :, lanes].astype(jnp.float32)
            total = total + v * v
        scale = lax.rsqrt(total / L + EPS) * mask_ref[:, lanes].astype(jnp.float32) / L
        off = off_ref[:, lanes]
        odd = ((off & 1) == 1).astype(jnp.bfloat16) > 0
        high = (off >= 2).astype(jnp.bfloat16) > 0
        full = (off == SPAN).astype(jnp.bfloat16) > 0
        zero = jnp.zeros((rows, LANES), jnp.bfloat16)
        plain = [zero] * SPAN
        moved = [zero] * 2
        for j in range(LE):
            sample = t_ref[j, :, lanes] if j < L else zero
            now = jnp.where(odd, plain[-1], sample)
            value = jnp.where(full, plain[0], jnp.where(high, moved[0], now))
            e_ref[j, :, lanes] = (value.astype(jnp.float32) * scale).astype(jnp.bfloat16)
            plain = plain[1:] + [sample]
            moved = moved[1:] + [now]


def embed(templates, offsets, masks, piece):
    k, channels = offsets.shape
    rows = k // PIECES
    steps = rows // ROWS
    first = piece * steps
    width = 2 * LANES
    return pl.pallas_call(
        embed_kernel,
        grid=(steps, channels // width),
        in_specs=[
            pl.BlockSpec((L, ROWS, width), lambda i, j: (0, first + i, j)),
            pl.BlockSpec((ROWS, width), lambda i, j: (first + i, j)),
            pl.BlockSpec((ROWS, width), lambda i, j: (first + i, j)),
        ],
        out_specs=pl.BlockSpec((LE, ROWS, width), lambda i, j: (0, i, j)),
        out_shape=jax.ShapeDtypeStruct((LE, rows, channels), jnp.bfloat16),
        compiler_params=pltpu.CompilerParams(vmem_limit_bytes=VMEM),
        cost_estimate=pl.CostEstimate(
            flops=20 * LE * rows * channels,
            bytes_accessed=2 * 2 * LE * rows * channels,
            transcendentals=0,
        ),
    )(templates, offsets, masks)


def ring_position(b, n):
    z, y = b // 2, b % 2
    return z * (1 - y) + (n - 1 - z) * y


def ring_block(p, n):
    half = n // 2
    low = (p < half) * 1 if isinstance(p, int) else (p < half).astype(jnp.int32)
    return low * (2 * p) + (1 - low) * (2 * (n - 1 - p) + 1)


def ring_gather(x, n, beside):
    order = [ring_block(p, n) for p in range(n)]
    up = [(order[p], order[(p + 1) % n]) for p in range(n)]
    down = [(order[(p + 1) % n], order[p]) for p in range(n)]
    blocks = {0: x}
    done = []
    a = b = x
    for step in range(1, n // 2 + 1):
        a = lax.ppermute(a, "blk", up)
        if step < n // 2:
            b = lax.ppermute(b, "blk", down)
        if step <= PIECES:
            done.append(beside(step - 1))
            a, b, done[-1] = lax.optimization_barrier((a, b, done[-1]))
        blocks[n - step] = a
        if step < n // 2:
            blocks[step] = b
    return [blocks[d] for d in range(n)], done


def shift(value, lanes):
    moved = pltpu.roll(value, LANES - lanes, 1)
    lane = lax.broadcasted_iota(jnp.int32, value.shape, 1)
    return jnp.where(lane < LANES - lanes, moved, 0.0)


def extend(x_ref, first, period, start, size):
    rows = pl.ds(start, size)
    for i in range(TAPS):
        before = x_ref[first + i - period, rows, :].astype(jnp.float32)
        x_ref[first + i, rows, :] = shift(before, 1).astype(jnp.bfloat16)


def prepare(n, block_refs, flat_ref, x_ref, n_ref):
    lags, width = block_refs[0].shape
    period = n * lags // LANES
    me = ring_position(lax.axis_index("blk"), n)
    for d in range(n):
        where = ring_block(lax.rem(me + d, n), n)
        for w in range(width // LANES):
            flat_ref[w, pl.ds(pl.multiple_of(where * lags, lags), lags), :] = block_refs[d][
                :, w * LANES : (w + 1) * LANES
            ].astype(jnp.float32)

    def turn(u, carry):
        for w in range(width // LANES):
            value = flat_ref[w, pl.ds(u, LANES, stride=period), :]
            x_ref[u, w * LANES : (w + 1) * LANES, :] = value.T.astype(jnp.bfloat16)
        return carry

    lax.fori_loop(0, period, turn, 0)

    groups = period // GROUP

    def norms(i, carry):
        rows = pl.ds(pl.multiple_of(i * 16, 16), 16)
        square = []
        for u in range(period):
            value = x_ref[u, rows, :].astype(jnp.float32)
            square.append(value * value)
        sums = []
        for g in range(groups + LE // GROUP - 1):
            if g < groups:
                total = square[g * GROUP]
                for r in range(1, GROUP):
                    total = total + square[g * GROUP + r]
            else:
                total = shift(sums[g - groups], 1)
            sums.append(total)
        for g in range(groups):
            tail = sums[g + 1]
            for j in range(2, LE // GROUP):
                tail = tail + sums[g + j]
            tails = [None] * GROUP
            for r in range(GROUP - 1, -1, -1):
                tail = tail + square[g * GROUP + r]
                tails[r] = tail
            head = None
            for r in range(GROUP):
                total = tails[r]
                if r > 0:
                    s = g * GROUP + LE + r - 1
                    value = shift(square[s % period], s // period)
                    head = value if r == 1 else head + value
                    total = total + head
                n_ref[g * GROUP + r, rows, :] = lax.rsqrt(total / LE + EPS)
        return carry

    lax.fori_loop(0, width // 16, norms, 0)


def build(x_ref, n_ref, w_ref, tap0, start, size):
    period, width, _ = n_ref.shape
    for i in range(size // 16):
        first = pl.multiple_of(start + i * 16, 16)
        rows = pl.ds(first, 16)
        for u0 in range(0, period, 8):
            norm = [n_ref[u0 + u, rows, :] for u in range(8)]
            for s in range(TAPS + 7):
                value = x_ref[tap0 + u0 + s, rows, :].astype(jnp.float32)
                for tap in range(max(0, s - 7), min(TAPS, s + 1)):
                    u = s - tap
                    where = pl.ds(pl.multiple_of(tap * width + first, 16), 16)
                    lanes = slice((u0 + u) * LANES, (u0 + u + 1) * LANES)
                    w_ref[where, lanes] = (value * norm[u]).astype(jnp.bfloat16)


def correlate_kernel(n, steps, *refs):
    blocks = refs[:n]
    e_refs = refs[n : n + PIECES]
    mine_ref, other_ref, acc_ref, turned_ref, flat_ref, x_ref, n_ref, even_ref, odd_ref = refs[
        n + PIECES :
    ]
    lags, width = blocks[0].shape
    period = n_ref.shape[0]
    tiles = n * lags // TILE
    share = width // tiles
    step = pl.program_id(0)

    @pl.when(step == 0)
    def _():
        prepare(n, blocks, flat_ref, x_ref, n_ref)
        acc_ref[...] = jnp.zeros_like(acc_ref)

        def first(i, carry):
            start = pl.multiple_of(i * 16, 16)
            extend(x_ref, period, period, start, 16)
            extend(x_ref, period + TAPS, period, start, 16)
            build(x_ref, n_ref, even_ref, 0, start, 16)
            return carry

        lax.fori_loop(0, width // 16, first, 0)

    def advance(now_ref, later_ref, part, tap0):
        def tile(m, carry):
            columns = pl.ds(pl.multiple_of(m * TILE, TILE), TILE)
            weights = jnp.concatenate(
                [
                    jnp.concatenate([e_ref[part * TAPS + tap] for e_ref in e_refs], axis=0)
                    for tap in range(TAPS)
                ],
                axis=1,
            )
            acc_ref[:, columns] += jnp.dot(
                weights, now_ref[:, columns], preferred_element_type=jnp.float32
            )
            start = pl.multiple_of(m * share, share)
            build(x_ref, n_ref, later_ref, tap0, start, share)
            extend(x_ref, tap0 + TAPS + period, period, start, share)
            return carry

        lax.fori_loop(0, tiles, tile, 0)

    advance(even_ref, odd_ref, 0, step * 2 * TAPS + TAPS)
    advance(odd_ref, even_ref, 1, step * 2 * TAPS + 2 * TAPS)

    @pl.when(step == steps - 1)
    def _():
        for u in range(period):
            value = acc_ref[:, u * LANES : (u + 1) * LANES]
            turned_ref[pl.ds(u, LANES, stride=period), :] = value.T
        core = lax.axis_index("chan")
        half = n * lags // 2
        for out_ref, first in ((mine_ref, core * half), (other_ref, (1 - core) * half)):
            for v in range(0, half, LANES):
                rows = pl.ds(pl.multiple_of(first + v, LANES), LANES)
                out_ref[:, v : v + LANES] = turned_ref[rows, :].T


def correlate(blocks, pieces):
    n = len(blocks)
    lags, width = blocks[0].shape
    k = PIECES * pieces[0].shape[1]
    period = n * lags // LANES
    steps = LE // (2 * TAPS)
    whole = pl.BlockSpec(memory_space=pltpu.VMEM)
    e_spec = pl.BlockSpec((2 * TAPS, k // PIECES, width), lambda i: (i, 0, 0))
    return pl.pallas_call(
        functools.partial(correlate_kernel, n, steps),
        grid=(steps,),
        in_specs=[whole] * n + [e_spec] * PIECES,
        out_specs=[whole, whole],
        out_shape=[jax.ShapeDtypeStruct((k, n * lags // 2), jnp.float32)] * 2,
        scratch_shapes=[
            pltpu.VMEM((k, n * lags), jnp.float32),
            pltpu.VMEM((n * lags, k), jnp.float32),
            pltpu.VMEM((width // LANES, n * lags, LANES), jnp.float32),
            pltpu.VMEM((period + LE + 2 * TAPS, width, LANES), jnp.bfloat16),
            pltpu.VMEM((period, width, LANES), jnp.float32),
            pltpu.VMEM((TAPS * width, n * lags), jnp.bfloat16),
            pltpu.VMEM((TAPS * width, n * lags), jnp.bfloat16),
        ],
        compiler_params=pltpu.CompilerParams(vmem_limit_bytes=VMEM),
        cost_estimate=pl.CostEstimate(
            flops=2 * n * lags * LE * width * k,
            bytes_accessed=2 * LE * width * k,
            transcendentals=0,
        ),
    )(*blocks, *pieces)


def per_device(n, records, templates, offsets, masks):
    blocks, pieces = ring_gather(
        records.T, n, lambda piece: embed(templates, offsets, masks, piece)
    )
    mine, other = correlate(blocks, pieces)
    return mine + lax.ppermute(other, "chan", [(0, 1), (1, 0)])


def solution(mesh):
    return jax.shard_map(
        functools.partial(per_device, mesh.shape["blk"]),
        mesh=mesh,
        in_specs=(
            P("chan", ("groups", "blk")),
            P(None, ("groups", "blk"), "chan"),
            P(("groups", "blk"), "chan"),
            P(("groups", "blk"), "chan"),
        ),
        out_specs=P(("groups", "blk"), "chan"),
        check_vma=False,
    )
```

time: 106 us -> 111 us (1.047)
  Pallas kernels: 90.9 us -> 96 us
    pallas_call x1, Pallas kernels: 69.5 us -> 74.7 us  [correlate(): pl.pallas_call(functools.partial(correlate_kernel, n, steps), grid=(steps...]
  transfers between devices with their start and end apart: 8 -> 8, of which waited for: 1 -> 1; matrix products, arithmetic and copies ran while one was open for 0% -> 0% of each run, Pallas kernels for 20% -> 19%
where the time goes in v5:
time: 111 us
  Pallas kernels  96 us (86%)
  starting transfers between devices  9.31 us (8%)
  waiting for transfers between devices  1.76 us (2%)
  other arithmetic  1.7 us (2%)
  local copies, waits for them, and re-layouts  1.68 us (2%)
    pallas_call x1, Pallas kernels, correlate(): pl.pallas_call(functools.partial(correlate_kernel, n, steps), grid=(steps...  74.7 us
    pallas_call x4, Pallas kernels, embed(): pl.pallas_call(embed_kernel, grid=(steps, channels // width), in_specs=[p...  21.3 us
    ppermute x3, starting transfers between devices, ring_gather(): b = lax.ppermute(b, 'blk', down)  6.93 us
    ppermute x4, starting transfers between devices, ring_gather(): a = lax.ppermute(a, 'blk', up)  2.38 us
  transfers between devices with their start and end apart: 8, of which 1 were waited for; matrix products, arithmetic and copies ran while one was open for 0% of the time, Pallas kernels for 19%

profile of v5, /device:TPU:0, one launch (start us, length us, event | category | flops | bytes accessed | tf_op | source)
XLA Modules:
  0.0 110.6 jit_solution(1626697455614257822)
XLA Ops:
  0.0 1.0 copy.5
  1.0 3.0 %collective-permute-start.1 = (bf16[128,512]{1,0:T(8,128)(2,1)S(1)}, bf16[128,512]{1,0:T(8,128)(2,1)S(1)}, u32[]{:S(2)}, u32[]{:S(2)}) collective-permute-start(bf16[128,512]{1,0:T(8,128)(2,1)S(1)} %bitcast.1), channel_id=1, source_target_pairs={{4,0},{8,4},{12,8},{14,12},{10,14},{6,10},{2,6},{0,2},{5,1},{9,5},... | collective-permute-start | bytes 393224 | tf_op jit(solution)/shard_map/ppermute | solution.py:94
  4.0 0.1 collective-permute-start
  4.2 5.3 %shard_map.46.refs_8_ = bf16[104,32,512]{2,1,0:T(8,128)(2,1)} custom-call(bf16[100,128,512]{2,1,0:T(8,128)(2,1)} %t_ref.7, s32[128,512]{1,0:T(8,128)} %off_ref.7, s32[128,512]{1,0:T(8,128)} %mask_ref.7), custom_call_target="tpu_custom_call" | custom-call | flops 34078720 | bytes 6815744 | tf_op jit(solution)/shard_map/pallas_call | solution.py:54
  9.5 0.0 collective-permute-done.1.refs_1_
  9.5 0.0 collective-permute-done.refs_7_
  9.5 2.0 %collective-permute-start.3 = (bf16[128,512]{1,0:T(8,128)(2,1)S(1)}, bf16[128,512]{1,0:T(8,128)(2,1)S(1)}, u32[]{:S(2)}, u32[]{:S(2)}) collective-permute-start(bf16[128,512]{1,0:T(8,128)(2,1)S(1)} %collective-permute-done.1.refs_1_), channel_id=1, source_target_pairs={{4,0},{8,4},{12,8},{14,12},{10,14},{6,10},{2,6},{0,2},{5,1},{9,5},... | collective-permute-start | bytes 393224 | tf_op jit(solution)/shard_map/ppermute | solution.py:94
  11.5 0.1 collective-permute-start.2
  11.6 5.4 %shard_map.47.refs_9_ = bf16[104,32,512]{2,1,0:T(8,128)(2,1)} custom-call(bf16[100,128,512]{2,1,0:T(8,128)(2,1)} %t_ref.7, s32[128,512]{1,0:T(8,128)} %off_ref.7, s32[128,512]{1,0:T(8,128)} %mask_ref.7), custom_call_target="tpu_custom_call" | custom-call | flops 34078720 | bytes 6815744 | tf_op jit(solution)/shard_map/pallas_call | solution.py:54
  16.9 0.0 collective-permute-done.3.refs_2_
  17.0 0.0 collective-permute-done.2.refs_6_
  17.0 2.0 %collective-permute-start.5 = (bf16[128,512]{1,0:T(8,128)(2,1)S(1)}, bf16[128,512]{1,0:T(8,128)(2,1)S(1)}, u32[]{:S(2)}, u32[]{:S(2)}) collective-permute-start(bf16[128,512]{1,0:T(8,128)(2,1)S(1)} %collective-permute-done.3.refs_2_), channel_id=1, source_target_pairs={{4,0},{8,4},{12,8},{14,12},{10,14},{6,10},{2,6},{0,2},{5,1},{9,5},... | collective-permute-start | bytes 393224 | tf_op jit(solution)/shard_map/ppermute | solution.py:94
  18.9 0.1 collective-permute-start.4
  19.1 5.4 %shard_map.48.refs_10_ = bf16[104,32,512]{2,1,0:T(8,128)(2,1)} custom-call(bf16[100,128,512]{2,1,0:T(8,128)(2,1)} %t_ref.7, s32[128,512]{1,0:T(8,128)} %off_ref.7, s32[128,512]{1,0:T(8,128)} %mask_ref.7), custom_call_target="tpu_custom_call" | custom-call | flops 34078720 | bytes 6815744 | tf_op jit(solution)/shard_map/pallas_call | solution.py:54
  24.4 0.0 collective-permute-done.5.refs_3_
  24.5 0.0 collective-permute-done.4.refs_5_
  24.5 2.0 %collective-permute-start.6 = (bf16[128,512]{1,0:T(8,128)(2,1)S(1)}, bf16[128,512]{1,0:T(8,128)(2,1)S(1)}, u32[]{:S(2)}, u32[]{:S(2)}) collective-permute-start(bf16[128,512]{1,0:T(8,128)(2,1)S(1)} %collective-permute-done.4.refs_5_), channel_id=1, source_target_pairs={{0,4},{4,8},{8,12},{12,14},{14,10},{10,6},{6,2},{2,0},{1,5},{5,9},... | collective-permute-start | bytes 393224 | tf_op jit(solution)/shard_map/ppermute | solution.py:92
  26.5 5.3 %shard_map.49.refs_11_ = bf16[104,32,512]{2,1,0:T(8,128)(2,1)} custom-call(bf16[100,128,512]{2,1,0:T(8,128)(2,1)} %t_ref.7, s32[128,512]{1,0:T(8,128)} %off_ref.7, s32[128,512]{1,0:T(8,128)} %mask_ref.7), custom_call_target="tpu_custom_call" | custom-call | flops 34078720 | bytes 6815744 | tf_op jit(solution)/shard_map/pallas_call | solution.py:54
  31.8 0.0 collective-permute-done.6.refs_4_
  31.8 0.6 copy-done.7
  32.5 74.7 %shard_map.50 = (f32[128,512]{1,0:T(8,128)}, f32[128,512]{1,0:T(8,128)}) custom-call(bf16[128,512]{1,0:T(8,128)(2,1)} %bitcast.3, bf16[128,512]{1,0:T(8,128)(2,1)} %copy-done.1, bf16[128,512]{1,0:T(8,128)(2,1)} %copy-done.3, bf16[128,512]{1,0:T(8,128)(2,1)} %copy-done.5, bf16[128,512]{1,0:T(8,128)(2,1)} %copy-done.7, bf16[128,512]{1,0:T(8,128)(2,1)} %copy-done.6, ...), custom_call_target="tpu_custom_call" | custom-call | flops 13958643712 | bytes 13631488 | tf_op jit(solution)/shard_map/pallas_call | solution.py:261
  107.1 0.0 collective-permute-start.7
  107.1 1.7 %collective-permute-done.7 = f32[128,512]{1,0:T(8,128)S(1)} collective-permute-done((f32[128,512]{1,0:T(8,128)}, f32[128,512]{1,0:T(8,128)S(1)}, u32[]{:S(2)}, u32[]{:S(2)}) %collective-permute-start.7) | collective-permute-done | bytes 262176 | tf_op jit(solution)/shard_map/ppermute | solution.py:290
  108.9 1.7 %add.3 = f32[128,512]{1,0:T(8,128)} add(f32[128,512]{1,0:T(8,128)} %get-tuple-element.29, f32[128,512]{1,0:T(8,128)S(1)} %collective-permute-done.7) | non-fusion elementwise | flops 65536 | bytes 786432 | tf_op jit(solution)/shard_map/add | solution.py:290
  (15 shorter events, 0.0 us)
Async XLA Ops:
  1.0 8.5 %copy-start = (bf16[512,128]{0,1:T(8,128)(2,1)}, bf16[512,128]{0,1:T(8,128)(2,1)S(1)}, u32[]{:S(2)}) copy-start(bf16[512,128]{0,1:T(8,128)(2,1)S(1)} %copy.5) | copy-start | bytes 393220
  1.0 8.4 %collective-permute-start.1 = (bf16[128,512]{1,0:T(8,128)(2,1)S(1)}, bf16[128,512]{1,0:T(8,128)(2,1)S(1)}, u32[]{:S(2)}, u32[]{:S(2)}) collective-permute-start(bf16[128,512]{1,0:T(8,128)(2,1)S(1)} %bitcast.1), channel_id=1, source_target_pairs={{4,0},{8,4},{12,8},{14,12},{10,14},{6,10},{2,6},{0,2},{5,1},{9,5},... | collective-permute-start | bytes 393224 | tf_op jit(solution)/shard_map/ppermute | solution.py:94
  4.0 5.4 %collective-permute-start = (bf16[128,512]{1,0:T(8,128)(2,1)S(1)}, bf16[128,512]{1,0:T(8,128)(2,1)S(1)}, u32[]{:S(2)}, u32[]{:S(2)}) collective-permute-start(bf16[128,512]{1,0:T(8,128)(2,1)S(1)} %bitcast.2), channel_id=1, source_target_pairs={{0,4},{4,8},{8,12},{12,14},{14,10},{10,6},{6,2},{2,0},{1,5},{5,9},... | collective-permute-start | bytes 393224 | tf_op jit(solution)/shard_map/ppermute | solution.py:92
  9.5 7.5 %copy-start.1 = (bf16[128,512]{1,0:T(8,128)(2,1)}, bf16[128,512]{1,0:T(8,128)(2,1)S(1)}, u32[]{:S(2)}) copy-start(bf16[128,512]{1,0:T(8,128)(2,1)S(1)} %collective-permute-done.1.refs_1_) | copy-start | bytes 393220
  9.5 7.5 %copy-start.2 = (bf16[128,512]{1,0:T(8,128)(2,1)}, bf16[128,512]{1,0:T(8,128)(2,1)S(1)}, u32[]{:S(2)}) copy-start(bf16[128,512]{1,0:T(8,128)(2,1)S(1)} %collective-permute-done.refs_7_) | copy-start | bytes 393220
  9.5 7.5 %collective-permute-start.3 = (bf16[128,512]{1,0:T(8,128)(2,1)S(1)}, bf16[128,512]{1,0:T(8,128)(2,1)S(1)}, u32[]{:S(2)}, u32[]{:S(2)}) collective-permute-start(bf16[128,512]{1,0:T(8,128)(2,1)S(1)} %collective-permute-done.1.refs_1_), channel_id=1, source_target_pairs={{4,0},{8,4},{12,8},{14,12},{10,14},{6,10},{2,6},{0,2},{5,1},{9,5},... | collective-permute-start | bytes 393224 | tf_op jit(solution)/shard_map/ppermute | solution.py:94
  11.5 5.5 %collective-permute-start.2 = (bf16[128,512]{1,0:T(8,128)(2,1)S(1)}, bf16[128,512]{1,0:T(8,128)(2,1)S(1)}, u32[]{:S(2)}, u32[]{:S(2)}) collective-permute-start(bf16[128,512]{1,0:T(8,128)(2,1)S(1)} %collective-permute-done.refs_7_), channel_id=1, source_target_pairs={{0,4},{4,8},{8,12},{12,14},{14,10},{10,6},{6,2},{2,0},{1,5},{5,9},... | collective-permute-start | bytes 393224 | tf_op jit(solution)/shard_map/ppermute | solution.py:92
  17.0 7.5 %copy-start.3 = (bf16[128,512]{1,0:T(8,128)(2,1)}, bf16[128,512]{1,0:T(8,128)(2,1)S(1)}, u32[]{:S(2)}) copy-start(bf16[128,512]{1,0:T(8,128)(2,1)S(1)} %collective-permute-done.3.refs_2_) | copy-start | bytes 393220
  17.0 7.5 %copy-start.4 = (bf16[128,512]{1,0:T(8,128)(2,1)}, bf16[128,512]{1,0:T(8,128)(2,1)S(1)}, u32[]{:S(2)}) copy-start(bf16[128,512]{1,0:T(8,128)(2,1)S(1)} %collective-permute-done.2.refs_6_) | copy-start | bytes 393220
  17.0 7.5 %collective-permute-start.5 = (bf16[128,512]{1,0:T(8,128)(2,1)S(1)}, bf16[128,512]{1,0:T(8,128)(2,1)S(1)}, u32[]{:S(2)}, u32[]{:S(2)}) collective-permute-start(bf16[128,512]{1,0:T(8,128)(2,1)S(1)} %collective-permute-done.3.refs_2_), channel_id=1, source_target_pairs={{4,0},{8,4},{12,8},{14,12},{10,14},{6,10},{2,6},{0,2},{5,1},{9,5},... | collective-permute-start | bytes 393224 | tf_op jit(solution)/shard_map/ppermute | solution.py:94
  18.9 5.5 %collective-permute-start.4 = (bf16[128,512]{1,0:T(8,128)(2,1)S(1)}, bf16[128,512]{1,0:T(8,128)(2,1)S(1)}, u32[]{:S(2)}, u32[]{:S(2)}) collective-permute-start(bf16[128,512]{1,0:T(8,128)(2,1)S(1)} %collective-permute-done.2.refs_6_), channel_id=1, source_target_pairs={{0,4},{4,8},{8,12},{12,14},{14,10},{10,6},{6,2},{2,0},{1,5},{5,9},... | collective-permute-start | bytes 393224 | tf_op jit(solution)/shard_map/ppermute | solution.py:92
  24.4 7.4 %copy-start.5 = (bf16[128,512]{1,0:T(8,128)(2,1)}, bf16[128,512]{1,0:T(8,128)(2,1)S(1)}, u32[]{:S(2)}) copy-start(bf16[128,512]{1,0:T(8,128)(2,1)S(1)} %collective-permute-done.5.refs_3_) | copy-start | bytes 393220
  24.5 7.3 %copy-start.6 = (bf16[128,512]{1,0:T(8,128)(2,1)}, bf16[128,512]{1,0:T(8,128)(2,1)S(1)}, u32[]{:S(2)}) copy-start(bf16[128,512]{1,0:T(8,128)(2,1)S(1)} %collective-permute-done.4.refs_5_) | copy-start | bytes 393220
  24.5 7.3 %collective-permute-start.6 = (bf16[128,512]{1,0:T(8,128)(2,1)S(1)}, bf16[128,512]{1,0:T(8,128)(2,1)S(1)}, u32[]{:S(2)}, u32[]{:S(2)}) collective-permute-start(bf16[128,512]{1,0:T(8,128)(2,1)S(1)} %collective-permute-done.4.refs_5_), channel_id=1, source_target_pairs={{0,4},{4,8},{8,12},{12,14},{14,10},{10,6},{6,2},{2,0},{1,5},{5,9},... | collective-permute-start | bytes 393224 | tf_op jit(solution)/shard_map/ppermute | solution.py:92
  31.8 0.6 copy-start.7
  107.1 1.7 %collective-permute-start.7 = (f32[128,512]{1,0:T(8,128)}, f32[128,512]{1,0:T(8,128)S(1)}, u32[]{:S(2)}, u32[]{:S(2)}) collective-permute-start(f32[128,512]{1,0:T(8,128)} %get-tuple-element.30), channel_id=1, source_target_pairs={{0,1},{1,0},{2,3},{3,2},{4,5},{5,4},{6,7},{7,6},{8,9},{9,8},{10,11... | collective-permute-start | bytes 786440 | tf_op jit(solution)/shard_map/ppermute | solution.py:290

commit v6 on v5

--- a/solution.py
+++ b/solution.py
@@ -114,7 +114,7 @@
         x_ref[first + i, rows, :] = shift(before, 1).astype(jnp.bfloat16)
 
 
-def prepare(n, block_refs, flat_ref, x_ref, n_ref):
+def prepare(n, block_refs, flat_ref, x_ref, high_ref, low_ref):
     lags, width = block_refs[0].shape
     period = n * lags // LANES
     me = ring_position(lax.axis_index("blk"), n)
@@ -166,50 +166,56 @@
                     value = shift(square[s % period], s // period)
                     head = value if r == 1 else head + value
                     total = total + head
-                n_ref[g * GROUP + r, rows, :] = lax.rsqrt(total / LE + EPS)
+                norm = lax.rsqrt(total / LE + EPS)
+                high = norm.astype(jnp.bfloat16)
+                high_ref[g * GROUP + r, rows, :] = high
+                low_ref[g * GROUP + r, rows, :] = (norm - high.astype(jnp.float32)).astype(
+                    jnp.bfloat16
+                )
         return carry
 
     lax.fori_loop(0, width // 16, norms, 0)
 
 
-def build(x_ref, n_ref, w_ref, tap0, start, size):
-    period, width, _ = n_ref.shape
+def build(x_ref, high_ref, low_ref, w_ref, tap0, start, size):
+    period, width, _ = high_ref.shape
     for i in range(size // 16):
         first = pl.multiple_of(start + i * 16, 16)
         rows = pl.ds(first, 16)
         for u0 in range(0, period, 8):
-            norm = [n_ref[u0 + u, rows, :] for u in range(8)]
+            high = [high_ref[u0 + u, rows, :] for u in range(8)]
+            low = [low_ref[u0 + u, rows, :] for u in range(8)]
             for s in range(TAPS + 7):
-                value = x_ref[tap0 + u0 + s, rows, :].astype(jnp.float32)
+                value = x_ref[tap0 + u0 + s, rows, :]
                 for tap in range(max(0, s - 7), min(TAPS, s + 1)):
                     u = s - tap
                     where = pl.ds(pl.multiple_of(tap * width + first, 16), 16)
                     lanes = slice((u0 + u) * LANES, (u0 + u + 1) * LANES)
-                    w_ref[where, lanes] = (value * norm[u]).astype(jnp.bfloat16)
+                    w_ref[where, lanes] = value * high[u] + value * low[u]
 
 
 def correlate_kernel(n, steps, *refs):
     blocks = refs[:n]
     e_refs = refs[n : n + PIECES]
-    mine_ref, other_ref, acc_ref, turned_ref, flat_ref, x_ref, n_ref, even_ref, odd_ref = refs[
+    mine_ref, other_ref, acc_ref, turned_ref, flat_ref, x_ref, high_ref, low_ref, even_ref, odd_ref = refs[
         n + PIECES :
     ]
     lags, width = blocks[0].shape
-    period = n_ref.shape[0]
+    period = high_ref.shape[0]
     tiles = n * lags // TILE
     share = width // tiles
     step = pl.program_id(0)
 
     @pl.when(step == 0)
     def _():
-        prepare(n, blocks, flat_ref, x_ref, n_ref)
+        prepare(n, blocks, flat_ref, x_ref, high_ref, low_ref)
         acc_ref[...] = jnp.zeros_like(acc_ref)
 
         def first(i, carry):
             start = pl.multiple_of(i * 16, 16)
             extend(x_ref, period, period, start, 16)
             extend(x_ref, period + TAPS, period, start, 16)
-            build(x_ref, n_ref, even_ref, 0, start, 16)
+            build(x_ref, high_ref, low_ref, even_ref, 0, start, 16)
             return carry
 
         lax.fori_loop(0, width // 16, first, 0)
@@ -228,7 +234,7 @@
                 weights, now_ref[:, columns], preferred_element_type=jnp.float32
             )
             start = pl.multiple_of(m * share, share)
-            build(x_ref, n_ref, later_ref, tap0, start, share)
+            build(x_ref, high_ref, low_ref, later_ref, tap0, start, share)
             extend(x_ref, tap0 + TAPS + period, period, start, share)
             return carry
 
@@ -269,7 +275,8 @@
             pltpu.VMEM((n * lags, k), jnp.float32),
             pltpu.VMEM((width // LANES, n * lags, LANES), jnp.float32),
             pltpu.VMEM((period + LE + 2 * TAPS, width, LANES), jnp.bfloat16),
-            pltpu.VMEM((period, width, LANES), jnp.float32),
+            pltpu.VMEM((period, width, LANES), jnp.bfloat16),
+            pltpu.VMEM((period, width, LANES), jnp.bfloat16),
             pltpu.VMEM((TAPS * width, n * lags), jnp.bfloat16),
             pltpu.VMEM((TAPS * width, n * lags), jnp.bfloat16),
         ],

time: 111 us -> 125 us (1.13)
  Pallas kernels: 96 us -> 110 us
    pallas_call x1, Pallas kernels: 74.7 us -> 88.6 us  [correlate(): pl.pallas_call(functools.partial(correlate_kernel, n, steps), grid=(steps...]
  transfers between devices with their start and end apart: 8 -> 8, of which waited for: 1 -> 1; matrix products, arithmetic and copies ran while one was open for 0% -> 0% of each run, Pallas kernels for 19% -> 17%
where the time goes in v6:
time: 125 us
  Pallas kernels  110 us (88%)
  starting transfers between devices  9.31 us (7%)
  waiting for transfers between devices  1.76 us (1%)
  other arithmetic  1.7 us (1%)
  local copies, waits for them, and re-layouts  1.68 us (1%)
    pallas_call x1, Pallas kernels, correlate(): pl.pallas_call(functools.partial(correlate_kernel, n, steps), grid=(steps...  88.6 us
    pallas_call x4, Pallas kernels, embed(): pl.pallas_call(embed_kernel, grid=(steps, channels // width), in_specs=[p...  21.3 us
    ppermute x3, starting transfers between devices, ring_gather(): b = lax.ppermute(b, 'blk', down)  6.93 us
  transfers between devices with their start and end apart: 8, of which 1 were waited for; matrix products, arithmetic and copies ran while one was open for 0% of the time, Pallas kernels for 17%

profile of v6, /device:TPU:0, one launch (start us, length us, event | category | flops | bytes accessed | tf_op | source)
XLA Modules:
  0.0 124.5 jit_solution(17816467863223316011)
XLA Ops:
  0.0 1.0 copy.5
  1.0 3.0 %collective-permute-start.1 = (bf16[128,512]{1,0:T(8,128)(2,1)S(1)}, bf16[128,512]{1,0:T(8,128)(2,1)S(1)}, u32[]{:S(2)}, u32[]{:S(2)}) collective-permute-start(bf16[128,512]{1,0:T(8,128)(2,1)S(1)} %bitcast.1), channel_id=1, source_target_pairs={{4,0},{8,4},{12,8},{14,12},{10,14},{6,10},{2,6},{0,2},{5,1},{9,5},... | collective-permute-start | bytes 393224 | tf_op jit(solution)/shard_map/ppermute | solution.py:94
  4.0 0.1 collective-permute-start
  4.2 5.3 %shard_map.46.refs_8_ = bf16[104,32,512]{2,1,0:T(8,128)(2,1)} custom-call(bf16[100,128,512]{2,1,0:T(8,128)(2,1)} %t_ref.7, s32[128,512]{1,0:T(8,128)} %off_ref.7, s32[128,512]{1,0:T(8,128)} %mask_ref.7), custom_call_target="tpu_custom_call" | custom-call | flops 34078720 | bytes 6815744 | tf_op jit(solution)/shard_map/pallas_call | solution.py:54
  9.5 0.0 collective-permute-done.1.refs_1_
  9.5 0.0 collective-permute-done.refs_7_
  9.5 2.0 %collective-permute-start.3 = (bf16[128,512]{1,0:T(8,128)(2,1)S(1)}, bf16[128,512]{1,0:T(8,128)(2,1)S(1)}, u32[]{:S(2)}, u32[]{:S(2)}) collective-permute-start(bf16[128,512]{1,0:T(8,128)(2,1)S(1)} %collective-permute-done.1.refs_1_), channel_id=1, source_target_pairs={{4,0},{8,4},{12,8},{14,12},{10,14},{6,10},{2,6},{0,2},{5,1},{9,5},... | collective-permute-start | bytes 393224 | tf_op jit(solution)/shard_map/ppermute | solution.py:94
  11.5 0.1 collective-permute-start.2
  11.6 5.4 %shard_map.47.refs_9_ = bf16[104,32,512]{2,1,0:T(8,128)(2,1)} custom-call(bf16[100,128,512]{2,1,0:T(8,128)(2,1)} %t_ref.7, s32[128,512]{1,0:T(8,128)} %off_ref.7, s32[128,512]{1,0:T(8,128)} %mask_ref.7), custom_call_target="tpu_custom_call" | custom-call | flops 34078720 | bytes 6815744 | tf_op jit(solution)/shard_map/pallas_call | solution.py:54
  16.9 0.0 collective-permute-done.3.refs_2_
  17.0 0.0 collective-permute-done.2.refs_6_
  17.0 2.0 %collective-permute-start.5 = (bf16[128,512]{1,0:T(8,128)(2,1)S(1)}, bf16[128,512]{1,0:T(8,128)(2,1)S(1)}, u32[]{:S(2)}, u32[]{:S(2)}) collective-permute-start(bf16[128,512]{1,0:T(8,128)(2,1)S(1)} %collective-permute-done.3.refs_2_), channel_id=1, source_target_pairs={{4,0},{8,4},{12,8},{14,12},{10,14},{6,10},{2,6},{0,2},{5,1},{9,5},... | collective-permute-start | bytes 393224 | tf_op jit(solution)/shard_map/ppermute | solution.py:94
  18.9 0.1 collective-permute-start.4
  19.1 5.4 %shard_map.48.refs_10_ = bf16[104,32,512]{2,1,0:T(8,128)(2,1)} custom-call(bf16[100,128,512]{2,1,0:T(8,128)(2,1)} %t_ref.7, s32[128,512]{1,0:T(8,128)} %off_ref.7, s32[128,512]{1,0:T(8,128)} %mask_ref.7), custom_call_target="tpu_custom_call" | custom-call | flops 34078720 | bytes 6815744 | tf_op jit(solution)/shard_map/pallas_call | solution.py:54
  24.4 0.0 collective-permute-done.5.refs_3_
  24.5 0.0 collective-permute-done.4.refs_5_
  24.5 2.0 %collective-permute-start.6 = (bf16[128,512]{1,0:T(8,128)(2,1)S(1)}, bf16[128,512]{1,0:T(8,128)(2,1)S(1)}, u32[]{:S(2)}, u32[]{:S(2)}) collective-permute-start(bf16[128,512]{1,0:T(8,128)(2,1)S(1)} %collective-permute-done.4.refs_5_), channel_id=1, source_target_pairs={{0,4},{4,8},{8,12},{12,14},{14,10},{10,6},{6,2},{2,0},{1,5},{5,9},... | collective-permute-start | bytes 393224 | tf_op jit(solution)/shard_map/ppermute | solution.py:92
  26.5 5.3 %shard_map.49.refs_11_ = bf16[104,32,512]{2,1,0:T(8,128)(2,1)} custom-call(bf16[100,128,512]{2,1,0:T(8,128)(2,1)} %t_ref.7, s32[128,512]{1,0:T(8,128)} %off_ref.7, s32[128,512]{1,0:T(8,128)} %mask_ref.7), custom_call_target="tpu_custom_call" | custom-call | flops 34078720 | bytes 6815744 | tf_op jit(solution)/shard_map/pallas_call | solution.py:54
  31.8 0.0 collective-permute-done.6.refs_4_
  31.8 0.6 copy-done.7
  32.5 88.6 %shard_map.50 = (f32[128,512]{1,0:T(8,128)}, f32[128,512]{1,0:T(8,128)}) custom-call(bf16[128,512]{1,0:T(8,128)(2,1)} %bitcast.3, bf16[128,512]{1,0:T(8,128)(2,1)} %copy-done.1, bf16[128,512]{1,0:T(8,128)(2,1)} %copy-done.3, bf16[128,512]{1,0:T(8,128)(2,1)} %copy-done.5, bf16[128,512]{1,0:T(8,128)(2,1)} %copy-done.7, bf16[128,512]{1,0:T(8,128)(2,1)} %copy-done.6, ...), custom_call_target="tpu_custom_call" | custom-call | flops 13958643712 | bytes 13631488 | tf_op jit(solution)/shard_map/pallas_call | solution.py:267
  121.1 0.0 collective-permute-start.7
  121.1 1.7 %collective-permute-done.7 = f32[128,512]{1,0:T(8,128)S(1)} collective-permute-done((f32[128,512]{1,0:T(8,128)}, f32[128,512]{1,0:T(8,128)S(1)}, u32[]{:S(2)}, u32[]{:S(2)}) %collective-permute-start.7) | collective-permute-done | bytes 262176 | tf_op jit(solution)/shard_map/ppermute | solution.py:297
  122.8 1.7 %add.3 = f32[128,512]{1,0:T(8,128)} add(f32[128,512]{1,0:T(8,128)} %get-tuple-element.29, f32[128,512]{1,0:T(8,128)S(1)} %collective-permute-done.7) | non-fusion elementwise | flops 65536 | bytes 786432 | tf_op jit(solution)/shard_map/add | solution.py:297
  (15 shorter events, 0.0 us)
Async XLA Ops:
  1.0 8.5 %copy-start = (bf16[512,128]{0,1:T(8,128)(2,1)}, bf16[512,128]{0,1:T(8,128)(2,1)S(1)}, u32[]{:S(2)}) copy-start(bf16[512,128]{0,1:T(8,128)(2,1)S(1)} %copy.5) | copy-start | bytes 393220
  1.0 8.4 %collective-permute-start.1 = (bf16[128,512]{1,0:T(8,128)(2,1)S(1)}, bf16[128,512]{1,0:T(8,128)(2,1)S(1)}, u32[]{:S(2)}, u32[]{:S(2)}) collective-permute-start(bf16[128,512]{1,0:T(8,128)(2,1)S(1)} %bitcast.1), channel_id=1, source_target_pairs={{4,0},{8,4},{12,8},{14,12},{10,14},{6,10},{2,6},{0,2},{5,1},{9,5},... | collective-permute-start | bytes 393224 | tf_op jit(solution)/shard_map/ppermute | solution.py:94
  4.0 5.4 %collective-permute-start = (bf16[128,512]{1,0:T(8,128)(2,1)S(1)}, bf16[128,512]{1,0:T(8,128)(2,1)S(1)}, u32[]{:S(2)}, u32[]{:S(2)}) collective-permute-start(bf16[128,512]{1,0:T(8,128)(2,1)S(1)} %bitcast.2), channel_id=1, source_target_pairs={{0,4},{4,8},{8,12},{12,14},{14,10},{10,6},{6,2},{2,0},{1,5},{5,9},... | collective-permute-start | bytes 393224 | tf_op jit(solution)/shard_map/ppermute | solution.py:92
  9.5 7.5 %copy-start.1 = (bf16[128,512]{1,0:T(8,128)(2,1)}, bf16[128,512]{1,0:T(8,128)(2,1)S(1)}, u32[]{:S(2)}) copy-start(bf16[128,512]{1,0:T(8,128)(2,1)S(1)} %collective-permute-done.1.refs_1_) | copy-start | bytes 393220
  9.5 7.5 %copy-start.2 = (bf16[128,512]{1,0:T(8,128)(2,1)}, bf16[128,512]{1,0:T(8,128)(2,1)S(1)}, u32[]{:S(2)}) copy-start(bf16[128,512]{1,0:T(8,128)(2,1)S(1)} %collective-permute-done.refs_7_) | copy-start | bytes 393220
  9.5 7.5 %collective-permute-start.3 = (bf16[128,512]{1,0:T(8,128)(2,1)S(1)}, bf16[128,512]{1,0:T(8,128)(2,1)S(1)}, u32[]{:S(2)}, u32[]{:S(2)}) collective-permute-start(bf16[128,512]{1,0:T(8,128)(2,1)S(1)} %collective-permute-done.1.refs_1_), channel_id=1, source_target_pairs={{4,0},{8,4},{12,8},{14,12},{10,14},{6,10},{2,6},{0,2},{5,1},{9,5},... | collective-permute-start | bytes 393224 | tf_op jit(solution)/shard_map/ppermute | solution.py:94
  11.5 5.5 %collective-permute-start.2 = (bf16[128,512]{1,0:T(8,128)(2,1)S(1)}, bf16[128,512]{1,0:T(8,128)(2,1)S(1)}, u32[]{:S(2)}, u32[]{:S(2)}) collective-permute-start(bf16[128,512]{1,0:T(8,128)(2,1)S(1)} %collective-permute-done.refs_7_), channel_id=1, source_target_pairs={{0,4},{4,8},{8,12},{12,14},{14,10},{10,6},{6,2},{2,0},{1,5},{5,9},... | collective-permute-start | bytes 393224 | tf_op jit(solution)/shard_map/ppermute | solution.py:92
  17.0 7.5 %copy-start.3 = (bf16[128,512]{1,0:T(8,128)(2,1)}, bf16[128,512]{1,0:T(8,128)(2,1)S(1)}, u32[]{:S(2)}) copy-start(bf16[128,512]{1,0:T(8,128)(2,1)S(1)} %collective-permute-done.3.refs_2_) | copy-start | bytes 393220
  17.0 7.5 %copy-start.4 = (bf16[128,512]{1,0:T(8,128)(2,1)}, bf16[128,512]{1,0:T(8,128)(2,1)S(1)}, u32[]{:S(2)}) copy-start(bf16[128,512]{1,0:T(8,128)(2,1)S(1)} %collective-permute-done.2.refs_6_) | copy-start | bytes 393220
  17.0 7.5 %collective-permute-start.5 = (bf16[128,512]{1,0:T(8,128)(2,1)S(1)}, bf16[128,512]{1,0:T(8,128)(2,1)S(1)}, u32[]{:S(2)}, u32[]{:S(2)}) collective-permute-start(bf16[128,512]{1,0:T(8,128)(2,1)S(1)} %collective-permute-done.3.refs_2_), channel_id=1, source_target_pairs={{4,0},{8,4},{12,8},{14,12},{10,14},{6,10},{2,6},{0,2},{5,1},{9,5},... | collective-permute-start | bytes 393224 | tf_op jit(solution)/shard_map/ppermute | solution.py:94
  18.9 5.5 %collective-permute-start.4 = (bf16[128,512]{1,0:T(8,128)(2,1)S(1)}, bf16[128,512]{1,0:T(8,128)(2,1)S(1)}, u32[]{:S(2)}, u32[]{:S(2)}) collective-permute-start(bf16[128,512]{1,0:T(8,128)(2,1)S(1)} %collective-permute-done.2.refs_6_), channel_id=1, source_target_pairs={{0,4},{4,8},{8,12},{12,14},{14,10},{10,6},{6,2},{2,0},{1,5},{5,9},... | collective-permute-start | bytes 393224 | tf_op jit(solution)/shard_map/ppermute | solution.py:92
  24.4 7.4 %copy-start.5 = (bf16[128,512]{1,0:T(8,128)(2,1)}, bf16[128,512]{1,0:T(8,128)(2,1)S(1)}, u32[]{:S(2)}) copy-start(bf16[128,512]{1,0:T(8,128)(2,1)S(1)} %collective-permute-done.5.refs_3_) | copy-start | bytes 393220
  24.5 7.3 %copy-start.6 = (bf16[128,512]{1,0:T(8,128)(2,1)}, bf16[128,512]{1,0:T(8,128)(2,1)S(1)}, u32[]{:S(2)}) copy-start(bf16[128,512]{1,0:T(8,128)(2,1)S(1)} %collective-permute-done.4.refs_5_) | copy-start | bytes 393220
  24.5 7.3 %collective-permute-start.6 = (bf16[128,512]{1,0:T(8,128)(2,1)S(1)}, bf16[128,512]{1,0:T(8,128)(2,1)S(1)}, u32[]{:S(2)}, u32[]{:S(2)}) collective-permute-start(bf16[128,512]{1,0:T(8,128)(2,1)S(1)} %collective-permute-done.4.refs_5_), channel_id=1, source_target_pairs={{0,4},{4,8},{8,12},{12,14},{14,10},{10,6},{6,2},{2,0},{1,5},{5,9},... | collective-permute-start | bytes 393224 | tf_op jit(solution)/shard_map/ppermute | solution.py:92
  31.8 0.6 copy-start.7
  121.1 1.7 %collective-permute-start.7 = (f32[128,512]{1,0:T(8,128)}, f32[128,512]{1,0:T(8,128)S(1)}, u32[]{:S(2)}, u32[]{:S(2)}) collective-permute-start(f32[128,512]{1,0:T(8,128)} %get-tuple-element.30), channel_id=1, source_target_pairs={{0,1},{1,0},{2,3},{3,2},{4,5},{5,4},{6,7},{7,6},{8,9},{9,8},{10,11... | collective-permute-start | bytes 786440 | tf_op jit(solution)/shard_map/ppermute | solution.py:297

commit v7 on v4

--- a/solution.py
+++ b/solution.py
@@ -14,10 +14,11 @@
 LANES = 128
 PIECES = 4
 ROWS = 16
-TAPS = 4
-TILE = 512
+TAPS = 8
+TILE = 256
 GROUP = 8
-VMEM = 56 * 1024 * 1024
+EMBED_VMEM = 8 * 1024 * 1024
+VMEM = 28 * 1024 * 1024
 
 
 def embed_kernel(t_ref, off_ref, mask_ref, e_ref):
@@ -61,7 +62,7 @@
         ],
         out_specs=pl.BlockSpec((LE, ROWS, width), lambda i, j: (0, i, j)),
         out_shape=jax.ShapeDtypeStruct((LE, rows, channels), jnp.bfloat16),
-        compiler_params=pltpu.CompilerParams(vmem_limit_bytes=VMEM),
+        compiler_params=pltpu.CompilerParams(vmem_limit_bytes=EMBED_VMEM),
         cost_estimate=pl.CostEstimate(
             flops=20 * LE * rows * channels,
             bytes_accessed=2 * 2 * LE * rows * channels,
@@ -127,7 +128,6 @@
                         (8, LANES), jnp.float32
                     )
 
-    x_ref[:, (lags + LE) * n :, :] = jnp.zeros((width // LANES, 2 * TAPS * n, LANES), jnp.float32)
     size = GROUP * n
 
     def energy(g, carry):
@@ -166,26 +166,11 @@
     lax.fori_loop(0, lags // GROUP, norms, 0)
 
 
-def build(x_ref, n_ref, w_ref, n, tap0, m):
-    tiles = x_ref.shape[0]
-    size = 8 * n
-    for i in range(TILE // size):
-        row = m * TILE + i * size
-        rows = pl.ds(pl.multiple_of(row, size), size)
-        for w in range(tiles):
-            norm = n_ref[w, rows, :]
-            xs = x_ref[w, pl.ds(pl.multiple_of(row + tap0 * n, n), (TAPS + 7) * n), :]
-            for tap in range(TAPS):
-                value = (xs[tap * n : tap * n + size] * norm).astype(jnp.bfloat16)
-                w_ref[rows, (tap * tiles + w) * LANES : (tap * tiles + w + 1) * LANES] = value
-
-
 def correlate_kernel(n, steps, *refs):
     blocks = refs[:n]
     e_refs = refs[n : n + PIECES]
-    mine_ref, other_ref, acc_ref, turned_ref, x_ref, g_ref, n_ref, even_ref, odd_ref = refs[n + PIECES :]
+    mine_ref, other_ref, acc_ref, x_ref, g_ref, n_ref = refs[n + PIECES :]
     lags, width = blocks[0].shape
-    tiles = n * lags // TILE
     step = pl.program_id(0)
 
     @pl.when(step == 0)
@@ -193,46 +178,33 @@
         prepare(n, blocks, x_ref, g_ref, n_ref)
         acc_ref[...] = jnp.zeros_like(acc_ref)
 
-        def first(m, carry):
-            build(x_ref, n_ref, even_ref, n, 0, m)
-            return carry
-
-        lax.fori_loop(0, tiles, first, 0)
-
-    def advance(now_ref, later_ref, part, tap0):
+    def tile(m, carry):
+        rows = pl.ds(pl.multiple_of(m * TILE, TILE), TILE)
+        parts = []
+        for tap in range(TAPS):
+            first = pl.multiple_of(m * TILE + (step * TAPS + tap) * n, n)
+            for w in range(width // LANES):
+                value = x_ref[w, pl.ds(first, TILE), :] * n_ref[w, rows, :]
+                parts.append(value.astype(jnp.bfloat16))
+        windows = jnp.concatenate(parts, axis=1)
         weights = jnp.concatenate(
-            [
-                jnp.concatenate([e_ref[part * TAPS + tap] for e_ref in e_refs], axis=0)
-                for tap in range(TAPS)
-            ],
+            [jnp.concatenate([e_ref[tap] for e_ref in e_refs], axis=0) for tap in range(TAPS)],
             axis=1,
         )
-
-        def tile(m, carry):
-            rows = pl.ds(pl.multiple_of(m * TILE, TILE), TILE)
-            acc_ref[:, rows] += lax.dot_general(
-                weights,
-                now_ref[rows, :],
-                (((1,), (1,)), ((), ())),
-                preferred_element_type=jnp.float32,
-            )
-            build(x_ref, n_ref, later_ref, n, tap0, m)
-            return carry
-
-        lax.fori_loop(0, tiles, tile, 0)
-
-    advance(even_ref, odd_ref, 0, step * 2 * TAPS + TAPS)
-    advance(odd_ref, even_ref, 1, step * 2 * TAPS + 2 * TAPS)
+        acc_ref[rows, :] += lax.dot_general(
+            windows, weights, (((1,), (1,)), ((), ())), preferred_element_type=jnp.float32
+        )
+        return carry
+
+    lax.fori_loop(0, n * lags // TILE, tile, 0)
 
     @pl.when(step == steps - 1)
     def _():
-        for u in range(0, n * lags, LANES):
-            turned_ref[u : u + LANES, :] = acc_ref[:, u : u + LANES].T
         core = lax.axis_index("chan")
         half = n // 2
         for out_ref, first in ((mine_ref, core * half), (other_ref, (1 - core) * half)):
             for v in range(half):
-                value = turned_ref[pl.ds(first + v, lags, stride=n), :]
+                value = acc_ref[pl.ds(first + v, lags, stride=n), :]
                 out_ref[:, v * lags : (v + 1) * lags] = value.T
 
 
@@ -240,9 +212,9 @@
     n = len(blocks)
     lags, width = blocks[0].shape
     k = PIECES * pieces[0].shape[1]
-    steps = LE // (2 * TAPS)
+    steps = LE // TAPS
     whole = pl.BlockSpec(memory_space=pltpu.VMEM)
-    e_spec = pl.BlockSpec((2 * TAPS, k // PIECES, width), lambda i: (i, 0, 0))
+    e_spec = pl.BlockSpec((TAPS, k // PIECES, width), lambda i: (i, 0, 0))
     return pl.pallas_call(
         functools.partial(correlate_kernel, n, steps),
         grid=(steps,),
@@ -250,13 +222,10 @@
         out_specs=[whole, whole],
         out_shape=[jax.ShapeDtypeStruct((k, n * lags // 2), jnp.float32)] * 2,
         scratch_shapes=[
-            pltpu.VMEM((k, n * lags), jnp.float32),
             pltpu.VMEM((n * lags, k), jnp.float32),
-            pltpu.VMEM((width // LANES, (lags + LE + 2 * TAPS) * n, LANES), jnp.float32),
+            pltpu.VMEM((width // LANES, (lags + LE) * n, LANES), jnp.float32),
             pltpu.VMEM((width // LANES, (lags + LE) // GROUP, n, LANES), jnp.float32),
             pltpu.VMEM((width // LANES, lags * n, LANES), jnp.float32),
-            pltpu.VMEM((n * lags, TAPS * width), jnp.bfloat16),
-            pltpu.VMEM((n * lags, TAPS * width), jnp.bfloat16),
         ],
         compiler_params=pltpu.CompilerParams(vmem_limit_bytes=VMEM),
         cost_estimate=pl.CostEstimate(

time: 106 us -> 75.6 us (0.71)
  Pallas kernels: 90.9 us -> 50.5 us
  waiting for transfers between devices: 1.76 us -> 9 us
  local copies, waits for them, and re-layouts: 1.68 us -> 7.63 us
  starting transfers between devices: 9.31 us -> 7.43 us
    pallas_call x1, Pallas kernels: 69.5 us -> 40.6 us  [correlate(): pl.pallas_call(functools.partial(correlate_kernel, n, steps), grid=(steps...]
    pallas_call x4, Pallas kernels: 21.3 us -> 9.92 us  [embed(): pl.pallas_call(embed_kernel, grid=(steps, channels // width), in_specs=[p...]
    ppermute x4, waiting for transfers between devices: 0.01 us -> 6.58 us  [ring_gather(): a = lax.ppermute(a, 'blk', up)]
    unnamed x17 -> x7, local copies, waits for them, and re-layouts: 1.68 us -> 7.63 us
    ppermute x4, starting transfers between devices: 2.38 us -> 0.81 us  [ring_gather(): a = lax.ppermute(a, 'blk', up)]
  transfers between devices with their start and end apart: 8 -> 8, of which waited for: 1 -> 6; matrix products, arithmetic and copies ran while one was open for 0% -> 0% of each run, Pallas kernels for 20% -> 13%
where the time goes in v7:
time: 75.6 us; the launch traced here: 75.4 us
  Pallas kernels  50.5 us (67%)
  waiting for transfers between devices  9 us (12%)
  local copies, waits for them, and re-layouts  7.63 us (10%)
  starting transfers between devices  7.43 us (10%)
    pallas_call x1, Pallas kernels, correlate(): pl.pallas_call(functools.partial(correlate_kernel, n, steps), grid=(steps...  40.6 us
    pallas_call x4, Pallas kernels, embed(): pl.pallas_call(embed_kernel, grid=(steps, channels // width), in_specs=[p...  9.92 us
    unnamed x7, local copies, waits for them, and re-layouts  7.63 us
    ppermute x4, waiting for transfers between devices, ring_gather(): a = lax.ppermute(a, 'blk', up)  6.58 us
    ppermute x3, starting transfers between devices, ring_gather(): b = lax.ppermute(b, 'blk', down)  6.55 us
    ppermute x1, waiting for transfers between devices, per_device(): return mine + lax.ppermute(other, 'chan', [(0, 1), (1, 0)])  1.52 us
  transfers between devices with their start and end apart: 8, of which 6 were waited for; matrix products, arithmetic and copies ran while one was open for 0% of the time, Pallas kernels for 13%

profile of v7, /device:TPU:0, one launch (start us, length us, event | category | flops | bytes accessed | tf_op | source)
XLA Modules:
  0.0 75.4 jit_solution(16292278155575714725)
XLA Ops:
  0.0 1.0 %copy.5 = bf16[512,128]{0,1:T(8,128)(2,1)S(1)} copy(bf16[512,128]{1,0:T(8,128)(2,1)} %param.4) | data formatting | bytes 262144 | tf_op args[0]
  1.0 3.0 %collective-permute-start.1 = (bf16[128,512]{1,0:T(8,128)(2,1)S(1)}, bf16[128,512]{1,0:T(8,128)(2,1)S(1)}, u32[]{:S(2)}, u32[]{:S(2)}) collective-permute-start(bf16[128,512]{1,0:T(8,128)(2,1)S(1)} %bitcast.1), channel_id=1, source_target_pairs={{4,0},{8,4},{12,8},{14,12},{10,14},{6,10},{2,6},{0,2},{5,1},{9,5},... | collective-permute-start | bytes 393224 | tf_op jit(solution)/shard_map/ppermute | solution.py:95
  4.0 0.1 collective-permute-start
  4.2 4.7 %copy-done = bf16[100,128,512]{2,1,0:T(8,128)(2,1)S(1)} copy-done((bf16[100,128,512]{2,1,0:T(8,128)(2,1)S(1)}, bf16[100,128,512]{2,1,0:T(8,128)(2,1)}, u32[]{:S(2)}) %copy-start) | copy-done | bytes 13107224
  8.9 0.9 %copy-done.1 = s32[128,512]{1,0:T(8,128)S(1)} copy-done((s32[128,512]{1,0:T(8,128)S(1)}, s32[128,512]{1,0:T(8,128)}, u32[]{:S(2)}) %copy-start.1) | copy-done | bytes 262168
  9.8 0.9 %copy-done.2 = s32[128,512]{1,0:T(8,128)S(1)} copy-done((s32[128,512]{1,0:T(8,128)S(1)}, s32[128,512]{1,0:T(8,128)}, u32[]{:S(2)}) %copy-start.2) | copy-done | bytes 262168
  10.8 2.5 %shard_map.46.refs_8_ = bf16[104,32,512]{2,1,0:T(8,128)(2,1)S(1)} custom-call(bf16[100,128,512]{2,1,0:T(8,128)(2,1)S(1)} %copy-done, s32[128,512]{1,0:T(8,128)S(1)} %copy-done.1, s32[128,512]{1,0:T(8,128)S(1)} %copy-done.2), custom_call_target="tpu_custom_call" | custom-call | flops 34078720 | bytes 6815744 | tf_op jit(solution)/shard_map/pallas_call | solution.py:55
  13.3 2.0 %collective-permute-start.3 = (bf16[128,512]{1,0:T(8,128)(2,1)S(1)}, bf16[128,512]{1,0:T(8,128)(2,1)S(1)}, u32[]{:S(2)}, u32[]{:S(2)}) collective-permute-start(bf16[128,512]{1,0:T(8,128)(2,1)S(1)} %collective-permute-done.1.refs_1_), channel_id=1, source_target_pairs={{4,0},{8,4},{12,8},{14,12},{10,14},{6,10},{2,6},{0,2},{5,1},{9,5},... | collective-permute-start | bytes 393224 | tf_op jit(solution)/shard_map/ppermute | solution.py:95
  15.2 0.1 collective-permute-start.2
  15.4 2.5 %shard_map.47.refs_9_ = bf16[104,32,512]{2,1,0:T(8,128)(2,1)S(1)} custom-call(bf16[100,128,512]{2,1,0:T(8,128)(2,1)S(1)} %copy-done, s32[128,512]{1,0:T(8,128)S(1)} %copy-done.1, s32[128,512]{1,0:T(8,128)S(1)} %copy-done.2), custom_call_target="tpu_custom_call" | custom-call | flops 34078720 | bytes 6815744 | tf_op jit(solution)/shard_map/pallas_call | solution.py:55
  17.9 0.4 collective-permute-done.3.refs_2_
  18.3 1.9 %collective-permute-done.2.refs_6_ = bf16[128,512]{1,0:T(8,128)(2,1)S(1)} collective-permute-done((bf16[128,512]{1,0:T(8,128)(2,1)S(1)}, bf16[128,512]{1,0:T(8,128)(2,1)S(1)}, u32[]{:S(2)}, u32[]{:S(2)}) %collective-permute-start.2) | collective-permute-done | bytes 131104 | tf_op jit(solution)/shard_map/ppermute | solution.py:93
  20.2 1.6 %collective-permute-start.5 = (bf16[128,512]{1,0:T(8,128)(2,1)S(1)}, bf16[128,512]{1,0:T(8,128)(2,1)S(1)}, u32[]{:S(2)}, u32[]{:S(2)}) collective-permute-start(bf16[128,512]{1,0:T(8,128)(2,1)S(1)} %collective-permute-done.3.refs_2_), channel_id=1, source_target_pairs={{4,0},{8,4},{12,8},{14,12},{10,14},{6,10},{2,6},{0,2},{5,1},{9,5},... | collective-permute-start | bytes 393224 | tf_op jit(solution)/shard_map/ppermute | solution.py:95
  21.8 0.4 collective-permute-start.4
  22.2 2.5 %shard_map.48.refs_10_ = bf16[104,32,512]{2,1,0:T(8,128)(2,1)S(1)} custom-call(bf16[100,128,512]{2,1,0:T(8,128)(2,1)S(1)} %copy-done, s32[128,512]{1,0:T(8,128)S(1)} %copy-done.1, s32[128,512]{1,0:T(8,128)S(1)} %copy-done.2), custom_call_target="tpu_custom_call" | custom-call | flops 34078720 | bytes 6815744 | tf_op jit(solution)/shard_map/pallas_call | solution.py:55
  24.7 0.4 collective-permute-done.5.refs_3_
  25.2 2.3 %collective-permute-done.4.refs_5_ = bf16[128,512]{1,0:T(8,128)(2,1)S(1)} collective-permute-done((bf16[128,512]{1,0:T(8,128)(2,1)S(1)}, bf16[128,512]{1,0:T(8,128)(2,1)S(1)}, u32[]{:S(2)}, u32[]{:S(2)}) %collective-permute-start.4) | collective-permute-done | bytes 131104 | tf_op jit(solution)/shard_map/ppermute | solution.py:93
  27.5 0.1 collective-permute-start.6
  27.6 2.5 %shard_map.49.refs_11_ = bf16[104,32,512]{2,1,0:T(8,128)(2,1)S(1)} custom-call(bf16[100,128,512]{2,1,0:T(8,128)(2,1)S(1)} %copy-done, s32[128,512]{1,0:T(8,128)S(1)} %copy-done.1, s32[128,512]{1,0:T(8,128)S(1)} %copy-done.2), custom_call_target="tpu_custom_call" | custom-call | flops 34078720 | bytes 6815744 | tf_op jit(solution)/shard_map/pallas_call | solution.py:55
  30.1 2.4 %collective-permute-done.6.refs_4_ = bf16[128,512]{1,0:T(8,128)(2,1)S(1)} collective-permute-done((bf16[128,512]{1,0:T(8,128)(2,1)S(1)}, bf16[128,512]{1,0:T(8,128)(2,1)S(1)}, u32[]{:S(2)}, u32[]{:S(2)}) %collective-permute-start.6) | collective-permute-done | bytes 131104 | tf_op jit(solution)/shard_map/ppermute | solution.py:93
  32.5 40.6 %shard_map.50 = (f32[128,512]{1,0:T(8,128)S(1)}, f32[128,512]{1,0:T(8,128)S(1)}) custom-call(bf16[128,512]{1,0:T(8,128)(2,1)S(1)} %bitcast.3, bf16[128,512]{1,0:T(8,128)(2,1)S(1)} %collective-permute-done.1.refs_1_, bf16[128,512]{1,0:T(8,128)(2,1)S(1)} %collective-permute-done.3.refs_2_, bf16[128,512]{1,0:T(8,128)(2,1)S(1)} %collective-permute-done.5.refs_3_, ...), custom_call_target="tpu_custom_call" | custom-call | flops 13958643712 | bytes 13631488 | tf_op jit(solution)/shard_map/pallas_call | solution.py:218
  73.0 0.1 collective-permute-start.7
  73.1 1.5 %collective-permute-done.7 = f32[128,512]{1,0:T(8,128)S(1)} collective-permute-done((f32[128,512]{1,0:T(8,128)S(1)}, f32[128,512]{1,0:T(8,128)S(1)}, u32[]{:S(2)}, u32[]{:S(2)}) %collective-permute-start.7) | collective-permute-done | bytes 262176 | tf_op jit(solution)/shard_map/ppermute | solution.py:244
  74.6 0.7 add.3
  (5 shorter events, 0.0 us)
Async XLA Ops:
  1.0 12.3 %collective-permute-start.1 = (bf16[128,512]{1,0:T(8,128)(2,1)S(1)}, bf16[128,512]{1,0:T(8,128)(2,1)S(1)}, u32[]{:S(2)}, u32[]{:S(2)}) collective-permute-start(bf16[128,512]{1,0:T(8,128)(2,1)S(1)} %bitcast.1), channel_id=1, source_target_pairs={{4,0},{8,4},{12,8},{14,12},{10,14},{6,10},{2,6},{0,2},{5,1},{9,5},... | collective-permute-start | bytes 393224 | tf_op jit(solution)/shard_map/ppermute | solution.py:95
  4.0 9.2 %collective-permute-start = (bf16[128,512]{1,0:T(8,128)(2,1)S(1)}, bf16[128,512]{1,0:T(8,128)(2,1)S(1)}, u32[]{:S(2)}, u32[]{:S(2)}) collective-permute-start(bf16[128,512]{1,0:T(8,128)(2,1)S(1)} %bitcast.2), channel_id=1, source_target_pairs={{0,4},{4,8},{8,12},{12,14},{14,10},{10,6},{6,2},{2,0},{1,5},{5,9},... | collective-permute-start | bytes 393224 | tf_op jit(solution)/shard_map/ppermute | solution.py:93
  4.2 4.7 %copy-start = (bf16[100,128,512]{2,1,0:T(8,128)(2,1)S(1)}, bf16[100,128,512]{2,1,0:T(8,128)(2,1)}, u32[]{:S(2)}) copy-start(bf16[100,128,512]{2,1,0:T(8,128)(2,1)} %t_ref.7) | copy-start | bytes 39321604
  8.9 0.9 %copy-start.1 = (s32[128,512]{1,0:T(8,128)S(1)}, s32[128,512]{1,0:T(8,128)}, u32[]{:S(2)}) copy-start(s32[128,512]{1,0:T(8,128)} %off_ref.7) | copy-start | bytes 786436
  9.8 0.9 %copy-start.2 = (s32[128,512]{1,0:T(8,128)S(1)}, s32[128,512]{1,0:T(8,128)}, u32[]{:S(2)}) copy-start(s32[128,512]{1,0:T(8,128)} %mask_ref.7) | copy-start | bytes 786436
  13.3 5.0 %collective-permute-start.3 = (bf16[128,512]{1,0:T(8,128)(2,1)S(1)}, bf16[128,512]{1,0:T(8,128)(2,1)S(1)}, u32[]{:S(2)}, u32[]{:S(2)}) collective-permute-start(bf16[128,512]{1,0:T(8,128)(2,1)S(1)} %collective-permute-done.1.refs_1_), channel_id=1, source_target_pairs={{4,0},{8,4},{12,8},{14,12},{10,14},{6,10},{2,6},{0,2},{5,1},{9,5},... | collective-permute-start | bytes 393224 | tf_op jit(solution)/shard_map/ppermute | solution.py:95
  15.2 5.0 %collective-permute-start.2 = (bf16[128,512]{1,0:T(8,128)(2,1)S(1)}, bf16[128,512]{1,0:T(8,128)(2,1)S(1)}, u32[]{:S(2)}, u32[]{:S(2)}) collective-permute-start(bf16[128,512]{1,0:T(8,128)(2,1)S(1)} %collective-permute-done.refs_7_), channel_id=1, source_target_pairs={{0,4},{4,8},{8,12},{12,14},{14,10},{10,6},{6,2},{2,0},{1,5},{5,9},... | collective-permute-start | bytes 393224 | tf_op jit(solution)/shard_map/ppermute | solution.py:93
  20.2 5.0 %collective-permute-start.5 = (bf16[128,512]{1,0:T(8,128)(2,1)S(1)}, bf16[128,512]{1,0:T(8,128)(2,1)S(1)}, u32[]{:S(2)}, u32[]{:S(2)}) collective-permute-start(bf16[128,512]{1,0:T(8,128)(2,1)S(1)} %collective-permute-done.3.refs_2_), channel_id=1, source_target_pairs={{4,0},{8,4},{12,8},{14,12},{10,14},{6,10},{2,6},{0,2},{5,1},{9,5},... | collective-permute-start | bytes 393224 | tf_op jit(solution)/shard_map/ppermute | solution.py:95
  21.8 5.7 %collective-permute-start.4 = (bf16[128,512]{1,0:T(8,128)(2,1)S(1)}, bf16[128,512]{1,0:T(8,128)(2,1)S(1)}, u32[]{:S(2)}, u32[]{:S(2)}) collective-permute-start(bf16[128,512]{1,0:T(8,128)(2,1)S(1)} %collective-permute-done.2.refs_6_), channel_id=1, source_target_pairs={{0,4},{4,8},{8,12},{12,14},{14,10},{10,6},{6,2},{2,0},{1,5},{5,9},... | collective-permute-start | bytes 393224 | tf_op jit(solution)/shard_map/ppermute | solution.py:93
  27.5 5.0 %collective-permute-start.6 = (bf16[128,512]{1,0:T(8,128)(2,1)S(1)}, bf16[128,512]{1,0:T(8,128)(2,1)S(1)}, u32[]{:S(2)}, u32[]{:S(2)}) collective-permute-start(bf16[128,512]{1,0:T(8,128)(2,1)S(1)} %collective-permute-done.4.refs_5_), channel_id=1, source_target_pairs={{0,4},{4,8},{8,12},{12,14},{14,10},{10,6},{6,2},{2,0},{1,5},{5,9},... | collective-permute-start | bytes 393224 | tf_op jit(solution)/shard_map/ppermute | solution.py:93
  73.0 1.6 %collective-permute-start.7 = (f32[128,512]{1,0:T(8,128)S(1)}, f32[128,512]{1,0:T(8,128)S(1)}, u32[]{:S(2)}, u32[]{:S(2)}) collective-permute-start(f32[128,512]{1,0:T(8,128)S(1)} %get-tuple-element.30), channel_id=1, source_target_pairs={{0,1},{1,0},{2,3},{3,2},{4,5},{5,4},{6,7},{7,6},{8,9},{9,8},{10,11... | collective-permute-start | bytes 786440 | tf_op jit(solution)/shard_map/ppermute | solution.py:244

commit v8 on v7

--- a/solution.py
+++ b/solution.py
@@ -15,22 +15,22 @@
 PIECES = 4
 ROWS = 16
 TAPS = 8
-TILE = 256
+TILE = 512
 GROUP = 8
 EMBED_VMEM = 8 * 1024 * 1024
 VMEM = 28 * 1024 * 1024
 
 
-def embed_kernel(t_ref, off_ref, mask_ref, e_ref):
-    rows, cols = off_ref.shape
+def embed_kernel(t_ref, place_ref, e_ref):
+    rows, cols = place_ref.shape
     for w in range(cols // LANES):
         lanes = slice(w * LANES, (w + 1) * LANES)
         total = jnp.zeros((rows, LANES), jnp.float32)
         for l in range(L):
             v = t_ref[l, :, lanes].astype(jnp.float32)
             total = total + v * v
-        scale = lax.rsqrt(total / L + EPS) * mask_ref[:, lanes].astype(jnp.float32) / L
-        off = off_ref[:, lanes]
+        scale = lax.rsqrt(total / L + EPS) * (place_ref[:, lanes] >> 3).astype(jnp.float32) / L
+        off = place_ref[:, lanes] & 7
         odd = ((off & 1) == 1).astype(jnp.bfloat16) > 0
         high = (off >= 2).astype(jnp.bfloat16) > 0
         full = (off == SPAN).astype(jnp.bfloat16) > 0
@@ -46,8 +46,8 @@
             moved = moved[1:] + [now]
 
 
-def embed(templates, offsets, masks, piece):
-    k, channels = offsets.shape
+def embed(templates, places, piece):
+    k, channels = places.shape
     rows = k // PIECES
     steps = rows // ROWS
     first = piece * steps
@@ -58,7 +58,6 @@
         in_specs=[
             pl.BlockSpec((L, ROWS, width), lambda i, j: (0, first + i, j)),
             pl.BlockSpec((ROWS, width), lambda i, j: (first + i, j)),
-            pl.BlockSpec((ROWS, width), lambda i, j: (first + i, j)),
         ],
         out_specs=pl.BlockSpec((LE, ROWS, width), lambda i, j: (0, i, j)),
         out_shape=jax.ShapeDtypeStruct((LE, rows, channels), jnp.bfloat16),
@@ -68,7 +67,7 @@
             bytes_accessed=2 * 2 * LE * rows * channels,
             transcendentals=0,
         ),
-    )(templates, offsets, masks)
+    )(templates, places)
 
 
 def ring_position(b, n):
@@ -93,8 +92,9 @@
         a = lax.ppermute(a, "blk", up)
         if step < n // 2:
             b = lax.ppermute(b, "blk", down)
-        if step <= PIECES:
-            done.append(beside(step - 1))
+        last = step == n // 2
+        while step > 1 and len(done) < (PIECES if last else min(step - 1, PIECES)):
+            done.append(beside(len(done)))
             a, b, done[-1] = lax.optimization_barrier((a, b, done[-1]))
         blocks[n - step] = a
         if step < n // 2:
@@ -237,9 +237,8 @@
 
 
 def per_device(n, records, templates, offsets, masks):
-    blocks, pieces = ring_gather(
-        records.T, n, lambda piece: embed(templates, offsets, masks, piece)
-    )
+    places = offsets + 8 * masks
+    blocks, pieces = ring_gather(records.T, n, lambda piece: embed(templates, places, piece))
     mine, other = correlate(blocks, pieces)
     return mine + lax.ppermute(other, "chan", [(0, 1), (1, 0)])
 

time: 75.6 us -> 68.8 us (0.910)
  Pallas kernels: 50.5 us -> 46.4 us
  local copies, waits for them, and re-layouts: 7.63 us -> 5.72 us
  waiting for transfers between devices: 9 us -> 7.15 us
  other arithmetic: 0.74 us -> 1.81 us
    ppermute x4, starting transfers between devices: 0.81 us -> 5.36 us  [ring_gather(): a = lax.ppermute(a, 'blk', up)]
    pallas_call x1, Pallas kernels: 40.6 us -> 36 us  [correlate(): pl.pallas_call(functools.partial(correlate_kernel, n, steps), grid=(steps...]
    ppermute x3, starting transfers between devices: 6.55 us -> 2.03 us  [ring_gather(): b = lax.ppermute(b, 'blk', down)]
    unnamed x7 -> x3, local copies, waits for them, and re-layouts: 7.63 us -> 5.72 us
    ppermute x4, waiting for transfers between devices: 6.58 us -> 5.28 us  [ring_gather(): a = lax.ppermute(a, 'blk', up)]
    add x0 -> x1, other arithmetic: none -> 1.06 us  [per_device(): places = offsets + 8 * masks]
  transfers between devices with their start and end apart: 8 -> 8, of which waited for: 6 -> 4; matrix products, arithmetic and copies ran while one was open for 0% -> 2% of each run, Pallas kernels for 13% -> 15%
where the time goes in v8:
time: 68.8 us; the launch traced here: 68.6 us
  Pallas kernels  46.4 us (67%)
  starting transfers between devices  7.46 us (11%)
  waiting for transfers between devices  7.15 us (10%)
  local copies, waits for them, and re-layouts  5.72 us (8%)
  other arithmetic  1.81 us (3%)
    pallas_call x1, Pallas kernels, correlate(): pl.pallas_call(functools.partial(correlate_kernel, n, steps), grid=(steps...  36 us
    pallas_call x4, Pallas kernels, embed(): pl.pallas_call(embed_kernel, grid=(steps, channels // width), in_specs=[p...  10.3 us
    unnamed x3, local copies, waits for them, and re-layouts  5.72 us
    ppermute x4, starting transfers between devices, ring_gather(): a = lax.ppermute(a, 'blk', up)  5.36 us
    ppermute x4, waiting for transfers between devices, ring_gather(): a = lax.ppermute(a, 'blk', up)  5.28 us
    ppermute x3, starting transfers between devices, ring_gather(): b = lax.ppermute(b, 'blk', down)  2.03 us
    ppermute x1, waiting for transfers between devices, per_device(): return mine + lax.ppermute(other, 'chan', [(0, 1), (1, 0)])  1.52 us
  transfers between devices with their start and end apart: 8, of which 4 were waited for; matrix products, arithmetic and copies ran while one was open for 2% of the time, Pallas kernels for 15%

profile of v8, /device:TPU:0, one launch (start us, length us, event | category | flops | bytes accessed | tf_op | source)
XLA Modules:
  0.0 68.6 jit_solution(239333202486345390)
XLA Ops:
  0.0 1.0 %copy.5 = bf16[512,128]{0,1:T(8,128)(2,1)S(1)} copy(bf16[512,128]{1,0:T(8,128)(2,1)} %param.4) | data formatting | bytes 262144 | tf_op args[0]
  1.0 3.1 %collective-permute-start.1 = (bf16[128,512]{1,0:T(8,128)(2,1)S(1)}, bf16[128,512]{1,0:T(8,128)(2,1)S(1)}, u32[]{:S(2)}, u32[]{:S(2)}) collective-permute-start(bf16[128,512]{1,0:T(8,128)(2,1)S(1)} %bitcast.1), channel_id=1, source_target_pairs={{0,4},{4,8},{8,12},{12,14},{14,10},{10,6},{6,2},{2,0},{1,5},{5,9},... | collective-permute-start | bytes 393224 | tf_op jit(solution)/shard_map/ppermute | solution.py:92
  4.1 0.0 collective-permute-start
  4.1 3.4 %collective-permute-done.1.refs_7_ = bf16[128,512]{1,0:T(8,128)(2,1)S(1)} collective-permute-done((bf16[128,512]{1,0:T(8,128)(2,1)S(1)}, bf16[128,512]{1,0:T(8,128)(2,1)S(1)}, u32[]{:S(2)}, u32[]{:S(2)}) %collective-permute-start.1) | collective-permute-done | bytes 131104 | tf_op jit(solution)/shard_map/ppermute | solution.py:92
  7.5 1.8 %collective-permute-start.2 = (bf16[128,512]{1,0:T(8,128)(2,1)S(1)}, bf16[128,512]{1,0:T(8,128)(2,1)S(1)}, u32[]{:S(2)}, u32[]{:S(2)}) collective-permute-start(bf16[128,512]{1,0:T(8,128)(2,1)S(1)} %collective-permute-done.1.refs_7_), channel_id=1, source_target_pairs={{0,4},{4,8},{8,12},{12,14},{14,10},{10,6},{6,2},{2,0},{1,5},{5,9},... | collective-permute-start | bytes 393224 | tf_op jit(solution)/shard_map/ppermute | solution.py:92
  9.3 0.0 collective-permute-done.refs_1_
  9.3 0.2 collective-permute-start.3
  9.6 1.1 %multiply_add_fusion.place_ref = s32[128,512]{1,0:T(8,128)S(1)} fusion(s32[128,512]{1,0:T(8,128)} %param.6, s32[128,512]{1,0:T(8,128)} %param.7), kind=kLoop, calls=%fused_computation | loop fusion | flops 131072 | bytes 786432 | tf_op jit(solution)/shard_map/add | solution.py:240
  10.6 0.0 copy-start
  10.6 4.7 %copy-done = bf16[100,128,512]{2,1,0:T(8,128)(2,1)S(1)} copy-done((bf16[100,128,512]{2,1,0:T(8,128)(2,1)S(1)}, bf16[100,128,512]{2,1,0:T(8,128)(2,1)}, u32[]{:S(2)}) %copy-start) | copy-done | bytes 13107224
  15.4 2.6 %shard_map.46.refs_8_ = bf16[104,32,512]{2,1,0:T(8,128)(2,1)S(1)} custom-call(bf16[100,128,512]{2,1,0:T(8,128)(2,1)S(1)} %copy-done, s32[128,512]{1,0:T(8,128)S(1)} %multiply_add_fusion.place_ref), custom_call_target="tpu_custom_call" | custom-call | flops 34078720 | bytes 6815744 | tf_op jit(solution)/shard_map/pallas_call | solution.py:55
  18.0 1.8 %collective-permute-start.5 = (bf16[128,512]{1,0:T(8,128)(2,1)S(1)}, bf16[128,512]{1,0:T(8,128)(2,1)S(1)}, u32[]{:S(2)}, u32[]{:S(2)}) collective-permute-start(bf16[128,512]{1,0:T(8,128)(2,1)S(1)} %collective-permute-done.3.refs_2_), channel_id=1, source_target_pairs={{4,0},{8,4},{12,8},{14,12},{10,14},{6,10},{2,6},{0,2},{5,1},{9,5},... | collective-permute-start | bytes 393224 | tf_op jit(solution)/shard_map/ppermute | solution.py:94
  19.7 0.3 collective-permute-start.4
  20.0 2.6 %shard_map.47.refs_9_ = bf16[104,32,512]{2,1,0:T(8,128)(2,1)S(1)} custom-call(bf16[100,128,512]{2,1,0:T(8,128)(2,1)S(1)} %copy-done, s32[128,512]{1,0:T(8,128)S(1)} %multiply_add_fusion.place_ref), custom_call_target="tpu_custom_call" | custom-call | flops 34078720 | bytes 6815744 | tf_op jit(solution)/shard_map/pallas_call | solution.py:55
  22.6 0.3 collective-permute-done.5.refs_3_
  23.0 1.8 %collective-permute-done.4.refs_5_ = bf16[128,512]{1,0:T(8,128)(2,1)S(1)} collective-permute-done((bf16[128,512]{1,0:T(8,128)(2,1)S(1)}, bf16[128,512]{1,0:T(8,128)(2,1)S(1)}, u32[]{:S(2)}, u32[]{:S(2)}) %collective-permute-start.4) | collective-permute-done | bytes 131104 | tf_op jit(solution)/shard_map/ppermute | solution.py:92
  24.8 0.2 collective-permute-start.6
  25.0 2.6 %shard_map.49.refs_11_ = bf16[104,32,512]{2,1,0:T(8,128)(2,1)S(1)} custom-call(bf16[100,128,512]{2,1,0:T(8,128)(2,1)S(1)} %copy-done, s32[128,512]{1,0:T(8,128)S(1)} %multiply_add_fusion.place_ref), custom_call_target="tpu_custom_call" | custom-call | flops 34078720 | bytes 6815744 | tf_op jit(solution)/shard_map/pallas_call | solution.py:55
  27.6 2.6 %shard_map.48.refs_10_ = bf16[104,32,512]{2,1,0:T(8,128)(2,1)S(1)} custom-call(bf16[100,128,512]{2,1,0:T(8,128)(2,1)S(1)} %copy-done, s32[128,512]{1,0:T(8,128)S(1)} %multiply_add_fusion.place_ref), custom_call_target="tpu_custom_call" | custom-call | flops 34078720 | bytes 6815744 | tf_op jit(solution)/shard_map/pallas_call | solution.py:55
  30.2 0.0 collective-permute-done.6.refs_4_
  30.2 36.0 %shard_map.50 = (f32[128,512]{1,0:T(8,128)S(1)}, f32[128,512]{1,0:T(8,128)S(1)}) custom-call(bf16[128,512]{1,0:T(8,128)(2,1)S(1)} %bitcast.3, bf16[128,512]{1,0:T(8,128)(2,1)S(1)} %collective-permute-done.refs_1_, bf16[128,512]{1,0:T(8,128)(2,1)S(1)} %collective-permute-done.3.refs_2_, bf16[128,512]{1,0:T(8,128)(2,1)S(1)} %collective-permute-done.5.refs_3_, ...), custom_call_target="tpu_custom_call" | custom-call | flops 13958643712 | bytes 13631488 | tf_op jit(solution)/shard_map/pallas_call | solution.py:218
  66.3 0.1 collective-permute-start.7
  66.3 1.5 %collective-permute-done.7 = f32[128,512]{1,0:T(8,128)S(1)} collective-permute-done((f32[128,512]{1,0:T(8,128)S(1)}, f32[128,512]{1,0:T(8,128)S(1)}, u32[]{:S(2)}, u32[]{:S(2)}) %collective-permute-start.7) | collective-permute-done | bytes 262176 | tf_op jit(solution)/shard_map/ppermute | solution.py:243
  67.9 0.7 %add.7 = f32[128,512]{1,0:T(8,128)} add(f32[128,512]{1,0:T(8,128)S(1)} %get-tuple-element.27, f32[128,512]{1,0:T(8,128)S(1)} %collective-permute-done.7) | non-fusion elementwise | flops 65536 | bytes 786432 | tf_op jit(solution)/shard_map/add | solution.py:243
  (2 shorter events, 0.0 us)
Async XLA Ops:
  1.0 6.5 %collective-permute-start.1 = (bf16[128,512]{1,0:T(8,128)(2,1)S(1)}, bf16[128,512]{1,0:T(8,128)(2,1)S(1)}, u32[]{:S(2)}, u32[]{:S(2)}) collective-permute-start(bf16[128,512]{1,0:T(8,128)(2,1)S(1)} %bitcast.1), channel_id=1, source_target_pairs={{0,4},{4,8},{8,12},{12,14},{14,10},{10,6},{6,2},{2,0},{1,5},{5,9},... | collective-permute-start | bytes 393224 | tf_op jit(solution)/shard_map/ppermute | solution.py:92
  4.1 5.2 %collective-permute-start = (bf16[128,512]{1,0:T(8,128)(2,1)S(1)}, bf16[128,512]{1,0:T(8,128)(2,1)S(1)}, u32[]{:S(2)}, u32[]{:S(2)}) collective-permute-start(bf16[128,512]{1,0:T(8,128)(2,1)S(1)} %bitcast.2), channel_id=1, source_target_pairs={{4,0},{8,4},{12,8},{14,12},{10,14},{6,10},{2,6},{0,2},{5,1},{9,5},... | collective-permute-start | bytes 393224 | tf_op jit(solution)/shard_map/ppermute | solution.py:94
  7.5 10.4 %collective-permute-start.2 = (bf16[128,512]{1,0:T(8,128)(2,1)S(1)}, bf16[128,512]{1,0:T(8,128)(2,1)S(1)}, u32[]{:S(2)}, u32[]{:S(2)}) collective-permute-start(bf16[128,512]{1,0:T(8,128)(2,1)S(1)} %collective-permute-done.1.refs_7_), channel_id=1, source_target_pairs={{0,4},{4,8},{8,12},{12,14},{14,10},{10,6},{6,2},{2,0},{1,5},{5,9},... | collective-permute-start | bytes 393224 | tf_op jit(solution)/shard_map/ppermute | solution.py:92
  9.3 8.6 %collective-permute-start.3 = (bf16[128,512]{1,0:T(8,128)(2,1)S(1)}, bf16[128,512]{1,0:T(8,128)(2,1)S(1)}, u32[]{:S(2)}, u32[]{:S(2)}) collective-permute-start(bf16[128,512]{1,0:T(8,128)(2,1)S(1)} %collective-permute-done.refs_1_), channel_id=1, source_target_pairs={{4,0},{8,4},{12,8},{14,12},{10,14},{6,10},{2,6},{0,2},{5,1},{9,5},... | collective-permute-start | bytes 393224 | tf_op jit(solution)/shard_map/ppermute | solution.py:94
  10.6 4.7 %copy-start = (bf16[100,128,512]{2,1,0:T(8,128)(2,1)S(1)}, bf16[100,128,512]{2,1,0:T(8,128)(2,1)}, u32[]{:S(2)}) copy-start(bf16[100,128,512]{2,1,0:T(8,128)(2,1)} %t_ref.7) | copy-start | bytes 39321604
  18.0 5.0 %collective-permute-start.5 = (bf16[128,512]{1,0:T(8,128)(2,1)S(1)}, bf16[128,512]{1,0:T(8,128)(2,1)S(1)}, u32[]{:S(2)}, u32[]{:S(2)}) collective-permute-start(bf16[128,512]{1,0:T(8,128)(2,1)S(1)} %collective-permute-done.3.refs_2_), channel_id=1, source_target_pairs={{4,0},{8,4},{12,8},{14,12},{10,14},{6,10},{2,6},{0,2},{5,1},{9,5},... | collective-permute-start | bytes 393224 | tf_op jit(solution)/shard_map/ppermute | solution.py:94
  19.7 5.1 %collective-permute-start.4 = (bf16[128,512]{1,0:T(8,128)(2,1)S(1)}, bf16[128,512]{1,0:T(8,128)(2,1)S(1)}, u32[]{:S(2)}, u32[]{:S(2)}) collective-permute-start(bf16[128,512]{1,0:T(8,128)(2,1)S(1)} %collective-permute-done.2.refs_6_), channel_id=1, source_target_pairs={{0,4},{4,8},{8,12},{12,14},{14,10},{10,6},{6,2},{2,0},{1,5},{5,9},... | collective-permute-start | bytes 393224 | tf_op jit(solution)/shard_map/ppermute | solution.py:92
  24.8 5.4 %collective-permute-start.6 = (bf16[128,512]{1,0:T(8,128)(2,1)S(1)}, bf16[128,512]{1,0:T(8,128)(2,1)S(1)}, u32[]{:S(2)}, u32[]{:S(2)}) collective-permute-start(bf16[128,512]{1,0:T(8,128)(2,1)S(1)} %collective-permute-done.4.refs_5_), channel_id=1, source_target_pairs={{0,4},{4,8},{8,12},{12,14},{14,10},{10,6},{6,2},{2,0},{1,5},{5,9},... | collective-permute-start | bytes 393224 | tf_op jit(solution)/shard_map/ppermute | solution.py:92
  66.3 1.6 %collective-permute-start.7 = (f32[128,512]{1,0:T(8,128)S(1)}, f32[128,512]{1,0:T(8,128)S(1)}, u32[]{:S(2)}, u32[]{:S(2)}) collective-permute-start(f32[128,512]{1,0:T(8,128)S(1)} %get-tuple-element.28), channel_id=1, source_target_pairs={{0,1},{1,0},{2,3},{3,2},{4,5},{5,4},{6,7},{7,6},{8,9},{9,8},{10,11... | collective-permute-start | bytes 786440 | tf_op jit(solution)/shard_map/ppermute | solution.py:243

commit v9 on v8

--- a/solution.py
+++ b/solution.py
@@ -14,10 +14,10 @@
 LANES = 128
 PIECES = 4
 ROWS = 16
-TAPS = 8
-TILE = 512
+TAPS = 4
+TILE = 1024
 GROUP = 8
-EMBED_VMEM = 8 * 1024 * 1024
+EMBED_VMEM = 44 * 1024 * 1024
 VMEM = 28 * 1024 * 1024
 
 
@@ -92,9 +92,8 @@
         a = lax.ppermute(a, "blk", up)
         if step < n // 2:
             b = lax.ppermute(b, "blk", down)
-        last = step == n // 2
-        while step > 1 and len(done) < (PIECES if last else min(step - 1, PIECES)):
-            done.append(beside(len(done)))
+        if step <= PIECES:
+            done.append(beside(step - 1))
             a, b, done[-1] = lax.optimization_barrier((a, b, done[-1]))
         blocks[n - step] = a
         if step < n // 2:

time: 68.8 us -> 67 us (0.974)
  Pallas kernels: 46.4 us -> 52.8 us
  local copies, waits for them, and re-layouts: 5.72 us -> 1 us
  waiting for transfers between devices: 7.15 us -> 2.58 us
  starting transfers between devices: 7.46 us -> 8.36 us
    pallas_call x4, Pallas kernels: 10.3 us -> 16.6 us  [embed(): pl.pallas_call(embed_kernel, grid=(steps, channels // width), in_specs=[p...]
    unnamed x3 -> x1, local copies, waits for them, and re-layouts: 5.72 us -> 1 us
    ppermute x3, starting transfers between devices: 2.03 us -> 6.55 us  [ring_gather(): b = lax.ppermute(b, 'blk', down)]
    ppermute x4, waiting for transfers between devices: 5.28 us -> 1.05 us  [ring_gather(): a = lax.ppermute(a, 'blk', up)]
    ppermute x4, starting transfers between devices: 5.36 us -> 1.73 us  [ring_gather(): a = lax.ppermute(a, 'blk', up)]
  transfers between devices with their start and end apart: 8 -> 8, of which waited for: 4 -> 3; matrix products, arithmetic and copies ran while one was open for 2% -> 2% of each run, Pallas kernels for 15% -> 25%
where the time goes in v9:
time: 67 us; the launch traced here: 66.7 us
  Pallas kernels  52.8 us (79%)
  starting transfers between devices  8.36 us (12%)
  waiting for transfers between devices  2.58 us (4%)
  other arithmetic  1.8 us (3%)
  local copies, waits for them, and re-layouts  1 us (1%)
    pallas_call x1, Pallas kernels, correlate(): pl.pallas_call(functools.partial(correlate_kernel, n, steps), grid=(steps...  36.2 us
    pallas_call x4, Pallas kernels, embed(): pl.pallas_call(embed_kernel, grid=(steps, channels // width), in_specs=[p...  16.6 us
    ppermute x3, starting transfers between devices, ring_gather(): b = lax.ppermute(b, 'blk', down)  6.55 us
    ppermute x4, starting transfers between devices, ring_gather(): a = lax.ppermute(a, 'blk', up)  1.73 us
    ppermute x1, waiting for transfers between devices, per_device(): return mine + lax.ppermute(other, 'chan', [(0, 1), (1, 0)])  1.52 us
  transfers between devices with their start and end apart: 8, of which 3 were waited for; matrix products, arithmetic and copies ran while one was open for 2% of the time, Pallas kernels for 25%

profile of v9, /device:TPU:0, one launch (start us, length us, event | category | flops | bytes accessed | tf_op | source)
XLA Modules:
  0.0 66.7 jit_solution(15284824325507882074)
XLA Ops:
  0.0 1.0 %copy.5 = bf16[512,128]{0,1:T(8,128)(2,1)S(1)} copy(bf16[512,128]{1,0:T(8,128)(2,1)} %param.4) | data formatting | bytes 262144 | tf_op args[0]
  1.0 3.0 %collective-permute-start.1 = (bf16[128,512]{1,0:T(8,128)(2,1)S(1)}, bf16[128,512]{1,0:T(8,128)(2,1)S(1)}, u32[]{:S(2)}, u32[]{:S(2)}) collective-permute-start(bf16[128,512]{1,0:T(8,128)(2,1)S(1)} %bitcast.1), channel_id=1, source_target_pairs={{4,0},{8,4},{12,8},{14,12},{10,14},{6,10},{2,6},{0,2},{5,1},{9,5},... | collective-permute-start | bytes 393224 | tf_op jit(solution)/shard_map/ppermute | solution.py:94
  4.0 0.1 collective-permute-start
  4.2 1.1 %multiply_add_fusion.place_ref = s32[128,512]{1,0:T(8,128)S(1)} fusion(s32[128,512]{1,0:T(8,128)} %param.6, s32[128,512]{1,0:T(8,128)} %param.7), kind=kLoop, calls=%fused_computation | loop fusion | flops 131072 | bytes 786432 | tf_op jit(solution)/shard_map/add | solution.py:239
  5.2 4.1 %shard_map.46.refs_8_ = bf16[104,32,512]{2,1,0:T(8,128)(2,1)S(1)} custom-call(bf16[100,128,512]{2,1,0:T(8,128)(2,1)} %t_ref.7, s32[128,512]{1,0:T(8,128)S(1)} %multiply_add_fusion.place_ref), custom_call_target="tpu_custom_call" | custom-call | flops 34078720 | bytes 6815744 | tf_op jit(solution)/shard_map/pallas_call | solution.py:55
  9.4 0.0 collective-permute-done.1.refs_1_
  9.4 0.0 collective-permute-done.refs_7_
  9.4 2.0 %collective-permute-start.3 = (bf16[128,512]{1,0:T(8,128)(2,1)S(1)}, bf16[128,512]{1,0:T(8,128)(2,1)S(1)}, u32[]{:S(2)}, u32[]{:S(2)}) collective-permute-start(bf16[128,512]{1,0:T(8,128)(2,1)S(1)} %collective-permute-done.1.refs_1_), channel_id=1, source_target_pairs={{4,0},{8,4},{12,8},{14,12},{10,14},{6,10},{2,6},{0,2},{5,1},{9,5},... | collective-permute-start | bytes 393224 | tf_op jit(solution)/shard_map/ppermute | solution.py:94
  11.4 0.1 collective-permute-start.2
  11.5 4.1 %shard_map.47.refs_9_ = bf16[104,32,512]{2,1,0:T(8,128)(2,1)S(1)} custom-call(bf16[100,128,512]{2,1,0:T(8,128)(2,1)} %t_ref.7, s32[128,512]{1,0:T(8,128)S(1)} %multiply_add_fusion.place_ref), custom_call_target="tpu_custom_call" | custom-call | flops 34078720 | bytes 6815744 | tf_op jit(solution)/shard_map/pallas_call | solution.py:55
  15.6 0.0 collective-permute-done.3.refs_2_
  15.6 0.7 %collective-permute-done.2.refs_6_ = bf16[128,512]{1,0:T(8,128)(2,1)S(1)} collective-permute-done((bf16[128,512]{1,0:T(8,128)(2,1)S(1)}, bf16[128,512]{1,0:T(8,128)(2,1)S(1)}, u32[]{:S(2)}, u32[]{:S(2)}) %collective-permute-start.2) | collective-permute-done | bytes 131104 | tf_op jit(solution)/shard_map/ppermute | solution.py:92
  16.3 1.6 %collective-permute-start.5 = (bf16[128,512]{1,0:T(8,128)(2,1)S(1)}, bf16[128,512]{1,0:T(8,128)(2,1)S(1)}, u32[]{:S(2)}, u32[]{:S(2)}) collective-permute-start(bf16[128,512]{1,0:T(8,128)(2,1)S(1)} %collective-permute-done.3.refs_2_), channel_id=1, source_target_pairs={{4,0},{8,4},{12,8},{14,12},{10,14},{6,10},{2,6},{0,2},{5,1},{9,5},... | collective-permute-start | bytes 393224 | tf_op jit(solution)/shard_map/ppermute | solution.py:94
  17.9 0.4 collective-permute-start.4
  18.3 4.1 %shard_map.48.refs_10_ = bf16[104,32,512]{2,1,0:T(8,128)(2,1)S(1)} custom-call(bf16[100,128,512]{2,1,0:T(8,128)(2,1)} %t_ref.7, s32[128,512]{1,0:T(8,128)S(1)} %multiply_add_fusion.place_ref), custom_call_target="tpu_custom_call" | custom-call | flops 34078720 | bytes 6815744 | tf_op jit(solution)/shard_map/pallas_call | solution.py:55
  22.5 0.0 collective-permute-done.5.refs_3_
  22.5 0.4 collective-permute-done.4.refs_5_
  22.9 1.0 %collective-permute-start.6 = (bf16[128,512]{1,0:T(8,128)(2,1)S(1)}, bf16[128,512]{1,0:T(8,128)(2,1)S(1)}, u32[]{:S(2)}, u32[]{:S(2)}) collective-permute-start(bf16[128,512]{1,0:T(8,128)(2,1)S(1)} %collective-permute-done.4.refs_5_), channel_id=1, source_target_pairs={{0,4},{4,8},{8,12},{12,14},{14,10},{10,6},{6,2},{2,0},{1,5},{5,9},... | collective-permute-start | bytes 393224 | tf_op jit(solution)/shard_map/ppermute | solution.py:92
  23.9 4.1 %shard_map.49.refs_11_ = bf16[104,32,512]{2,1,0:T(8,128)(2,1)S(1)} custom-call(bf16[100,128,512]{2,1,0:T(8,128)(2,1)} %t_ref.7, s32[128,512]{1,0:T(8,128)S(1)} %multiply_add_fusion.place_ref), custom_call_target="tpu_custom_call" | custom-call | flops 34078720 | bytes 6815744 | tf_op jit(solution)/shard_map/pallas_call | solution.py:55
  28.1 0.0 collective-permute-done.6.refs_4_
  28.1 36.2 %shard_map.50 = (f32[128,512]{1,0:T(8,128)S(1)}, f32[128,512]{1,0:T(8,128)S(1)}) custom-call(bf16[128,512]{1,0:T(8,128)(2,1)S(1)} %bitcast.3, bf16[128,512]{1,0:T(8,128)(2,1)S(1)} %collective-permute-done.1.refs_1_, bf16[128,512]{1,0:T(8,128)(2,1)S(1)} %collective-permute-done.3.refs_2_, bf16[128,512]{1,0:T(8,128)(2,1)S(1)} %collective-permute-done.5.refs_3_, ...), custom_call_target="tpu_custom_call" | custom-call | flops 13958643712 | bytes 13631488 | tf_op jit(solution)/shard_map/pallas_call | solution.py:217
  64.3 0.1 collective-permute-start.7
  64.4 1.5 %collective-permute-done.7 = f32[128,512]{1,0:T(8,128)S(1)} collective-permute-done((f32[128,512]{1,0:T(8,128)S(1)}, f32[128,512]{1,0:T(8,128)S(1)}, u32[]{:S(2)}, u32[]{:S(2)}) %collective-permute-start.7) | collective-permute-done | bytes 262176 | tf_op jit(solution)/shard_map/ppermute | solution.py:242
  65.9 0.7 %add.7 = f32[128,512]{1,0:T(8,128)} add(f32[128,512]{1,0:T(8,128)S(1)} %get-tuple-element.29, f32[128,512]{1,0:T(8,128)S(1)} %collective-permute-done.7) | non-fusion elementwise | flops 65536 | bytes 786432 | tf_op jit(solution)/shard_map/add | solution.py:242
Async XLA Ops:
  1.0 8.4 %collective-permute-start.1 = (bf16[128,512]{1,0:T(8,128)(2,1)S(1)}, bf16[128,512]{1,0:T(8,128)(2,1)S(1)}, u32[]{:S(2)}, u32[]{:S(2)}) collective-permute-start(bf16[128,512]{1,0:T(8,128)(2,1)S(1)} %bitcast.1), channel_id=1, source_target_pairs={{4,0},{8,4},{12,8},{14,12},{10,14},{6,10},{2,6},{0,2},{5,1},{9,5},... | collective-permute-start | bytes 393224 | tf_op jit(solution)/shard_map/ppermute | solution.py:94
  4.0 5.4 %collective-permute-start = (bf16[128,512]{1,0:T(8,128)(2,1)S(1)}, bf16[128,512]{1,0:T(8,128)(2,1)S(1)}, u32[]{:S(2)}, u32[]{:S(2)}) collective-permute-start(bf16[128,512]{1,0:T(8,128)(2,1)S(1)} %bitcast.2), channel_id=1, source_target_pairs={{0,4},{4,8},{8,12},{12,14},{14,10},{10,6},{6,2},{2,0},{1,5},{5,9},... | collective-permute-start | bytes 393224 | tf_op jit(solution)/shard_map/ppermute | solution.py:92
  9.4 6.2 %collective-permute-start.3 = (bf16[128,512]{1,0:T(8,128)(2,1)S(1)}, bf16[128,512]{1,0:T(8,128)(2,1)S(1)}, u32[]{:S(2)}, u32[]{:S(2)}) collective-permute-start(bf16[128,512]{1,0:T(8,128)(2,1)S(1)} %collective-permute-done.1.refs_1_), channel_id=1, source_target_pairs={{4,0},{8,4},{12,8},{14,12},{10,14},{6,10},{2,6},{0,2},{5,1},{9,5},... | collective-permute-start | bytes 393224 | tf_op jit(solution)/shard_map/ppermute | solution.py:94
  11.4 5.0 %collective-permute-start.2 = (bf16[128,512]{1,0:T(8,128)(2,1)S(1)}, bf16[128,512]{1,0:T(8,128)(2,1)S(1)}, u32[]{:S(2)}, u32[]{:S(2)}) collective-permute-start(bf16[128,512]{1,0:T(8,128)(2,1)S(1)} %collective-permute-done.refs_7_), channel_id=1, source_target_pairs={{0,4},{4,8},{8,12},{12,14},{14,10},{10,6},{6,2},{2,0},{1,5},{5,9},... | collective-permute-start | bytes 393224 | tf_op jit(solution)/shard_map/ppermute | solution.py:92
  16.3 6.2 %collective-permute-start.5 = (bf16[128,512]{1,0:T(8,128)(2,1)S(1)}, bf16[128,512]{1,0:T(8,128)(2,1)S(1)}, u32[]{:S(2)}, u32[]{:S(2)}) collective-permute-start(bf16[128,512]{1,0:T(8,128)(2,1)S(1)} %collective-permute-done.3.refs_2_), channel_id=1, source_target_pairs={{4,0},{8,4},{12,8},{14,12},{10,14},{6,10},{2,6},{0,2},{5,1},{9,5},... | collective-permute-start | bytes 393224 | tf_op jit(solution)/shard_map/ppermute | solution.py:94
  17.9 5.0 %collective-permute-start.4 = (bf16[128,512]{1,0:T(8,128)(2,1)S(1)}, bf16[128,512]{1,0:T(8,128)(2,1)S(1)}, u32[]{:S(2)}, u32[]{:S(2)}) collective-permute-start(bf16[128,512]{1,0:T(8,128)(2,1)S(1)} %collective-permute-done.2.refs_6_), channel_id=1, source_target_pairs={{0,4},{4,8},{8,12},{12,14},{14,10},{10,6},{6,2},{2,0},{1,5},{5,9},... | collective-permute-start | bytes 393224 | tf_op jit(solution)/shard_map/ppermute | solution.py:92
  22.9 5.2 %collective-permute-start.6 = (bf16[128,512]{1,0:T(8,128)(2,1)S(1)}, bf16[128,512]{1,0:T(8,128)(2,1)S(1)}, u32[]{:S(2)}, u32[]{:S(2)}) collective-permute-start(bf16[128,512]{1,0:T(8,128)(2,1)S(1)} %collective-permute-done.4.refs_5_), channel_id=1, source_target_pairs={{0,4},{4,8},{8,12},{12,14},{14,10},{10,6},{6,2},{2,0},{1,5},{5,9},... | collective-permute-start | bytes 393224 | tf_op jit(solution)/shard_map/ppermute | solution.py:92
  64.3 1.6 %collective-permute-start.7 = (f32[128,512]{1,0:T(8,128)S(1)}, f32[128,512]{1,0:T(8,128)S(1)}, u32[]{:S(2)}, u32[]{:S(2)}) collective-permute-start(f32[128,512]{1,0:T(8,128)S(1)} %get-tuple-element.30), channel_id=1, source_target_pairs={{0,1},{1,0},{2,3},{3,2},{4,5},{5,4},{6,7},{7,6},{8,9},{9,8},{10,11... | collective-permute-start | bytes 786440 | tf_op jit(solution)/shard_map/ppermute | solution.py:242

commit v10 on v9

--- a/solution.py
+++ b/solution.py
@@ -16,6 +16,7 @@
 ROWS = 16
 TAPS = 4
 TILE = 1024
+CHUNK = 8
 GROUP = 8
 EMBED_VMEM = 44 * 1024 * 1024
 VMEM = 28 * 1024 * 1024
@@ -179,13 +180,22 @@
 
     def tile(m, carry):
         rows = pl.ds(pl.multiple_of(m * TILE, TILE), TILE)
-        parts = []
-        for tap in range(TAPS):
-            first = pl.multiple_of(m * TILE + (step * TAPS + tap) * n, n)
-            for w in range(width // LANES):
-                value = x_ref[w, pl.ds(first, TILE), :] * n_ref[w, rows, :]
-                parts.append(value.astype(jnp.bfloat16))
-        windows = jnp.concatenate(parts, axis=1)
+        tiles = width // LANES
+        parts = [[[] for _ in range(tiles)] for _ in range(TAPS)]
+        size = CHUNK * n
+        for tap0 in range(0, TAPS, 2):
+            for w in range(tiles):
+                for c in range(0, TILE, size):
+                    first = pl.multiple_of(m * TILE + c, size)
+                    norm = n_ref[w, pl.ds(first, size), :]
+                    first = pl.multiple_of(first + (step * TAPS + tap0) * n, n)
+                    samples = x_ref[w, pl.ds(first, size + n), :]
+                    for tap in range(2):
+                        value = samples[tap * n : tap * n + size] * norm
+                        parts[tap0 + tap][w].append(value.astype(jnp.bfloat16))
+        windows = jnp.concatenate(
+            [jnp.concatenate(chunks, axis=0) for part in parts for chunks in part], axis=1
+        )
         weights = jnp.concatenate(
             [jnp.concatenate([e_ref[tap] for e_ref in e_refs], axis=0) for tap in range(TAPS)],
             axis=1,

time: 67 us -> 67 us (level)
  no operation moved by 1% of the time
where the time goes in v10:
time: 67 us; the launch traced here: 66.7 us
  Pallas kernels  52.8 us (79%)
  starting transfers between devices  8.36 us (12%)
  waiting for transfers between devices  2.58 us (4%)
  other arithmetic  1.8 us (3%)
  local copies, waits for them, and re-layouts  1 us (1%)
    pallas_call x1, Pallas kernels, correlate(): pl.pallas_call(functools.partial(correlate_kernel, n, steps), grid=(steps...  36.2 us
    pallas_call x4, Pallas kernels, embed(): pl.pallas_call(embed_kernel, grid=(steps, channels // width), in_specs=[p...  16.6 us
    ppermute x3, starting transfers between devices, ring_gather(): b = lax.ppermute(b, 'blk', down)  6.55 us
    ppermute x4, starting transfers between devices, ring_gather(): a = lax.ppermute(a, 'blk', up)  1.73 us
    ppermute x1, waiting for transfers between devices, per_device(): return mine + lax.ppermute(other, 'chan', [(0, 1), (1, 0)])  1.52 us
  transfers between devices with their start and end apart: 8, of which 3 were waited for; matrix products, arithmetic and copies ran while one was open for 2% of the time, Pallas kernels for 25%

profile of v10, /device:TPU:0, one launch (start us, length us, event | category | flops | bytes accessed | tf_op | source)
XLA Modules:
  0.0 66.7 jit_solution(1860355623932772062)
XLA Ops:
  0.0 1.0 %copy.5 = bf16[512,128]{0,1:T(8,128)(2,1)S(1)} copy(bf16[512,128]{1,0:T(8,128)(2,1)} %param.4) | data formatting | bytes 262144 | tf_op args[0]
  1.0 3.0 %collective-permute-start.1 = (bf16[128,512]{1,0:T(8,128)(2,1)S(1)}, bf16[128,512]{1,0:T(8,128)(2,1)S(1)}, u32[]{:S(2)}, u32[]{:S(2)}) collective-permute-start(bf16[128,512]{1,0:T(8,128)(2,1)S(1)} %bitcast.1), channel_id=1, source_target_pairs={{4,0},{8,4},{12,8},{14,12},{10,14},{6,10},{2,6},{0,2},{5,1},{9,5},... | collective-permute-start | bytes 393224 | tf_op jit(solution)/shard_map/ppermute | solution.py:95
  4.0 0.1 collective-permute-start
  4.2 1.1 %multiply_add_fusion.place_ref = s32[128,512]{1,0:T(8,128)S(1)} fusion(s32[128,512]{1,0:T(8,128)} %param.6, s32[128,512]{1,0:T(8,128)} %param.7), kind=kLoop, calls=%fused_computation | loop fusion | flops 131072 | bytes 786432 | tf_op jit(solution)/shard_map/add | solution.py:249
  5.2 4.1 %shard_map.46.refs_8_ = bf16[104,32,512]{2,1,0:T(8,128)(2,1)S(1)} custom-call(bf16[100,128,512]{2,1,0:T(8,128)(2,1)} %t_ref.7, s32[128,512]{1,0:T(8,128)S(1)} %multiply_add_fusion.place_ref), custom_call_target="tpu_custom_call" | custom-call | flops 34078720 | bytes 6815744 | tf_op jit(solution)/shard_map/pallas_call | solution.py:56
  9.4 0.0 collective-permute-done.1.refs_1_
  9.4 0.0 collective-permute-done.refs_7_
  9.4 2.0 %collective-permute-start.3 = (bf16[128,512]{1,0:T(8,128)(2,1)S(1)}, bf16[128,512]{1,0:T(8,128)(2,1)S(1)}, u32[]{:S(2)}, u32[]{:S(2)}) collective-permute-start(bf16[128,512]{1,0:T(8,128)(2,1)S(1)} %collective-permute-done.1.refs_1_), channel_id=1, source_target_pairs={{4,0},{8,4},{12,8},{14,12},{10,14},{6,10},{2,6},{0,2},{5,1},{9,5},... | collective-permute-start | bytes 393224 | tf_op jit(solution)/shard_map/ppermute | solution.py:95
  11.4 0.1 collective-permute-start.2
  11.5 4.1 %shard_map.47.refs_9_ = bf16[104,32,512]{2,1,0:T(8,128)(2,1)S(1)} custom-call(bf16[100,128,512]{2,1,0:T(8,128)(2,1)} %t_ref.7, s32[128,512]{1,0:T(8,128)S(1)} %multiply_add_fusion.place_ref), custom_call_target="tpu_custom_call" | custom-call | flops 34078720 | bytes 6815744 | tf_op jit(solution)/shard_map/pallas_call | solution.py:56
  15.6 0.0 collective-permute-done.3.refs_2_
  15.6 0.7 %collective-permute-done.2.refs_6_ = bf16[128,512]{1,0:T(8,128)(2,1)S(1)} collective-permute-done((bf16[128,512]{1,0:T(8,128)(2,1)S(1)}, bf16[128,512]{1,0:T(8,128)(2,1)S(1)}, u32[]{:S(2)}, u32[]{:S(2)}) %collective-permute-start.2) | collective-permute-done | bytes 131104 | tf_op jit(solution)/shard_map/ppermute | solution.py:93
  16.3 1.6 %collective-permute-start.5 = (bf16[128,512]{1,0:T(8,128)(2,1)S(1)}, bf16[128,512]{1,0:T(8,128)(2,1)S(1)}, u32[]{:S(2)}, u32[]{:S(2)}) collective-permute-start(bf16[128,512]{1,0:T(8,128)(2,1)S(1)} %collective-permute-done.3.refs_2_), channel_id=1, source_target_pairs={{4,0},{8,4},{12,8},{14,12},{10,14},{6,10},{2,6},{0,2},{5,1},{9,5},... | collective-permute-start | bytes 393224 | tf_op jit(solution)/shard_map/ppermute | solution.py:95
  17.9 0.4 collective-permute-start.4
  18.3 4.1 %shard_map.48.refs_10_ = bf16[104,32,512]{2,1,0:T(8,128)(2,1)S(1)} custom-call(bf16[100,128,512]{2,1,0:T(8,128)(2,1)} %t_ref.7, s32[128,512]{1,0:T(8,128)S(1)} %multiply_add_fusion.place_ref), custom_call_target="tpu_custom_call" | custom-call | flops 34078720 | bytes 6815744 | tf_op jit(solution)/shard_map/pallas_call | solution.py:56
  22.5 0.0 collective-permute-done.5.refs_3_
  22.5 0.4 collective-permute-done.4.refs_5_
  22.9 1.0 %collective-permute-start.6 = (bf16[128,512]{1,0:T(8,128)(2,1)S(1)}, bf16[128,512]{1,0:T(8,128)(2,1)S(1)}, u32[]{:S(2)}, u32[]{:S(2)}) collective-permute-start(bf16[128,512]{1,0:T(8,128)(2,1)S(1)} %collective-permute-done.4.refs_5_), channel_id=1, source_target_pairs={{0,4},{4,8},{8,12},{12,14},{14,10},{10,6},{6,2},{2,0},{1,5},{5,9},... | collective-permute-start | bytes 393224 | tf_op jit(solution)/shard_map/ppermute | solution.py:93
  23.9 4.1 %shard_map.49.refs_11_ = bf16[104,32,512]{2,1,0:T(8,128)(2,1)S(1)} custom-call(bf16[100,128,512]{2,1,0:T(8,128)(2,1)} %t_ref.7, s32[128,512]{1,0:T(8,128)S(1)} %multiply_add_fusion.place_ref), custom_call_target="tpu_custom_call" | custom-call | flops 34078720 | bytes 6815744 | tf_op jit(solution)/shard_map/pallas_call | solution.py:56
  28.1 0.0 collective-permute-done.6.refs_4_
  28.1 36.2 %shard_map.50 = (f32[128,512]{1,0:T(8,128)S(1)}, f32[128,512]{1,0:T(8,128)S(1)}) custom-call(bf16[128,512]{1,0:T(8,128)(2,1)S(1)} %bitcast.3, bf16[128,512]{1,0:T(8,128)(2,1)S(1)} %collective-permute-done.1.refs_1_, bf16[128,512]{1,0:T(8,128)(2,1)S(1)} %collective-permute-done.3.refs_2_, bf16[128,512]{1,0:T(8,128)(2,1)S(1)} %collective-permute-done.5.refs_3_, ...), custom_call_target="tpu_custom_call" | custom-call | flops 13958643712 | bytes 13631488 | tf_op jit(solution)/shard_map/pallas_call | solution.py:227
  64.3 0.1 collective-permute-start.7
  64.4 1.5 %collective-permute-done.7 = f32[128,512]{1,0:T(8,128)S(1)} collective-permute-done((f32[128,512]{1,0:T(8,128)S(1)}, f32[128,512]{1,0:T(8,128)S(1)}, u32[]{:S(2)}, u32[]{:S(2)}) %collective-permute-start.7) | collective-permute-done | bytes 262176 | tf_op jit(solution)/shard_map/ppermute | solution.py:252
  65.9 0.7 %add.7 = f32[128,512]{1,0:T(8,128)} add(f32[128,512]{1,0:T(8,128)S(1)} %get-tuple-element.29, f32[128,512]{1,0:T(8,128)S(1)} %collective-permute-done.7) | non-fusion elementwise | flops 65536 | bytes 786432 | tf_op jit(solution)/shard_map/add | solution.py:252
Async XLA Ops:
  1.0 8.4 %collective-permute-start.1 = (bf16[128,512]{1,0:T(8,128)(2,1)S(1)}, bf16[128,512]{1,0:T(8,128)(2,1)S(1)}, u32[]{:S(2)}, u32[]{:S(2)}) collective-permute-start(bf16[128,512]{1,0:T(8,128)(2,1)S(1)} %bitcast.1), channel_id=1, source_target_pairs={{4,0},{8,4},{12,8},{14,12},{10,14},{6,10},{2,6},{0,2},{5,1},{9,5},... | collective-permute-start | bytes 393224 | tf_op jit(solution)/shard_map/ppermute | solution.py:95
  4.0 5.4 %collective-permute-start = (bf16[128,512]{1,0:T(8,128)(2,1)S(1)}, bf16[128,512]{1,0:T(8,128)(2,1)S(1)}, u32[]{:S(2)}, u32[]{:S(2)}) collective-permute-start(bf16[128,512]{1,0:T(8,128)(2,1)S(1)} %bitcast.2), channel_id=1, source_target_pairs={{0,4},{4,8},{8,12},{12,14},{14,10},{10,6},{6,2},{2,0},{1,5},{5,9},... | collective-permute-start | bytes 393224 | tf_op jit(solution)/shard_map/ppermute | solution.py:93
  9.4 6.2 %collective-permute-start.3 = (bf16[128,512]{1,0:T(8,128)(2,1)S(1)}, bf16[128,512]{1,0:T(8,128)(2,1)S(1)}, u32[]{:S(2)}, u32[]{:S(2)}) collective-permute-start(bf16[128,512]{1,0:T(8,128)(2,1)S(1)} %collective-permute-done.1.refs_1_), channel_id=1, source_target_pairs={{4,0},{8,4},{12,8},{14,12},{10,14},{6,10},{2,6},{0,2},{5,1},{9,5},... | collective-permute-start | bytes 393224 | tf_op jit(solution)/shard_map/ppermute | solution.py:95
  11.4 5.0 %collective-permute-start.2 = (bf16[128,512]{1,0:T(8,128)(2,1)S(1)}, bf16[128,512]{1,0:T(8,128)(2,1)S(1)}, u32[]{:S(2)}, u32[]{:S(2)}) collective-permute-start(bf16[128,512]{1,0:T(8,128)(2,1)S(1)} %collective-permute-done.refs_7_), channel_id=1, source_target_pairs={{0,4},{4,8},{8,12},{12,14},{14,10},{10,6},{6,2},{2,0},{1,5},{5,9},... | collective-permute-start | bytes 393224 | tf_op jit(solution)/shard_map/ppermute | solution.py:93
  16.3 6.2 %collective-permute-start.5 = (bf16[128,512]{1,0:T(8,128)(2,1)S(1)}, bf16[128,512]{1,0:T(8,128)(2,1)S(1)}, u32[]{:S(2)}, u32[]{:S(2)}) collective-permute-start(bf16[128,512]{1,0:T(8,128)(2,1)S(1)} %collective-permute-done.3.refs_2_), channel_id=1, source_target_pairs={{4,0},{8,4},{12,8},{14,12},{10,14},{6,10},{2,6},{0,2},{5,1},{9,5},... | collective-permute-start | bytes 393224 | tf_op jit(solution)/shard_map/ppermute | solution.py:95
  17.9 5.0 %collective-permute-start.4 = (bf16[128,512]{1,0:T(8,128)(2,1)S(1)}, bf16[128,512]{1,0:T(8,128)(2,1)S(1)}, u32[]{:S(2)}, u32[]{:S(2)}) collective-permute-start(bf16[128,512]{1,0:T(8,128)(2,1)S(1)} %collective-permute-done.2.refs_6_), channel_id=1, source_target_pairs={{0,4},{4,8},{8,12},{12,14},{14,10},{10,6},{6,2},{2,0},{1,5},{5,9},... | collective-permute-start | bytes 393224 | tf_op jit(solution)/shard_map/ppermute | solution.py:93
  22.9 5.2 %collective-permute-start.6 = (bf16[128,512]{1,0:T(8,128)(2,1)S(1)}, bf16[128,512]{1,0:T(8,128)(2,1)S(1)}, u32[]{:S(2)}, u32[]{:S(2)}) collective-permute-start(bf16[128,512]{1,0:T(8,128)(2,1)S(1)} %collective-permute-done.4.refs_5_), channel_id=1, source_target_pairs={{0,4},{4,8},{8,12},{12,14},{14,10},{10,6},{6,2},{2,0},{1,5},{5,9},... | collective-permute-start | bytes 393224 | tf_op jit(solution)/shard_map/ppermute | solution.py:93
  64.3 1.6 %collective-permute-start.7 = (f32[128,512]{1,0:T(8,128)S(1)}, f32[128,512]{1,0:T(8,128)S(1)}, u32[]{:S(2)}, u32[]{:S(2)}) collective-permute-start(f32[128,512]{1,0:T(8,128)S(1)} %get-tuple-element.30), channel_id=1, source_target_pairs={{0,1},{1,0},{2,3},{3,2},{4,5},{5,4},{6,7},{7,6},{8,9},{9,8},{10,11... | collective-permute-start | bytes 786440 | tf_op jit(solution)/shard_map/ppermute | solution.py:252

commit v11 on v9

--- a/solution.py
+++ b/solution.py
@@ -112,21 +112,16 @@
                 for i in range(2):
                     x_ref[w, pl.ds((u + 8 * i) * n + v, 8, stride=n), :] = value[8 * i : 8 * i + 8]
 
-        @pl.when(v > 0)
-        def _():
-            for w in range(width // LANES):
-                for u in range(0, LE, 8):
-                    value = x_ref[w, pl.ds(u * n + v, 8, stride=n), :]
-                    x_ref[w, pl.ds((lags + u) * n + v - 1, 8, stride=n), :] = value
-
-        @pl.when(v == 0)
-        def _():
-            for w in range(width // LANES):
-                for u in range(0, LE, 8):
-                    x_ref[w, pl.ds((lags + u) * n + n - 1, 8, stride=n), :] = jnp.zeros(
-                        (8, LANES), jnp.float32
-                    )
-
+    inner = lax.broadcasted_iota(jnp.int32, (n, LANES), 0) < n - 1
+
+    def past(u, carry):
+        for w in range(width // LANES):
+            value = x_ref[w, pl.ds(pl.multiple_of(u * n, n), n), :]
+            value = jnp.where(inner, pltpu.roll(value, n - 1, 0), 0.0)
+            x_ref[w, pl.ds(pl.multiple_of((lags + u) * n, n), n), :] = value
+        return carry
+
+    lax.fori_loop(0, LE, past, 0, unroll=8)
     size = GROUP * n
 
     def energy(g, carry):

time: 67 us -> 66.8 us (level)
  no operation moved by 1% of the time
where the time goes in v11:
time: 66.8 us; the launch traced here: 66.4 us
  Pallas kernels  52.5 us (79%)
  starting transfers between devices  8.36 us (13%)
  waiting for transfers between devices  2.58 us (4%)
  other arithmetic  1.8 us (3%)
  local copies, waits for them, and re-layouts  1 us (1%)
    pallas_call x1, Pallas kernels, correlate(): pl.pallas_call(functools.partial(correlate_kernel, n, steps), grid=(steps...  36 us
    pallas_call x4, Pallas kernels, embed(): pl.pallas_call(embed_kernel, grid=(steps, channels // width), in_specs=[p...  16.6 us
    ppermute x3, starting transfers between devices, ring_gather(): b = lax.ppermute(b, 'blk', down)  6.55 us
    ppermute x4, starting transfers between devices, ring_gather(): a = lax.ppermute(a, 'blk', up)  1.73 us
    ppermute x1, waiting for transfers between devices, per_device(): return mine + lax.ppermute(other, 'chan', [(0, 1), (1, 0)])  1.52 us
  transfers between devices with their start and end apart: 8, of which 3 were waited for; matrix products, arithmetic and copies ran while one was open for 2% of the time, Pallas kernels for 25%

profile of v11, /device:TPU:0, one launch (start us, length us, event | category | flops | bytes accessed | tf_op | source)
XLA Modules:
  0.0 66.4 jit_solution(9807615710520699040)
XLA Ops:
  0.0 1.0 %copy.5 = bf16[512,128]{0,1:T(8,128)(2,1)S(1)} copy(bf16[512,128]{1,0:T(8,128)(2,1)} %param.4) | data formatting | bytes 262144 | tf_op args[0]
  1.0 3.0 %collective-permute-start.1 = (bf16[128,512]{1,0:T(8,128)(2,1)S(1)}, bf16[128,512]{1,0:T(8,128)(2,1)S(1)}, u32[]{:S(2)}, u32[]{:S(2)}) collective-permute-start(bf16[128,512]{1,0:T(8,128)(2,1)S(1)} %bitcast.1), channel_id=1, source_target_pairs={{4,0},{8,4},{12,8},{14,12},{10,14},{6,10},{2,6},{0,2},{5,1},{9,5},... | collective-permute-start | bytes 393224 | tf_op jit(solution)/shard_map/ppermute | solution.py:94
  4.0 0.1 collective-permute-start
  4.2 1.1 %multiply_add_fusion.place_ref = s32[128,512]{1,0:T(8,128)S(1)} fusion(s32[128,512]{1,0:T(8,128)} %param.6, s32[128,512]{1,0:T(8,128)} %param.7), kind=kLoop, calls=%fused_computation | loop fusion | flops 131072 | bytes 786432 | tf_op jit(solution)/shard_map/add | solution.py:234
  5.2 4.1 %shard_map.46.refs_8_ = bf16[104,32,512]{2,1,0:T(8,128)(2,1)S(1)} custom-call(bf16[100,128,512]{2,1,0:T(8,128)(2,1)} %t_ref.7, s32[128,512]{1,0:T(8,128)S(1)} %multiply_add_fusion.place_ref), custom_call_target="tpu_custom_call" | custom-call | flops 34078720 | bytes 6815744 | tf_op jit(solution)/shard_map/pallas_call | solution.py:55
  9.4 0.0 collective-permute-done.1.refs_1_
  9.4 0.0 collective-permute-done.refs_7_
  9.4 2.0 %collective-permute-start.3 = (bf16[128,512]{1,0:T(8,128)(2,1)S(1)}, bf16[128,512]{1,0:T(8,128)(2,1)S(1)}, u32[]{:S(2)}, u32[]{:S(2)}) collective-permute-start(bf16[128,512]{1,0:T(8,128)(2,1)S(1)} %collective-permute-done.1.refs_1_), channel_id=1, source_target_pairs={{4,0},{8,4},{12,8},{14,12},{10,14},{6,10},{2,6},{0,2},{5,1},{9,5},... | collective-permute-start | bytes 393224 | tf_op jit(solution)/shard_map/ppermute | solution.py:94
  11.4 0.1 collective-permute-start.2
  11.5 4.1 %shard_map.47.refs_9_ = bf16[104,32,512]{2,1,0:T(8,128)(2,1)S(1)} custom-call(bf16[100,128,512]{2,1,0:T(8,128)(2,1)} %t_ref.7, s32[128,512]{1,0:T(8,128)S(1)} %multiply_add_fusion.place_ref), custom_call_target="tpu_custom_call" | custom-call | flops 34078720 | bytes 6815744 | tf_op jit(solution)/shard_map/pallas_call | solution.py:55
  15.6 0.0 collective-permute-done.3.refs_2_
  15.6 0.7 %collective-permute-done.2.refs_6_ = bf16[128,512]{1,0:T(8,128)(2,1)S(1)} collective-permute-done((bf16[128,512]{1,0:T(8,128)(2,1)S(1)}, bf16[128,512]{1,0:T(8,128)(2,1)S(1)}, u32[]{:S(2)}, u32[]{:S(2)}) %collective-permute-start.2) | collective-permute-done | bytes 131104 | tf_op jit(solution)/shard_map/ppermute | solution.py:92
  16.3 1.6 %collective-permute-start.5 = (bf16[128,512]{1,0:T(8,128)(2,1)S(1)}, bf16[128,512]{1,0:T(8,128)(2,1)S(1)}, u32[]{:S(2)}, u32[]{:S(2)}) collective-permute-start(bf16[128,512]{1,0:T(8,128)(2,1)S(1)} %collective-permute-done.3.refs_2_), channel_id=1, source_target_pairs={{4,0},{8,4},{12,8},{14,12},{10,14},{6,10},{2,6},{0,2},{5,1},{9,5},... | collective-permute-start | bytes 393224 | tf_op jit(solution)/shard_map/ppermute | solution.py:94
  17.9 0.4 collective-permute-start.4
  18.3 4.1 %shard_map.48.refs_10_ = bf16[104,32,512]{2,1,0:T(8,128)(2,1)S(1)} custom-call(bf16[100,128,512]{2,1,0:T(8,128)(2,1)} %t_ref.7, s32[128,512]{1,0:T(8,128)S(1)} %multiply_add_fusion.place_ref), custom_call_target="tpu_custom_call" | custom-call | flops 34078720 | bytes 6815744 | tf_op jit(solution)/shard_map/pallas_call | solution.py:55
  22.5 0.0 collective-permute-done.5.refs_3_
  22.5 0.4 collective-permute-done.4.refs_5_
  22.9 1.0 %collective-permute-start.6 = (bf16[128,512]{1,0:T(8,128)(2,1)S(1)}, bf16[128,512]{1,0:T(8,128)(2,1)S(1)}, u32[]{:S(2)}, u32[]{:S(2)}) collective-permute-start(bf16[128,512]{1,0:T(8,128)(2,1)S(1)} %collective-permute-done.4.refs_5_), channel_id=1, source_target_pairs={{0,4},{4,8},{8,12},{12,14},{14,10},{10,6},{6,2},{2,0},{1,5},{5,9},... | collective-permute-start | bytes 393224 | tf_op jit(solution)/shard_map/ppermute | solution.py:92
  23.9 4.1 %shard_map.49.refs_11_ = bf16[104,32,512]{2,1,0:T(8,128)(2,1)S(1)} custom-call(bf16[100,128,512]{2,1,0:T(8,128)(2,1)} %t_ref.7, s32[128,512]{1,0:T(8,128)S(1)} %multiply_add_fusion.place_ref), custom_call_target="tpu_custom_call" | custom-call | flops 34078720 | bytes 6815744 | tf_op jit(solution)/shard_map/pallas_call | solution.py:55
  28.1 0.0 collective-permute-done.6.refs_4_
  28.1 36.0 %shard_map.50 = (f32[128,512]{1,0:T(8,128)S(1)}, f32[128,512]{1,0:T(8,128)S(1)}) custom-call(bf16[128,512]{1,0:T(8,128)(2,1)S(1)} %bitcast.3, bf16[128,512]{1,0:T(8,128)(2,1)S(1)} %collective-permute-done.1.refs_1_, bf16[128,512]{1,0:T(8,128)(2,1)S(1)} %collective-permute-done.3.refs_2_, bf16[128,512]{1,0:T(8,128)(2,1)S(1)} %collective-permute-done.5.refs_3_, ...), custom_call_target="tpu_custom_call" | custom-call | flops 13958643712 | bytes 13631488 | tf_op jit(solution)/shard_map/pallas_call | solution.py:212
  64.0 0.1 collective-permute-start.7
  64.1 1.5 %collective-permute-done.7 = f32[128,512]{1,0:T(8,128)S(1)} collective-permute-done((f32[128,512]{1,0:T(8,128)S(1)}, f32[128,512]{1,0:T(8,128)S(1)}, u32[]{:S(2)}, u32[]{:S(2)}) %collective-permute-start.7) | collective-permute-done | bytes 262176 | tf_op jit(solution)/shard_map/ppermute | solution.py:237
  65.6 0.7 %add.7 = f32[128,512]{1,0:T(8,128)} add(f32[128,512]{1,0:T(8,128)S(1)} %get-tuple-element.29, f32[128,512]{1,0:T(8,128)S(1)} %collective-permute-done.7) | non-fusion elementwise | flops 65536 | bytes 786432 | tf_op jit(solution)/shard_map/add | solution.py:237
Async XLA Ops:
  1.0 8.4 %collective-permute-start.1 = (bf16[128,512]{1,0:T(8,128)(2,1)S(1)}, bf16[128,512]{1,0:T(8,128)(2,1)S(1)}, u32[]{:S(2)}, u32[]{:S(2)}) collective-permute-start(bf16[128,512]{1,0:T(8,128)(2,1)S(1)} %bitcast.1), channel_id=1, source_target_pairs={{4,0},{8,4},{12,8},{14,12},{10,14},{6,10},{2,6},{0,2},{5,1},{9,5},... | collective-permute-start | bytes 393224 | tf_op jit(solution)/shard_map/ppermute | solution.py:94
  4.0 5.4 %collective-permute-start = (bf16[128,512]{1,0:T(8,128)(2,1)S(1)}, bf16[128,512]{1,0:T(8,128)(2,1)S(1)}, u32[]{:S(2)}, u32[]{:S(2)}) collective-permute-start(bf16[128,512]{1,0:T(8,128)(2,1)S(1)} %bitcast.2), channel_id=1, source_target_pairs={{0,4},{4,8},{8,12},{12,14},{14,10},{10,6},{6,2},{2,0},{1,5},{5,9},... | collective-permute-start | bytes 393224 | tf_op jit(solution)/shard_map/ppermute | solution.py:92
  9.4 6.2 %collective-permute-start.3 = (bf16[128,512]{1,0:T(8,128)(2,1)S(1)}, bf16[128,512]{1,0:T(8,128)(2,1)S(1)}, u32[]{:S(2)}, u32[]{:S(2)}) collective-permute-start(bf16[128,512]{1,0:T(8,128)(2,1)S(1)} %collective-permute-done.1.refs_1_), channel_id=1, source_target_pairs={{4,0},{8,4},{12,8},{14,12},{10,14},{6,10},{2,6},{0,2},{5,1},{9,5},... | collective-permute-start | bytes 393224 | tf_op jit(solution)/shard_map/ppermute | solution.py:94
  11.4 5.0 %collective-permute-start.2 = (bf16[128,512]{1,0:T(8,128)(2,1)S(1)}, bf16[128,512]{1,0:T(8,128)(2,1)S(1)}, u32[]{:S(2)}, u32[]{:S(2)}) collective-permute-start(bf16[128,512]{1,0:T(8,128)(2,1)S(1)} %collective-permute-done.refs_7_), channel_id=1, source_target_pairs={{0,4},{4,8},{8,12},{12,14},{14,10},{10,6},{6,2},{2,0},{1,5},{5,9},... | collective-permute-start | bytes 393224 | tf_op jit(solution)/shard_map/ppermute | solution.py:92
  16.3 6.2 %collective-permute-start.5 = (bf16[128,512]{1,0:T(8,128)(2,1)S(1)}, bf16[128,512]{1,0:T(8,128)(2,1)S(1)}, u32[]{:S(2)}, u32[]{:S(2)}) collective-permute-start(bf16[128,512]{1,0:T(8,128)(2,1)S(1)} %collective-permute-done.3.refs_2_), channel_id=1, source_target_pairs={{4,0},{8,4},{12,8},{14,12},{10,14},{6,10},{2,6},{0,2},{5,1},{9,5},... | collective-permute-start | bytes 393224 | tf_op jit(solution)/shard_map/ppermute | solution.py:94
  17.9 5.0 %collective-permute-start.4 = (bf16[128,512]{1,0:T(8,128)(2,1)S(1)}, bf16[128,512]{1,0:T(8,128)(2,1)S(1)}, u32[]{:S(2)}, u32[]{:S(2)}) collective-permute-start(bf16[128,512]{1,0:T(8,128)(2,1)S(1)} %collective-permute-done.2.refs_6_), channel_id=1, source_target_pairs={{0,4},{4,8},{8,12},{12,14},{14,10},{10,6},{6,2},{2,0},{1,5},{5,9},... | collective-permute-start | bytes 393224 | tf_op jit(solution)/shard_map/ppermute | solution.py:92
  22.9 5.2 %collective-permute-start.6 = (bf16[128,512]{1,0:T(8,128)(2,1)S(1)}, bf16[128,512]{1,0:T(8,128)(2,1)S(1)}, u32[]{:S(2)}, u32[]{:S(2)}) collective-permute-start(bf16[128,512]{1,0:T(8,128)(2,1)S(1)} %collective-permute-done.4.refs_5_), channel_id=1, source_target_pairs={{0,4},{4,8},{8,12},{12,14},{14,10},{10,6},{6,2},{2,0},{1,5},{5,9},... | collective-permute-start | bytes 393224 | tf_op jit(solution)/shard_map/ppermute | solution.py:92
  64.0 1.6 %collective-permute-start.7 = (f32[128,512]{1,0:T(8,128)S(1)}, f32[128,512]{1,0:T(8,128)S(1)}, u32[]{:S(2)}, u32[]{:S(2)}) collective-permute-start(f32[128,512]{1,0:T(8,128)S(1)} %get-tuple-element.30), channel_id=1, source_target_pairs={{0,1},{1,0},{2,3},{3,2},{4,5},{5,4},{6,7},{7,6},{8,9},{9,8},{10,11... | collective-permute-start | bytes 786440 | tf_op jit(solution)/shard_map/ppermute | solution.py:237

commit v12 on v11

--- a/solution.py
+++ b/solution.py
@@ -14,7 +14,7 @@
 LANES = 128
 PIECES = 4
 ROWS = 16
-TAPS = 4
+TAPS = 8
 TILE = 1024
 GROUP = 8
 EMBED_VMEM = 44 * 1024 * 1024

time: 66.8 us -> 64 us (0.958)
  Pallas kernels: 52.5 us -> 49.8 us
    pallas_call x1, Pallas kernels: 36 us -> 33.2 us  [correlate(): pl.pallas_call(functools.partial(correlate_kernel, n, steps), grid=(steps...]
  transfers between devices with their start and end apart: 8 -> 8, of which waited for: 3 -> 3; matrix products, arithmetic and copies ran while one was open for 2% -> 2% of each run, Pallas kernels for 25% -> 26%
where the time goes in v12:
time: 64 us; the launch traced here: 63.7 us
  Pallas kernels  49.8 us (78%)
  starting transfers between devices  8.36 us (13%)
  waiting for transfers between devices  2.58 us (4%)
  other arithmetic  1.8 us (3%)
  local copies, waits for them, and re-layouts  1 us (2%)
    pallas_call x1, Pallas kernels, correlate(): pl.pallas_call(functools.partial(correlate_kernel, n, steps), grid=(steps...  33.2 us
    pallas_call x4, Pallas kernels, embed(): pl.pallas_call(embed_kernel, grid=(steps, channels // width), in_specs=[p...  16.6 us
    ppermute x3, starting transfers between devices, ring_gather(): b = lax.ppermute(b, 'blk', down)  6.55 us
    ppermute x4, starting transfers between devices, ring_gather(): a = lax.ppermute(a, 'blk', up)  1.73 us
    ppermute x1, waiting for transfers between devices, per_device(): return mine + lax.ppermute(other, 'chan', [(0, 1), (1, 0)])  1.52 us
  transfers between devices with their start and end apart: 8, of which 3 were waited for; matrix products, arithmetic and copies ran while one was open for 2% of the time, Pallas kernels for 26%

profile of v12, /device:TPU:0, one launch (start us, length us, event | category | flops | bytes accessed | tf_op | source)
XLA Modules:
  0.0 63.7 jit_solution(7141157324787957976)
XLA Ops:
  0.0 1.0 %copy.5 = bf16[512,128]{0,1:T(8,128)(2,1)S(1)} copy(bf16[512,128]{1,0:T(8,128)(2,1)} %param.4) | data formatting | bytes 262144 | tf_op args[0]
  1.0 3.0 %collective-permute-start.1 = (bf16[128,512]{1,0:T(8,128)(2,1)S(1)}, bf16[128,512]{1,0:T(8,128)(2,1)S(1)}, u32[]{:S(2)}, u32[]{:S(2)}) collective-permute-start(bf16[128,512]{1,0:T(8,128)(2,1)S(1)} %bitcast.1), channel_id=1, source_target_pairs={{4,0},{8,4},{12,8},{14,12},{10,14},{6,10},{2,6},{0,2},{5,1},{9,5},... | collective-permute-start | bytes 393224 | tf_op jit(solution)/shard_map/ppermute | solution.py:94
  4.0 0.1 collective-permute-start
  4.2 1.1 %multiply_add_fusion.place_ref = s32[128,512]{1,0:T(8,128)S(1)} fusion(s32[128,512]{1,0:T(8,128)} %param.6, s32[128,512]{1,0:T(8,128)} %param.7), kind=kLoop, calls=%fused_computation | loop fusion | flops 131072 | bytes 786432 | tf_op jit(solution)/shard_map/add | solution.py:234
  5.2 4.1 %shard_map.46.refs_8_ = bf16[104,32,512]{2,1,0:T(8,128)(2,1)S(1)} custom-call(bf16[100,128,512]{2,1,0:T(8,128)(2,1)} %t_ref.7, s32[128,512]{1,0:T(8,128)S(1)} %multiply_add_fusion.place_ref), custom_call_target="tpu_custom_call" | custom-call | flops 34078720 | bytes 6815744 | tf_op jit(solution)/shard_map/pallas_call | solution.py:55
  9.4 0.0 collective-permute-done.1.refs_1_
  9.4 0.0 collective-permute-done.refs_7_
  9.4 2.0 %collective-permute-start.3 = (bf16[128,512]{1,0:T(8,128)(2,1)S(1)}, bf16[128,512]{1,0:T(8,128)(2,1)S(1)}, u32[]{:S(2)}, u32[]{:S(2)}) collective-permute-start(bf16[128,512]{1,0:T(8,128)(2,1)S(1)} %collective-permute-done.1.refs_1_), channel_id=1, source_target_pairs={{4,0},{8,4},{12,8},{14,12},{10,14},{6,10},{2,6},{0,2},{5,1},{9,5},... | collective-permute-start | bytes 393224 | tf_op jit(solution)/shard_map/ppermute | solution.py:94
  11.4 0.1 collective-permute-start.2
  11.5 4.1 %shard_map.47.refs_9_ = bf16[104,32,512]{2,1,0:T(8,128)(2,1)S(1)} custom-call(bf16[100,128,512]{2,1,0:T(8,128)(2,1)} %t_ref.7, s32[128,512]{1,0:T(8,128)S(1)} %multiply_add_fusion.place_ref), custom_call_target="tpu_custom_call" | custom-call | flops 34078720 | bytes 6815744 | tf_op jit(solution)/shard_map/pallas_call | solution.py:55
  15.6 0.0 collective-permute-done.3.refs_2_
  15.6 0.7 %collective-permute-done.2.refs_6_ = bf16[128,512]{1,0:T(8,128)(2,1)S(1)} collective-permute-done((bf16[128,512]{1,0:T(8,128)(2,1)S(1)}, bf16[128,512]{1,0:T(8,128)(2,1)S(1)}, u32[]{:S(2)}, u32[]{:S(2)}) %collective-permute-start.2) | collective-permute-done | bytes 131104 | tf_op jit(solution)/shard_map/ppermute | solution.py:92
  16.3 1.6 %collective-permute-start.5 = (bf16[128,512]{1,0:T(8,128)(2,1)S(1)}, bf16[128,512]{1,0:T(8,128)(2,1)S(1)}, u32[]{:S(2)}, u32[]{:S(2)}) collective-permute-start(bf16[128,512]{1,0:T(8,128)(2,1)S(1)} %collective-permute-done.3.refs_2_), channel_id=1, source_target_pairs={{4,0},{8,4},{12,8},{14,12},{10,14},{6,10},{2,6},{0,2},{5,1},{9,5},... | collective-permute-start | bytes 393224 | tf_op jit(solution)/shard_map/ppermute | solution.py:94
  17.9 0.4 collective-permute-start.4
  18.3 4.1 %shard_map.48.refs_10_ = bf16[104,32,512]{2,1,0:T(8,128)(2,1)S(1)} custom-call(bf16[100,128,512]{2,1,0:T(8,128)(2,1)} %t_ref.7, s32[128,512]{1,0:T(8,128)S(1)} %multiply_add_fusion.place_ref), custom_call_target="tpu_custom_call" | custom-call | flops 34078720 | bytes 6815744 | tf_op jit(solution)/shard_map/pallas_call | solution.py:55
  22.5 0.0 collective-permute-done.5.refs_3_
  22.5 0.4 collective-permute-done.4.refs_5_
  22.9 1.0 %collective-permute-start.6 = (bf16[128,512]{1,0:T(8,128)(2,1)S(1)}, bf16[128,512]{1,0:T(8,128)(2,1)S(1)}, u32[]{:S(2)}, u32[]{:S(2)}) collective-permute-start(bf16[128,512]{1,0:T(8,128)(2,1)S(1)} %collective-permute-done.4.refs_5_), channel_id=1, source_target_pairs={{0,4},{4,8},{8,12},{12,14},{14,10},{10,6},{6,2},{2,0},{1,5},{5,9},... | collective-permute-start | bytes 393224 | tf_op jit(solution)/shard_map/ppermute | solution.py:92
  23.9 4.1 %shard_map.49.refs_11_ = bf16[104,32,512]{2,1,0:T(8,128)(2,1)S(1)} custom-call(bf16[100,128,512]{2,1,0:T(8,128)(2,1)} %t_ref.7, s32[128,512]{1,0:T(8,128)S(1)} %multiply_add_fusion.place_ref), custom_call_target="tpu_custom_call" | custom-call | flops 34078720 | bytes 6815744 | tf_op jit(solution)/shard_map/pallas_call | solution.py:55
  28.1 0.0 collective-permute-done.6.refs_4_
  28.1 33.2 %shard_map.50 = (f32[128,512]{1,0:T(8,128)S(1)}, f32[128,512]{1,0:T(8,128)S(1)}) custom-call(bf16[128,512]{1,0:T(8,128)(2,1)S(1)} %bitcast.3, bf16[128,512]{1,0:T(8,128)(2,1)S(1)} %collective-permute-done.1.refs_1_, bf16[128,512]{1,0:T(8,128)(2,1)S(1)} %collective-permute-done.3.refs_2_, bf16[128,512]{1,0:T(8,128)(2,1)S(1)} %collective-permute-done.5.refs_3_, ...), custom_call_target="tpu_custom_call" | custom-call | flops 13958643712 | bytes 13631488 | tf_op jit(solution)/shard_map/pallas_call | solution.py:212
  61.3 0.1 collective-permute-start.7
  61.4 1.5 %collective-permute-done.7 = f32[128,512]{1,0:T(8,128)S(1)} collective-permute-done((f32[128,512]{1,0:T(8,128)S(1)}, f32[128,512]{1,0:T(8,128)S(1)}, u32[]{:S(2)}, u32[]{:S(2)}) %collective-permute-start.7) | collective-permute-done | bytes 262176 | tf_op jit(solution)/shard_map/ppermute | solution.py:237
  62.9 0.7 %add.7 = f32[128,512]{1,0:T(8,128)} add(f32[128,512]{1,0:T(8,128)S(1)} %get-tuple-element.29, f32[128,512]{1,0:T(8,128)S(1)} %collective-permute-done.7) | non-fusion elementwise | flops 65536 | bytes 786432 | tf_op jit(solution)/shard_map/add | solution.py:237
Async XLA Ops:
  1.0 8.4 %collective-permute-start.1 = (bf16[128,512]{1,0:T(8,128)(2,1)S(1)}, bf16[128,512]{1,0:T(8,128)(2,1)S(1)}, u32[]{:S(2)}, u32[]{:S(2)}) collective-permute-start(bf16[128,512]{1,0:T(8,128)(2,1)S(1)} %bitcast.1), channel_id=1, source_target_pairs={{4,0},{8,4},{12,8},{14,12},{10,14},{6,10},{2,6},{0,2},{5,1},{9,5},... | collective-permute-start | bytes 393224 | tf_op jit(solution)/shard_map/ppermute | solution.py:94
  4.0 5.4 %collective-permute-start = (bf16[128,512]{1,0:T(8,128)(2,1)S(1)}, bf16[128,512]{1,0:T(8,128)(2,1)S(1)}, u32[]{:S(2)}, u32[]{:S(2)}) collective-permute-start(bf16[128,512]{1,0:T(8,128)(2,1)S(1)} %bitcast.2), channel_id=1, source_target_pairs={{0,4},{4,8},{8,12},{12,14},{14,10},{10,6},{6,2},{2,0},{1,5},{5,9},... | collective-permute-start | bytes 393224 | tf_op jit(solution)/shard_map/ppermute | solution.py:92
  9.4 6.2 %collective-permute-start.3 = (bf16[128,512]{1,0:T(8,128)(2,1)S(1)}, bf16[128,512]{1,0:T(8,128)(2,1)S(1)}, u32[]{:S(2)}, u32[]{:S(2)}) collective-permute-start(bf16[128,512]{1,0:T(8,128)(2,1)S(1)} %collective-permute-done.1.refs_1_), channel_id=1, source_target_pairs={{4,0},{8,4},{12,8},{14,12},{10,14},{6,10},{2,6},{0,2},{5,1},{9,5},... | collective-permute-start | bytes 393224 | tf_op jit(solution)/shard_map/ppermute | solution.py:94
  11.4 5.0 %collective-permute-start.2 = (bf16[128,512]{1,0:T(8,128)(2,1)S(1)}, bf16[128,512]{1,0:T(8,128)(2,1)S(1)}, u32[]{:S(2)}, u32[]{:S(2)}) collective-permute-start(bf16[128,512]{1,0:T(8,128)(2,1)S(1)} %collective-permute-done.refs_7_), channel_id=1, source_target_pairs={{0,4},{4,8},{8,12},{12,14},{14,10},{10,6},{6,2},{2,0},{1,5},{5,9},... | collective-permute-start | bytes 393224 | tf_op jit(solution)/shard_map/ppermute | solution.py:92
  16.3 6.2 %collective-permute-start.5 = (bf16[128,512]{1,0:T(8,128)(2,1)S(1)}, bf16[128,512]{1,0:T(8,128)(2,1)S(1)}, u32[]{:S(2)}, u32[]{:S(2)}) collective-permute-start(bf16[128,512]{1,0:T(8,128)(2,1)S(1)} %collective-permute-done.3.refs_2_), channel_id=1, source_target_pairs={{4,0},{8,4},{12,8},{14,12},{10,14},{6,10},{2,6},{0,2},{5,1},{9,5},... | collective-permute-start | bytes 393224 | tf_op jit(solution)/shard_map/ppermute | solution.py:94
  17.9 5.0 %collective-permute-start.4 = (bf16[128,512]{1,0:T(8,128)(2,1)S(1)}, bf16[128,512]{1,0:T(8,128)(2,1)S(1)}, u32[]{:S(2)}, u32[]{:S(2)}) collective-permute-start(bf16[128,512]{1,0:T(8,128)(2,1)S(1)} %collective-permute-done.2.refs_6_), channel_id=1, source_target_pairs={{0,4},{4,8},{8,12},{12,14},{14,10},{10,6},{6,2},{2,0},{1,5},{5,9},... | collective-permute-start | bytes 393224 | tf_op jit(solution)/shard_map/ppermute | solution.py:92
  22.9 5.2 %collective-permute-start.6 = (bf16[128,512]{1,0:T(8,128)(2,1)S(1)}, bf16[128,512]{1,0:T(8,128)(2,1)S(1)}, u32[]{:S(2)}, u32[]{:S(2)}) collective-permute-start(bf16[128,512]{1,0:T(8,128)(2,1)S(1)} %collective-permute-done.4.refs_5_), channel_id=1, source_target_pairs={{0,4},{4,8},{8,12},{12,14},{14,10},{10,6},{6,2},{2,0},{1,5},{5,9},... | collective-permute-start | bytes 393224 | tf_op jit(solution)/shard_map/ppermute | solution.py:92
  61.3 1.6 %collective-permute-start.7 = (f32[128,512]{1,0:T(8,128)S(1)}, f32[128,512]{1,0:T(8,128)S(1)}, u32[]{:S(2)}, u32[]{:S(2)}) collective-permute-start(f32[128,512]{1,0:T(8,128)S(1)} %get-tuple-element.30), channel_id=1, source_target_pairs={{0,1},{1,0},{2,3},{3,2},{4,5},{5,4},{6,7},{7,6},{8,9},{9,8},{10,11... | collective-permute-start | bytes 786440 | tf_op jit(solution)/shard_map/ppermute | solution.py:237
